TPU v7x, 32 devices: a whole 2x2x4 slice. The times are simulated.
32 devices in a mesh: dp: 8 (over z, x), seq: 4 (over y, core).
Axes of the slice: x: 2, y: 2, z: 4, core: 2. Of those that a mesh axis runs over, the one named last changes fastest.
Arguments:
- inputs: bfloat16 [24, 1024, 1024], P('dp', 'seq'), may hold values from -6 to 6
- segment_ids: int32 [24, 1024], P('dp', 'seq'), may hold values from 0 to 7, as said below
- doc_times: int32 [24, 8], P('dp'), may hold values from 0 to 999
- time_weight: bfloat16 [256, 1024], replicated, may hold values from -0.375 to 0.375
- time_bias: bfloat16 [1024], replicated, may hold values from -3 to 3
- norm1_gain: bfloat16 [1024], replicated, may hold values from 0.099609375 to 1.8984375
- norm1_bias: bfloat16 [1024], replicated, may hold values from -3 to 3
- qkv_weight: bfloat16 [1024, 3072], replicated, may hold values from -0.1875 to 0.1875
- qkv_bias: bfloat16 [3072], replicated, may hold values from -3 to 3
- out_weight: bfloat16 [1024, 1024], replicated, may hold values from -1.5 to 1.5
- out_bias: bfloat16 [1024], replicated, may hold values from -3 to 3
- norm2_gain: bfloat16 [1024], replicated, may hold values from 0.099609375 to 1.8984375
- norm2_bias: bfloat16 [1024], replicated, may hold values from -3 to 3
- up_weight: bfloat16 [1024, 4096], replicated, may hold values from -0.1875 to 0.1875
- up_bias: bfloat16 [4096], replicated, may hold values from -3 to 3
- down_weight: bfloat16 [4096, 1024], replicated, may hold values from -0.09375 to 0.09375
- down_bias: bfloat16 [1024], replicated, may hold values from -3 to 3
- cotangent: bfloat16 [24, 1024, 1024], P('dp', 'seq'), may hold values from -6 to 6
Outputs:
- output: bfloat16 [24, 1024, 1024], P('dp', 'seq')
- input_grad: bfloat16 [24, 1024, 1024], P('dp', 'seq')
- time_weight_grad: float32 [256, 1024], P('dp')
- time_bias_grad: float32 [1024], P('dp')
- norm1_gain_grad: float32 [1024], P('dp')
- norm1_bias_grad: float32 [1024], P('dp')
- qkv_weight_grad: float32 [1024, 3072], P('dp')
- qkv_bias_grad: float32 [3072], P('dp')
- out_weight_grad: float32 [1024, 1024], P('dp')
- out_bias_grad: float32 [1024], P('dp')
- norm2_gain_grad: float32 [1024], P('dp')
- norm2_bias_grad: float32 [1024], P('dp')
- up_weight_grad: float32 [1024, 4096], P('dp')
- up_bias_grad: float32 [4096], P('dp')
- down_weight_grad: float32 [4096, 1024], P('dp')
- down_bias_grad: float32 [1024], P('dp')
Inputs may be any that keep to these rules, and one draw needn't show every extreme that they name: `segment_ids`: along each row the ids never fall and the last token has id 8 - 1. In each aligned block of 3 rows one row holds a document that begins among the first 256 tokens and ends among the last 256.
All inputs are finite; a program needn't handle non-finite values.
Results may differ from a plain program's by a relative error of at most 0.014.
Values may be sent and summed in bfloat16 or wider, within the bound.
No kernel may reach another device: no remote copies, remote signals or barrier semaphores. Data moves between devices by JAX's collectives and lax.ppermute only.
A program may use at most 320 MiB of HBM per device.

v0:
```python
import math

import jax
import jax.numpy as jnp
from jax import lax
from jax.sharding import PartitionSpec as P

HEADS = 16
HEAD_DIM = 64
TEMB = 256
SEGS = 8


EPSILON = 1e-05


def layer_norm(values, gain_vec, shift_vec):
    centred = values - jnp.mean(values, axis=-1, keepdims=True)
    spread = jnp.mean(centred * centred, axis=-1, keepdims=True)
    return centred * lax.rsqrt(spread + EPSILON) * gain_vec + shift_vec


def smooth_gate(values):
    return jax.nn.gelu(values, approximate=True)


def rotate(values, cos_tab, sin_tab):
    half_size = values.shape[-1] // 2
    part_one = values[..., :half_size]
    part_two = values[..., half_size:]
    return jnp.concatenate(
        [part_one * cos_tab - part_two * sin_tab, part_two * cos_tab + part_one * sin_tab], axis=-1
    )


def time_features(doc_times, feat_width):
    half_size = feat_width // 2
    frequency = jnp.exp(-math.log(10000.0) * jnp.arange(half_size, dtype=jnp.float32) / half_size)
    angles = doc_times.astype(jnp.float32)[..., None] * frequency
    return jnp.concatenate([jnp.sin(angles), jnp.cos(angles)], axis=-1)


def rotary_tables(positions, head_size):
    half_size = head_size // 2
    frequency = jnp.exp(
        -math.log(10000.0) * 2.0 * jnp.arange(half_size, dtype=jnp.float32) / head_size
    )
    angles = positions.astype(jnp.float32)[..., None] * frequency
    return (jnp.cos(angles)[..., None, :], jnp.sin(angles)[..., None, :])


def contract_rows(left_op, right_op):
    return lax.dot_general(
        left_op, right_op, (((0,), (0,)), ((), ())), preferred_element_type=jnp.float32
    )


def contract_cols(left_op, right_op):
    return lax.dot_general(
        left_op, right_op, (((1,), (1,)), ((), ())), preferred_element_type=jnp.float32
    )


def column_sum(values):
    return jnp.sum(values.astype(jnp.float32), axis=0)


def local(
    inputs,
    segment_ids,
    doc_times,
    time_weight,
    time_bias,
    norm1_gain,
    norm1_bias,
    qkv_weight,
    qkv_bias,
    out_weight,
    out_bias,
    norm2_gain,
    norm2_bias,
    up_weight,
    up_bias,
    down_weight,
    down_bias,
    cotangent,
):
    row_count, shard_len, model_width = inputs.shape
    head_size = HEAD_DIM
    score_scale = HEAD_DIM ** (-0.5)
    tokens = row_count * shard_len
    highest = lax.Precision.HIGHEST
    doc_slots = jnp.arange(SEGS, dtype=jnp.int32)
    onehot = (segment_ids[..., None] == doc_slots).astype(jnp.float32)
    positions = lax.axis_index("seq") * shard_len + jnp.arange(shard_len, dtype=jnp.int32)[None, :]
    positions = jnp.broadcast_to(positions, segment_ids.shape)
    cos_tab, sin_tab = rotary_tables(positions, head_size)
    features = time_features(doc_times, TEMB).astype(jnp.bfloat16)
    time_shift = jnp.dot(
        features.reshape(row_count * SEGS, TEMB), time_weight, preferred_element_type=jnp.float32
    )
    time_shift = time_shift.reshape(row_count, SEGS, model_width) + time_bias.astype(jnp.float32)
    stream = inputs.astype(jnp.float32) + jnp.einsum(
        "rsg,rgd->rsd", onehot, time_shift, precision=highest
    )
    normed1, norm1_back = jax.vjp(
        layer_norm, stream, norm1_gain.astype(jnp.float32), norm1_bias.astype(jnp.float32)
    )
    normed1_low = normed1.astype(jnp.bfloat16).reshape(tokens, model_width)
    qkv_all = jnp.dot(
        normed1_low, qkv_weight, preferred_element_type=jnp.float32
    ) + qkv_bias.astype(jnp.float32)
    qkv_all = qkv_all.reshape(row_count, shard_len, 3 * model_width)
    head_shape = (row_count, shard_len, HEADS, head_size)
    queries = rotate(qkv_all[..., :model_width].reshape(head_shape), cos_tab, sin_tab).astype(
        jnp.bfloat16
    )
    keys_rot = rotate(
        qkv_all[..., model_width : 2 * model_width].reshape(head_shape), cos_tab, sin_tab
    )
    keys_flat = keys_rot.astype(jnp.bfloat16).reshape(row_count, shard_len, model_width)
    values_low = qkv_all[..., 2 * model_width :].astype(jnp.bfloat16)
    keys_row, values_row, segs_row = (
        lax.all_gather(keys_flat, "seq", axis=1, tiled=True),
        lax.all_gather(values_low, "seq", axis=1, tiled=True),
        lax.all_gather(segment_ids, "seq", axis=1, tiled=True),
    )
    row_len = keys_row.shape[1]
    keys_heads = keys_row.reshape(row_count, row_len, HEADS, head_size)
    values_heads = values_row.reshape(row_count, row_len, HEADS, head_size)
    same_doc = segment_ids[:, None, :, None] == segs_row[:, None, None, :]
    scores = (
        jnp.einsum("rqhd,rkhd->rhqk", queries, keys_heads, preferred_element_type=jnp.float32)
        * score_scale
    )
    masked = jnp.where(same_doc, scores, -1e30)
    row_max = jnp.max(masked, axis=-1, keepdims=True)
    weights = jnp.where(same_doc, jnp.exp(masked - row_max), 0.0)
    row_total = jnp.sum(weights, axis=-1, keepdims=True)
    log_total = row_max + jnp.log(row_total)
    attn_probs = (weights / row_total).astype(jnp.bfloat16)
    attended = jnp.einsum(
        "rhqk,rkhd->rqhd", attn_probs, values_heads, preferred_element_type=jnp.float32
    )
    attended_low = attended.astype(jnp.bfloat16).reshape(tokens, model_width)
    branch = jnp.dot(
        attended_low, out_weight, preferred_element_type=jnp.float32
    ) + out_bias.astype(jnp.float32)
    middle = stream + branch.reshape(row_count, shard_len, model_width)
    normed2, norm2_back = jax.vjp(
        layer_norm, middle, norm2_gain.astype(jnp.float32), norm2_bias.astype(jnp.float32)
    )
    normed2_low = normed2.astype(jnp.bfloat16).reshape(tokens, model_width)
    hidden = jnp.dot(normed2_low, up_weight, preferred_element_type=jnp.float32) + up_bias.astype(
        jnp.float32
    )
    active, gate_back = jax.vjp(smooth_gate, hidden)
    active_low = active.astype(jnp.bfloat16)
    feed = jnp.dot(active_low, down_weight, preferred_element_type=jnp.float32) + down_bias.astype(
        jnp.float32
    )
    output = (middle + feed.reshape(row_count, shard_len, model_width)).astype(jnp.bfloat16)
    flat_cot = cotangent.reshape(tokens, model_width)
    down_w_grad = contract_rows(active_low, flat_cot)
    down_b_grad = column_sum(flat_cot)
    grad_hidden = gate_back(contract_cols(flat_cot, down_weight))[0].astype(jnp.bfloat16)
    up_w_grad = contract_rows(normed2_low, grad_hidden)
    up_b_grad = column_sum(grad_hidden)
    grad_normed2 = contract_cols(grad_hidden, up_weight).reshape(row_count, shard_len, model_width)
    grad_mid_norm, gain2_grad, shift2_grad = norm2_back(grad_normed2)
    grad_middle = cotangent.astype(jnp.float32) + grad_mid_norm
    grad_middle_low = grad_middle.astype(jnp.bfloat16).reshape(tokens, model_width)
    out_w_grad = contract_rows(attended_low, grad_middle_low)
    out_b_grad = column_sum(grad_middle_low)
    grad_attended = (
        contract_cols(grad_middle_low, out_weight).astype(jnp.bfloat16).reshape(head_shape)
    )
    scores_back = (
        jnp.einsum("rqhd,rkhd->rhqk", queries, keys_heads, preferred_element_type=jnp.float32)
        * score_scale
    )
    probs_back = jnp.exp(jnp.where(same_doc, scores_back - log_total, -1e30))
    grad_probs = jnp.einsum(
        "rqhd,rkhd->rhqk", grad_attended, values_heads, preferred_element_type=jnp.float32
    )
    row_delta = jnp.sum(grad_probs * probs_back, axis=-1, keepdims=True)
    grad_scores = (probs_back * (grad_probs - row_delta)).astype(jnp.bfloat16)
    grad_query = (
        jnp.einsum("rhqk,rkhd->rqhd", grad_scores, keys_heads, preferred_element_type=jnp.float32)
        * score_scale
    )
    grad_key_part = (
        jnp.einsum("rhqk,rqhd->rkhd", grad_scores, queries, preferred_element_type=jnp.float32)
        * score_scale
    )
    grad_value_part = jnp.einsum(
        "rhqk,rqhd->rkhd",
        probs_back.astype(jnp.bfloat16),
        grad_attended,
        preferred_element_type=jnp.float32,
    )
    grad_key, grad_value = (
        lax.psum_scatter(
            grad_key_part.reshape(row_count, row_len, model_width).astype(jnp.bfloat16),
            "seq",
            scatter_dimension=1,
            tiled=True,
        ).astype(jnp.float32),
        lax.psum_scatter(
            grad_value_part.reshape(row_count, row_len, model_width).astype(jnp.bfloat16),
            "seq",
            scatter_dimension=1,
            tiled=True,
        ).astype(jnp.float32),
    )
    grad_query = rotate(grad_query, cos_tab, -sin_tab).reshape(row_count, shard_len, model_width)
    grad_key = rotate(grad_key.reshape(head_shape), cos_tab, -sin_tab).reshape(
        row_count, shard_len, model_width
    )
    grad_qkv = jnp.concatenate([grad_query, grad_key, grad_value], axis=-1)
    grad_qkv = grad_qkv.astype(jnp.bfloat16).reshape(tokens, 3 * model_width)
    qkv_w_grad = contract_rows(normed1_low, grad_qkv)
    qkv_b_grad = column_sum(grad_qkv)
    grad_normed1 = contract_cols(grad_qkv, qkv_weight).reshape(row_count, shard_len, model_width)
    grad_start_norm, gain1_grad, shift1_grad = norm1_back(grad_normed1)
    grad_stream = grad_middle + grad_start_norm
    input_grad = grad_stream.astype(jnp.bfloat16)
    grad_shift = jnp.einsum("rsg,rsd->rgd", onehot, grad_stream, precision=highest)
    time_b_grad = jnp.sum(grad_shift, axis=(0, 1))
    time_w_grad = jnp.einsum(
        "rgt,rgd->td", features.astype(jnp.float32), grad_shift, precision=highest
    )
    time_w_part, qkv_w_part, out_w_part, up_w_part, down_w_part = (
        time_w_grad,
        qkv_w_grad,
        out_w_grad,
        up_w_grad,
        down_w_grad,
    )
    vectors = (
        time_b_grad,
        gain1_grad,
        shift1_grad,
        qkv_b_grad,
        out_b_grad,
        gain2_grad,
        shift2_grad,
        up_b_grad,
        down_b_grad,
    )
    reduced = (
        lax.psum_scatter(time_w_part, "dp", scatter_dimension=0, tiled=True),
        lax.psum_scatter(qkv_w_part, "dp", scatter_dimension=0, tiled=True),
        lax.psum_scatter(out_w_part, "dp", scatter_dimension=0, tiled=True),
        lax.psum_scatter(up_w_part, "dp", scatter_dimension=0, tiled=True),
        lax.psum_scatter(down_w_part, "dp", scatter_dimension=0, tiled=True),
        lax.psum_scatter(vectors[0], "dp", scatter_dimension=0, tiled=True),
        lax.psum_scatter(vectors[1], "dp", scatter_dimension=0, tiled=True),
        lax.psum_scatter(vectors[2], "dp", scatter_dimension=0, tiled=True),
        lax.psum_scatter(vectors[3], "dp", scatter_dimension=0, tiled=True),
        lax.psum_scatter(vectors[4], "dp", scatter_dimension=0, tiled=True),
        lax.psum_scatter(vectors[5], "dp", scatter_dimension=0, tiled=True),
        lax.psum_scatter(vectors[6], "dp", scatter_dimension=0, tiled=True),
        lax.psum_scatter(vectors[7], "dp", scatter_dimension=0, tiled=True),
        lax.psum_scatter(vectors[8], "dp", scatter_dimension=0, tiled=True),
    )
    finished = (
        lax.psum(reduced[0].astype(jnp.bfloat16), "seq").astype(jnp.float32),
        lax.psum(reduced[1].astype(jnp.bfloat16), "seq").astype(jnp.float32),
        lax.psum(reduced[2].astype(jnp.bfloat16), "seq").astype(jnp.float32),
        lax.psum(reduced[3].astype(jnp.bfloat16), "seq").astype(jnp.float32),
        lax.psum(reduced[4].astype(jnp.bfloat16), "seq").astype(jnp.float32),
        lax.psum(reduced[5].astype(jnp.bfloat16), "seq").astype(jnp.float32),
        lax.psum(reduced[6].astype(jnp.bfloat16), "seq").astype(jnp.float32),
        lax.psum(reduced[7].astype(jnp.bfloat16), "seq").astype(jnp.float32),
        lax.psum(reduced[8].astype(jnp.bfloat16), "seq").astype(jnp.float32),
        lax.psum(reduced[9].astype(jnp.bfloat16), "seq").astype(jnp.float32),
        lax.psum(reduced[10].astype(jnp.bfloat16), "seq").astype(jnp.float32),
        lax.psum(reduced[11].astype(jnp.bfloat16), "seq").astype(jnp.float32),
        lax.psum(reduced[12].astype(jnp.bfloat16), "seq").astype(jnp.float32),
        lax.psum(reduced[13].astype(jnp.bfloat16), "seq").astype(jnp.float32),
    )
    return (
        output,
        input_grad,
        finished[0],
        finished[5],
        finished[6],
        finished[7],
        finished[1],
        finished[8],
        finished[2],
        finished[9],
        finished[10],
        finished[11],
        finished[3],
        finished[12],
        finished[4],
        finished[13],
    )


def solution(mesh):
    placed = (
        P("dp", "seq", None),
        P("dp", "seq"),
        P("dp", None),
        P(),
        P(),
        P(),
        P(),
        P(),
        P(),
        P(),
        P(),
        P(),
        P(),
        P(),
        P(),
        P(),
        P(),
        P("dp", "seq", None),
    )
    return jax.shard_map(
        local,
        mesh=mesh,
        in_specs=placed,
        out_specs=(
            P("dp", "seq", None),
            P("dp", "seq", None),
            P("dp", None),
            P("dp"),
            P("dp"),
            P("dp"),
            P("dp", None),
            P("dp"),
            P("dp", None),
            P("dp"),
            P("dp"),
            P("dp"),
            P("dp", None),
            P("dp"),
            P("dp", None),
            P("dp"),
        ),
        check_vma=False,
    )
```

profile of v0, /device:TPU:0, one launch (start us, length us, event | category | flops | bytes accessed | tf_op | source)
XLA Modules:
  0.0 1501.8 jit_solution(2901086165632443084)
XLA Ops:
  54.5 39.6 %all-gather.5.cloned.1.call-done = bf16[3,1024,1024]{1,2,0:T(8,128)(2,1)} async-done(((bf16[3,256,1024]{1,2,0:T(8,128)(2,1)}), bf16[3,1024,1024]{1,2,0:T(8,128)(2,1)}) %all-gather.5.cloned.1.call-update) | async-done | bytes 6291472 | tf_op jit(solution)/shard_map/all_gather | solution.py:124
  94.1 23.2 %select_reduce_fusion = (f32[3,16,256]{2,1,0:T(8,128)S(1)}, f32[3,16,256,1024]{3,2,1,0:T(8,128)}) fusion(pred[3,256,1024]{2,1,0:T(8,128)(4,1)S(1)} %broadcast_compare_fusion, bf16[3,1024,16,64]{1,3,2,0:T(8,128)(2,1)} %bitcast.86, bf16[3,256,16,32]{1,3,2,0:T(8,128)(2,1)} %get-tuple-element.62, bf16[3,256,16,32]{1,3,2,0:T(8,128)(2,1)} %get-tuple-element.61), kind=kOutput, calls=%fused_computation.5 | convolution fusion | flops 1651494912 | bytes 59031552 | tf_op jit(solution)/shard_map/rqhd,rkhd->rhqk/dot_general | solution.py:133
  117.3 23.0 %fusion = f32[3,16,256]{2,1,0:T(8,128)S(1)} fusion(f32[3,16,256,1024]{3,2,1,0:T(8,128)} %get-tuple-element.79, f32[3,16,256]{2,1,0:T(8,128)S(1)} %get-tuple-element.78, pred[3,256,1024]{2,1,0:T(8,128)(4,1)S(1)} %broadcast_compare_fusion), kind=kLoop, calls=%fused_computation.6 | loop fusion | flops 62902272 | bytes 51216384 | tf_op jit(solution)/shard_map/reduce_sum | solution.py:139
  151.3 22.6 %fusion.20 = bf16[3,256,16,64]{1,3,2,0:T(8,128)(2,1)S(1)} fusion(bf16[3,1024,16,64]{1,3,2,0:T(8,128)(2,1)} %bitcast.88, f32[3,16,256,1024]{3,2,1,0:T(8,128)} %get-tuple-element.79, f32[3,16,256]{2,1,0:T(8,128)S(1)} %fusion, f32[3,16,256]{2,1,0:T(8,128)S(1)} %get-tuple-element.78, pred[3,256,1024]{2,1,0:T(8,128)(4,1)S(1)} %broadcast_compare_fusion), kind=kOutput, calls=%fused_computation.66 | convolution fusion | flops 1686896640 | bytes 59080704 | tf_op jit(solution)/shard_map/rhqk,rkhd->rqhd/dot_general | solution.py:142
  181.0 12.5 fusion.54
  193.6 12.4 convolution_add_fusion.1
  206.0 19.8 %convert_reduce_fusion = (f32[4096]{0:T(1024)}, bf16[768,4096]{1,0:T(8,128)(2,1)}) fusion(f32[768,4096]{1,0:T(8,128)} %fusion.54, f32[4096]{0:T(1024)S(1)} %convert_element_type.226, bf16[768,1024]{1,0:T(8,128)(2,1)S(1)} %bitcast.105, bf16[4096,1024]{1,0:T(8,128)(2,1)} %param.33), kind=kOutput, calls=%fused_computation.20 | convolution fusion | flops 6514798592 | bytes 28868608 | tf_op jit(solution)/shard_map/dot_general | solution.py:59
  225.8 11.6 fusion.53
  256.4 40.3 %multiply_reduce_fusion = (f32[3,16,256]{2,1,0:T(8,128)S(1)}, f32[3,16,256,1024]{3,2,1,0:T(8,128)}) fusion(f32[3,16,256,1024]{3,2,1,0:T(8,128)} %get-tuple-element.79, f32[3,16,256]{2,1,0:T(8,128)S(1)} %copy-done.21, pred[3,256,1024]{2,1,0:T(8,128)(4,1)S(1)} %broadcast_compare_fusion, bf16[3,256,16,64]{1,3,2,0:T(8,128)(2,1)S(1)} %copy.62, ...), kind=kOutput, calls=%fused_computation.1 | convolution fusion | flops 1673515008 | bytes 109412352 | tf_op jit(solution)/shard_map/rqhd,rkhd->rhqk/dot_general | solution.py:183
  296.7 40.4 %multiply_convert_fusion = bf16[3,16,256,1024]{3,2,1,0:T(8,128)(2,1)} fusion(f32[3,16,256,1024]{3,2,1,0:T(8,128)} %get-tuple-element.81, f32[3,16,256,1024]{3,2,1,0:T(8,128)} %get-tuple-element.79, f32[3,16,256]{2,1,0:T(8,128)S(1)} %get-tuple-element.80, f32[3,16,256]{2,1,0:T(8,128)S(1)} %copy-done.21, pred[3,256,1024]{2,1,0:T(8,128)(4,1)S(1)} %broadcast_compare_fusion), kind=kLoop, calls=%fused_computation | loop fusion | flops 75497472 | bytes 126713856 | tf_op jit(solution)/shard_map/convert_element_type | solution.py:187
  337.1 15.7 %multiply_convert_fusion.1 = bf16[3,16,64,1024]{3,2,1,0:T(8,128)(2,1)} fusion(bf16[3,16,256,1024]{3,2,1,0:T(8,128)(2,1)} %multiply_convert_fusion, bf16[3,256,16,32]{1,3,2,0:T(8,128)(2,1)} %get-tuple-element.62, bf16[3,256,16,32]{1,3,2,0:T(8,128)(2,1)} %get-tuple-element.61), kind=kOutput, calls=%fused_computation.21 | convolution fusion | flops 1620049920 | bytes 33030144 | tf_op jit(solution)/shard_map/rhqk,rqhd->rkhd/dot_general | solution.py:193
  352.9 24.9 %fusion.15 = bf16[3,16,64,1024]{3,2,1,0:T(8,128)(2,1)} fusion(bf16[3,256,16,64]{1,3,2,0:T(8,128)(2,1)S(1)} %copy.62, f32[3,16,256,1024]{3,2,1,0:T(8,128)} %get-tuple-element.79, f32[3,16,256]{2,1,0:T(8,128)S(1)} %copy-done.21, pred[3,256,1024]{2,1,0:T(8,128)(4,1)S(1)} %broadcast_compare_fusion), kind=kOutput, calls=%fused_computation.33 | convolution fusion | flops 1664090112 | bytes 59031552 | tf_op jit(solution)/shard_map/rhqk,rqhd->rkhd/dot_general | solution.py:196
  393.1 15.9 %multiply_bitcast_fusion = f32[3,256,16,64]{1,3,2,0:T(8,128)} fusion(bf16[3,1024,16,64]{1,3,2,0:T(8,128)(2,1)} %bitcast.87, bf16[3,16,256,1024]{3,2,1,0:T(8,128)(2,1)} %multiply_convert_fusion), kind=kOutput, calls=%fused_computation.42 | convolution fusion | flops 1611399168 | bytes 34603008 | tf_op jit(solution)/shard_map/rhqk,rkhd->rqhd/dot_general | solution.py:189
  420.9 51.5 %reduce-scatter.10.cloned.1.call-done = bf16[3,256,1024]{2,1,0:T(8,128)(2,1)} async-done(((bf16[3,1024,1024]{2,1,0:T(8,128)(2,1)}), bf16[3,256,1024]{2,1,0:T(8,128)(2,1)}) %reduce-scatter.10.cloned.1.call-update) | async-done | bytes 1572880 | tf_op jit(solution)/shard_map/reduce_scatter | solution.py:209
  472.4 10.6 fusion.44
  491.0 16.1 %fusion.43 = f32[4096,1024]{1,0:T(8,128)} fusion(bf16[768,1024]{1,0:T(8,128)(2,1)} %bitcast.104, f32[768,4096]{1,0:T(8,128)} %fusion.54, f32[4096]{0:T(1024)S(1)} %copy-done.46), kind=kOutput, calls=%fused_computation.118 | convolution fusion | flops 6473908224 | bytes 30949376 | tf_op jit(solution)/shard_map/dot_general | solution.py:53
  507.2 12.7 fusion.56
  520.2 12.4 convolution_bitcast_fusion
  532.6 31.3 %reduce-scatter.16.cloned.1.call-done = f32[128,1024]{1,0:T(8,128)} async-done(((f32[1024,1024]{1,0:T(8,128)}), f32[128,1024]{1,0:T(8,128)}) %reduce-scatter.16.cloned.1.call-update) | async-done | bytes 524304 | tf_op jit(solution)/shard_map/reduce_scatter | solution.py:254
  565.7 65.1 %reduce-scatter.12.cloned.1.call-done = f32[32,1024]{1,0:T(8,128)} async-done(((f32[256,1024]{1,0:T(8,128)}), f32[32,1024]{1,0:T(8,128)}) %reduce-scatter.12.cloned.1.call-update) | async-done | bytes 131088 | tf_op jit(solution)/shard_map/reduce_scatter | solution.py:252
  632.4 284.0 %reduce-scatter.20.cloned.1.call-done = f32[512,1024]{1,0:T(8,128)} async-done(((f32[4096,1024]{1,0:T(8,128)}), f32[512,1024]{1,0:T(8,128)}) %reduce-scatter.20.cloned.1.call-update) | async-done | bytes 2097168 | tf_op jit(solution)/shard_map/reduce_scatter | solution.py:256
  919.1 283.2 %reduce-scatter.18.cloned.1.call-done = f32[128,4096]{1,0:T(8,128)} async-done(((f32[1024,4096]{1,0:T(8,128)}), f32[128,4096]{1,0:T(8,128)}) %reduce-scatter.18.cloned.1.call-update) | async-done | bytes 2097168 | tf_op jit(solution)/shard_map/reduce_scatter | solution.py:255
  1205.1 207.1 %reduce-scatter.14.cloned.1.call-done = f32[128,3072]{1,0:T(8,128)} async-done(((f32[1024,3072]{1,0:T(8,128)}), f32[128,3072]{1,0:T(8,128)}) %reduce-scatter.14.cloned.1.call-update) | async-done | bytes 1572880 | tf_op jit(solution)/shard_map/reduce_scatter | solution.py:253
  1429.8 35.7 %all-reduce.9 = (bf16[1024]{0:T(1024)(128)(2,1)S(1)}, bf16[1024]{0:T(1024)(128)(2,1)S(1)}, bf16[1024]{0:T(1024)(128)(2,1)S(1)}, bf16[3072]{0:T(1024)(128)(2,1)S(...) all-reduce(f32[1024]{0:T(1024)S(1)} %get-tuple-element.83, ...), channel_id=5, replica_groups=mesh['dp'=8,'seq'=4] {'dp'}, use_global_device_ids=true, to_apply=%region_16.17.clone | all-reduce | flops 14336 | bytes 86016
  (240 shorter events, 172.9 us)
Async XLA Ops:
  7.2 168.5 %copy-start = (bf16[1024,1024]{1,0:T(8,128)(2,1)S(1)}, bf16[1024,1024]{1,0:T(8,128)(2,1)}, u32[]{:S(2)}) copy-start(bf16[1024,1024]{1,0:T(8,128)(2,1)} %param.27) | copy-start | bytes 6291460
  7.2 86.9 %all-gather.5.cloned.1.call-start = ((), (), s32[]{:S(2)}) async-start(), calls=%async_computation.8 | async-start | bytes 7864320 | tf_op jit(solution)/shard_map/all_gather | solution.py:124
  8.8 8.4 copy-start.31
  17.8 6.3 copy-start.14
  44.0 98.6 %all-gather.3.cloned.1.call-start = ((), (), s32[]{:S(2)}) async-start(), calls=%async_computation.7 | async-start | bytes 7864320 | tf_op jit(solution)/shard_map/all_gather | solution.py:125
  47.4 364.0 %reduce-scatter.8.cloned.1.call-start = ((), (), s32[]{:S(2)}) async-start(), calls=%async_computation.9 | async-start | bytes 7864320 | tf_op jit(solution)/shard_map/reduce_scatter | solution.py:203
  47.5 158.5 %copy-start.45 = (f32[4096]{0:T(1024)}, f32[4096]{0:T(1024)S(1)}, u32[]{:S(2)}) copy-start(f32[4096]{0:T(1024)S(1)} %convert_element_type.226) | copy-start | bytes 49156
  178.7 14.8 slice-start
  181.0 12.5 slice-start.1
  193.6 12.4 copy-start.11
  352.9 119.5 %reduce-scatter.10.cloned.1.call-start = ((), (), s32[]{:S(2)}) async-start(), calls=%async_computation.10 | async-start | bytes 7864320 | tf_op jit(solution)/shard_map/reduce_scatter | solution.py:209
  386.5 177.5 %reduce-scatter.16.cloned.1.call-start = ((), (), s32[]{:S(2)}) async-start(), calls=%async_computation.13 | async-start | bytes 4718592 | tf_op jit(solution)/shard_map/reduce_scatter | solution.py:254
  393.0 237.8 %reduce-scatter.12.cloned.1.call-start = ((), (), s32[]{:S(2)}) async-start(), calls=%async_computation.11 | async-start | bytes 1179648 | tf_op jit(solution)/shard_map/reduce_scatter | solution.py:252
  416.4 56.0 %copy-start.28 = (f32[3,256]{1,0:T(4,128)S(1)}, f32[3,256]{1,0:T(4,128)}, u32[]{:S(2)}) copy-start(f32[3,256]{1,0:T(4,128)} %copy-done.27) | copy-start | bytes 9220
  416.4 56.0 %copy-start.32 = (f32[1024]{0:T(1024)S(1)}, f32[1024]{0:T(1024)}, u32[]{:S(2)}) copy-start(f32[1024]{0:T(1024)} %copy-done.31) | copy-start | bytes 12292
  420.9 62.1 %copy-start.42 = (f32[3,256]{1,0:T(4,128)S(1)}, f32[3,256]{1,0:T(4,128)}, u32[]{:S(2)}) copy-start(f32[3,256]{1,0:T(4,128)} %copy-done.41) | copy-start | bytes 9220
  420.9 62.1 %copy-start.34 = (f32[3,256]{1,0:T(4,128)S(1)}, f32[3,256]{1,0:T(4,128)}, u32[]{:S(2)}) copy-start(f32[3,256]{1,0:T(4,128)} %copy-done.33) | copy-start | bytes 9220
  472.4 10.6 copy-start.4
  490.7 425.7 %reduce-scatter.20.cloned.1.call-start = ((), (), s32[]{:S(2)}) async-start(), calls=%async_computation.15 | async-start | bytes 18874368 | tf_op jit(solution)/shard_map/reduce_scatter | solution.py:256
  507.1 695.2 %reduce-scatter.18.cloned.1.call-start = ((), (), s32[]{:S(2)}) async-start(), calls=%async_computation.14 | async-start | bytes 18874368 | tf_op jit(solution)/shard_map/reduce_scatter | solution.py:255
  519.9 892.3 %reduce-scatter.14.cloned.1.call-start = ((), (), s32[]{:S(2)}) async-start(), calls=%async_computation.12 | async-start | bytes 14155776 | tf_op jit(solution)/shard_map/reduce_scatter | solution.py:253
  532.6 952.9 %all-reduce.14.cloned.1.call-start = ((), (), s32[]{:S(2)}) async-start(), calls=%async_computation.16 | async-start | bytes 6422528 | tf_op jit(solution)/shard_map/psum | solution.py:268
  1205.1 209.6 %copy-start.54 = (u32[32]{0:T(128)S(1)}, u32[32]{0:T(128)}, u32[]{:S(2)}) copy-start(u32[32]{0:T(128)} %constant.58) | copy-start | bytes 388
  1485.5 5.9 copy-start.23
  (45 other events, 110.3 us)
Sparse Core Ops, SparseCore 0:
  44.1 49.9 all-gather.4
  96.2 46.3 all-gather.2
  353.0 58.3 reduce-scatter.7
  414.0 58.3 reduce-scatter.9
  475.9 88.0 reduce-scatter.15
  567.6 63.2 reduce-scatter.11
  634.6 281.7 reduce-scatter.19
  920.6 281.6 reduce-scatter.17
  1205.9 206.2 reduce-scatter.13
  1415.9 69.5 all-reduce.13
where the time goes:
time: 1510 us; the launch traced here: 1500 us
  waiting for transfers between devices  974 us (65%)
  matrix products  273 us (18%)
  other arithmetic  118 us (8%)
  local copies, waits for them, and re-layouts  69.8 us (5%)
  blocking collectives  48.5 us (3%)
  between operations  17.3 us (1%)
    reduce_scatter x1, waiting for transfers between devices, local(): lax.psum_scatter(down_w_part, 'dp', scatter_dimension=0, tiled=True)  284 us
    reduce_scatter x1, waiting for transfers between devices, local(): lax.psum_scatter(up_w_part, 'dp', scatter_dimension=0, tiled=True)  283 us
    reduce_scatter x1, waiting for transfers between devices, local(): lax.psum_scatter(qkv_w_part, 'dp', scatter_dimension=0, tiled=True)  207 us
    reduce_scatter x1, waiting for transfers between devices, local(): lax.psum_scatter(time_w_part, 'dp', scatter_dimension=0, tiled=True)  65.1 us
    reduce_scatter x1, waiting for transfers between devices, local(): lax.psum_scatter(grad_value_part.reshape(row_count, row_len, model_width)...  51.5 us
    dot_general x4, matrix products, contract_rows(): lax.dot_general(left_op, right_op, (((0,), (0,)), ((), ())), preferred_el...  46.4 us
    dot_general x4, matrix products, contract_cols(): lax.dot_general(left_op, right_op, (((1,), (1,)), ((), ())), preferred_el...  44.9 us
    convert_element_type x1, other arithmetic, local(): grad_scores = (probs_back * (grad_probs - row_delta)).astype(jnp.bfloat16)  40.4 us
  transfers between devices with their start and end apart: 10, of which 10 were waited for; matrix products, arithmetic and copies ran while one was open for 13% of the time, Pallas kernels for 0%

commit v1 on v0

v1 whole, which is shorter than its diff:
```python
import functools
import math

import jax
import jax.numpy as jnp
from jax import lax
from jax.experimental import pallas as pl
from jax.experimental.pallas import tpu as pltpu
from jax.sharding import Mesh, PartitionSpec as P

HEADS = 16
HEAD_DIM = 64
TEMB = 256
SEGS = 8
EPSILON = 1e-05
F32 = jnp.float32
BF16 = jnp.bfloat16
NEG = -1e30
VMEM = 60 * 1024 * 1024


def swap(value, axis):
    return lax.ppermute(value, axis, [(0, 1), (1, 0)])


def layer_norm(values, gain_vec, shift_vec):
    centred = values - jnp.mean(values, axis=-1, keepdims=True)
    spread = jnp.mean(centred * centred, axis=-1, keepdims=True)
    return centred * lax.rsqrt(spread + EPSILON) * gain_vec + shift_vec


def time_features(doc_times, feat_width):
    half_size = feat_width // 2
    frequency = jnp.exp(-math.log(10000.0) * jnp.arange(half_size, dtype=F32) / half_size)
    angles = doc_times.astype(F32)[..., None] * frequency
    return jnp.concatenate([jnp.sin(angles), jnp.cos(angles)], axis=-1)


def rotary_tables(positions, head_size):
    half_size = head_size // 2
    frequency = jnp.exp(-math.log(10000.0) * 2.0 * jnp.arange(half_size, dtype=F32) / head_size)
    angles = positions.astype(F32)[..., None] * frequency
    cos_tab, sin_tab = jnp.cos(angles), jnp.sin(angles)
    return (
        jnp.concatenate([cos_tab] * 4, axis=-1),
        jnp.concatenate([-sin_tab, sin_tab, -sin_tab, sin_tab], axis=-1),
    )


def dot(left_op, right_op, left_dim=1, right_dim=0):
    return lax.dot_general(
        left_op, right_op, (((left_dim,), (right_dim,)), ((), ())), preferred_element_type=F32
    )


def turn(values, cos_tab, sin_tab):
    slabs = []
    lane = lax.broadcasted_iota(jnp.int32, (values.shape[0], 128), 1)
    first = lane % HEAD_DIM < HEAD_DIM // 2
    for start in range(0, values.shape[1], 128):
        slab = values[:, start : start + 128]
        partner = jnp.where(
            first, pltpu.roll(slab, 128 - HEAD_DIM // 2, 1), pltpu.roll(slab, HEAD_DIM // 2, 1)
        )
        slabs.append(slab * cos_tab + partner * sin_tab)
    return jnp.concatenate(slabs, axis=1)


def qkv_body(x_ref, w_ref, b_ref, cos_ref, sin_ref, *refs):
    q_ref, k_ref, v_ref = refs[-3:]
    width = q_ref.shape[-1]
    full = dot(x_ref[0, 0], w_ref[...]) + b_ref[...]
    cos_tab, sin_tab = cos_ref[0], sin_ref[0]
    q_ref[0, 0] = (turn(full[:, :width], cos_tab, sin_tab) * HEAD_DIM**-0.5).astype(BF16)
    k_ref[0, 0] = turn(full[:, width : 2 * width], cos_tab, sin_tab).astype(BF16)
    v_ref[0, 0] = full[:, 2 * width :].astype(BF16)


def project_qkv(x, weight, bias, cos_tab, sin_tab, offset, pieces, held=()):
    count, rows, shard, model = x.shape
    width = weight.shape[1] // 3
    out = jax.ShapeDtypeStruct((pieces, rows, shard, width), BF16)
    place = pl.BlockSpec((1, 1, shard, width), lambda p, r: (p + offset, r, 0, 0))
    table = pl.BlockSpec((1, shard, 128), lambda p, r: (p + offset, 0, 0))
    return pl.pallas_call(
        qkv_body,
        grid=(count, rows),
        in_specs=[
            pl.BlockSpec((1, 1, shard, model), lambda p, r: (p, r, 0, 0)),
            pl.BlockSpec((model, 3 * width), lambda p, r: (0, 0)),
            pl.BlockSpec((1, 3 * width), lambda p, r: (0, 0)),
            table,
            table,
        ]
        + [pl.BlockSpec(memory_space=pl.ANY)] * len(held),
        out_specs=[place] * 3,
        out_shape=[out] * 3,
        input_output_aliases={5 + n: n for n in range(len(held))},
        compiler_params=pltpu.CompilerParams(vmem_limit_bytes=VMEM),
        cost_estimate=pl.CostEstimate(
            flops=2 * count * rows * shard * model * 3 * width,
            bytes_accessed=2 * (count * rows * shard * (model + 3 * width) + model * 3 * width),
            transcendentals=0,
        ),
        name="qkv",
    )(x, weight, bias, cos_tab, sin_tab, *held)


def head_masks(shape, heads):
    lane = lax.broadcasted_iota(jnp.int32, shape, 1)
    return [(lane // HEAD_DIM == h) for h in range(heads)]


def attend_body(act_ref, q_ref, k_ref, v_ref, segq_ref, segk_ref, o_ref, lse_ref, vt, acc, top, tot, qm):
    row, piece = pl.program_id(0), pl.program_id(1)
    pieces, _, shard, width = k_ref.shape
    heads = width // HEAD_DIM

    @pl.when(piece == 0)
    def _():
        for j in range(pieces):
            vt[:, j * shard : (j + 1) * shard] = v_ref[j, 0].T

    q = q_ref[0, 0]
    for h, mask in enumerate(head_masks(q.shape, heads)):
        qm[h] = jnp.where(mask, q, jnp.zeros_like(q))
    acc[...] = jnp.zeros_like(acc)
    top[...] = jnp.full_like(top, NEG)
    tot[...] = jnp.zeros_like(tot)
    seg_q = segq_ref[0, 0]
    for j in range(pieces):

        @pl.when(act_ref[(row * pieces + piece) * pieces + j] != 0)
        def _():
            k = k_ref[j, 0]
            same = segk_ref[0][:, j : j + 1] == seg_q
            for h in range(heads):
                at = slice(h * HEAD_DIM, (h + 1) * HEAD_DIM)
                s = jnp.where(same, dot(k, qm[h], 1, 1), NEG)
                m_old = top[h : h + 1]
                m_new = jnp.maximum(m_old, jnp.max(s, axis=0, keepdims=True))
                fade = jnp.exp(m_old - m_new)
                p = jnp.exp(s - m_new)
                tot[h : h + 1] = tot[h : h + 1] * fade + jnp.sum(p, axis=0, keepdims=True)
                top[h : h + 1] = m_new
                acc[at] = acc[at] * fade + dot(
                    vt[at, j * shard : (j + 1) * shard], p.astype(BF16)
                )

    for h in range(heads):
        at = slice(h * HEAD_DIM, (h + 1) * HEAD_DIM)
        acc[at] = acc[at] / tot[h : h + 1]
    o_ref[0, 0] = acc[...].T.astype(BF16)
    lse_ref[0, 0] = top[...] + jnp.log(jnp.maximum(tot[...], 1e-30))


def attend(act, q, k, v, seg_row, seg_col):
    pieces, rows, shard, width = q.shape
    heads = width // HEAD_DIM
    one = pl.BlockSpec((1, 1, shard, width), lambda r, i, a: (i, r, 0, 0))
    whole = pl.BlockSpec((pieces, 1, shard, width), lambda r, i, a: (0, r, 0, 0))
    return pl.pallas_call(
        attend_body,
        grid_spec=pltpu.PrefetchScalarGridSpec(
            num_scalar_prefetch=1,
            grid=(rows, pieces),
            in_specs=[
                one,
                whole,
                whole,
                pl.BlockSpec((1, 1, 1, shard), lambda r, i, a: (r, i, 0, 0)),
                pl.BlockSpec((1, shard, pieces), lambda r, i, a: (r, 0, 0)),
            ],
            out_specs=[one, pl.BlockSpec((1, 1, 8, shard), lambda r, i, a: (r, i, 0, 0))],
            scratch_shapes=[
                pltpu.VMEM((width, pieces * shard), BF16),
                pltpu.VMEM((width, shard), F32),
                pltpu.VMEM((8, shard), F32),
                pltpu.VMEM((8, shard), F32),
                pltpu.VMEM((heads, shard, width), BF16),
            ],
        ),
        out_shape=[
            jax.ShapeDtypeStruct(q.shape, BF16),
            jax.ShapeDtypeStruct((rows, pieces, 8, shard), F32),
        ],
        compiler_params=pltpu.CompilerParams(vmem_limit_bytes=VMEM),
        cost_estimate=pl.CostEstimate(
            flops=4 * rows * (pieces * shard) ** 2 * width * 2,
            bytes_accessed=8 * rows * pieces * shard * width,
            transcendentals=rows * (pieces * shard) ** 2 * heads,
        ),
        name="attend",
    )(act, q, k, v, seg_row, seg_col)


def attend_back_body(
    act_ref, q_ref, k_ref, v_ref, o_ref, do_ref, lse_ref, segq_ref, segk_ref, cos_ref, sin_ref,
    g_ref, kt, dk, dv, dqt, qm, gm,
):
    row, piece = pl.program_id(0), pl.program_id(1)
    pieces, _, shard, width = k_ref.shape
    heads = width // HEAD_DIM

    @pl.when(piece == 0)
    def _():
        for j in range(pieces):
            kt[:, j * shard : (j + 1) * shard] = k_ref[j, 0].T
        dk[...] = jnp.zeros_like(dk)
        dv[...] = jnp.zeros_like(dv)

    q, do = q_ref[0, 0], do_ref[0, 0]
    for h, mask in enumerate(head_masks(q.shape, heads)):
        qm[h] = jnp.where(mask, q, jnp.zeros_like(q))
        gm[h] = jnp.where(mask, do, jnp.zeros_like(do))
    dqt[...] = jnp.zeros_like(dqt)
    prod = do.astype(F32) * o_ref[0, 0].astype(F32)
    prod_hi = prod.astype(BF16)
    prod_lo = (prod - prod_hi.astype(F32)).astype(BF16)
    pick = (
        lax.broadcasted_iota(jnp.int32, (8, width), 1) // HEAD_DIM
        == lax.broadcasted_iota(jnp.int32, (8, width), 0)
    ).astype(BF16)
    delta = dot(pick, prod_hi, 1, 1) + dot(pick, prod_lo, 1, 1)
    lse = lse_ref[0, 0]
    seg_q = segq_ref[0, 0]
    for j in range(pieces):

        @pl.when(act_ref[(row * pieces + piece) * pieces + j] != 0)
        def _():
            k, v = k_ref[j, 0], v_ref[j, 0]
            same = segk_ref[0][:, j : j + 1] == seg_q
            dk_sum = dk[j]
            dv_sum = dv[j]
            for h in range(heads):
                at = slice(h * HEAD_DIM, (h + 1) * HEAD_DIM)
                s = dot(k, qm[h], 1, 1)
                p = jnp.exp(jnp.where(same, s - lse[h : h + 1], NEG))
                dp = dot(v, gm[h], 1, 1)
                ds = (p * (dp - delta[h : h + 1])).astype(BF16)
                dv_sum = dv_sum + dot(p.astype(BF16), gm[h])
                dk_sum = dk_sum + dot(ds, qm[h])
                dqt[at] = dqt[at] + dot(kt[at, j * shard : (j + 1) * shard], ds)
            dk[j] = dk_sum
            dv[j] = dv_sum

    g_ref[piece, 0, :, 0:width] = turn(
        dqt[...].T * HEAD_DIM**-0.5, cos_ref[piece], -sin_ref[piece]
    ).astype(BF16)

    @pl.when(piece == pieces - 1)
    def _():
        for j in range(pieces):
            g_ref[j, 0, :, width : 2 * width] = turn(dk[j], cos_ref[j], -sin_ref[j]).astype(BF16)
            g_ref[j, 0, :, 2 * width :] = dv[j].astype(BF16)


def attend_back(act, q, k, v, o, do, lse, seg_row, seg_col, cos_tab, sin_tab):
    pieces, rows, shard, width = q.shape
    heads = width // HEAD_DIM
    one = pl.BlockSpec((1, 1, shard, width), lambda r, i, a: (i, r, 0, 0))
    whole = pl.BlockSpec((pieces, 1, shard, width), lambda r, i, a: (0, r, 0, 0))
    table = pl.BlockSpec((pieces, shard, 128), lambda r, i, a: (0, 0, 0))
    return pl.pallas_call(
        attend_back_body,
        grid_spec=pltpu.PrefetchScalarGridSpec(
            num_scalar_prefetch=1,
            grid=(rows, pieces),
            in_specs=[
                one,
                whole,
                whole,
                one,
                one,
                pl.BlockSpec((1, 1, 8, shard), lambda r, i, a: (r, i, 0, 0)),
                pl.BlockSpec((1, 1, 1, shard), lambda r, i, a: (r, i, 0, 0)),
                pl.BlockSpec((1, shard, pieces), lambda r, i, a: (r, 0, 0)),
                table,
                table,
            ],
            out_specs=pl.BlockSpec((pieces, 1, shard, 3 * width), lambda r, i, a: (0, r, 0, 0)),
            scratch_shapes=[
                pltpu.VMEM((width, pieces * shard), BF16),
                pltpu.VMEM((pieces, shard, width), F32),
                pltpu.VMEM((pieces, shard, width), F32),
                pltpu.VMEM((width, shard), F32),
                pltpu.VMEM((heads, shard, width), BF16),
                pltpu.VMEM((heads, shard, width), BF16),
            ],
        ),
        out_shape=jax.ShapeDtypeStruct((pieces, rows, shard, 3 * width), BF16),
        compiler_params=pltpu.CompilerParams(vmem_limit_bytes=VMEM),
        cost_estimate=pl.CostEstimate(
            flops=10 * rows * (pieces * shard) ** 2 * width * 2,
            bytes_accessed=16 * rows * pieces * shard * width,
            transcendentals=rows * (pieces * shard) ** 2 * heads,
        ),
        name="attend_back",
    )(act, q, k, v, o, do, lse, seg_row, seg_col, cos_tab, sin_tab)


def spread(own):
    one = swap(own, "c")
    two = swap(own, "y")
    three = swap(two, "c")
    return own, one, two, three


def exchange(parts):
    far = swap(parts[2:4], "y")
    return parts[0], swap(parts[1], "c"), far[0], swap(far[1], "c")


def pick(values, index, axis):
    return lax.dynamic_index_in_dim(values, index, axis, keepdims=False)


def local(
    inputs, segment_ids, doc_times, time_weight, time_bias, norm1_gain, norm1_bias, qkv_weight, qkv_bias,
    out_weight, out_bias, norm2_gain, norm2_bias, up_weight, up_bias, down_weight, down_bias, cotangent,
    *, dp,
):
    rows, shard, model = inputs.shape
    parts = 4
    tokens = rows * shard
    hidden_width = up_weight.shape[1]
    width = model // parts
    highest = lax.Precision.HIGHEST
    x_at, y_at, c_at = lax.axis_index("x"), lax.axis_index("y"), lax.axis_index("c")
    me = 2 * y_at + c_at
    order = [me ^ i for i in range(parts)]

    segs = jnp.stack(spread(segment_ids), axis=1)
    seg_row = segs[:, :, None, :]
    seg_col = segs.transpose(0, 2, 1)
    low_id, high_id = segs.min(axis=2), segs.max(axis=2)
    act = (low_id[:, :, None] <= high_id[:, None, :]) & (low_id[:, None, :] <= high_id[:, :, None])
    act = act.astype(jnp.int32).reshape(-1)
    positions = jnp.stack([o * shard + jnp.arange(shard, dtype=jnp.int32) for o in order])
    cos_tab, sin_tab = rotary_tables(positions, HEAD_DIM)

    doc_slots = jnp.arange(SEGS, dtype=jnp.int32)
    onehot = (segment_ids[..., None] == doc_slots).astype(F32)
    features = time_features(doc_times, TEMB).astype(BF16)
    time_shift = jnp.dot(features.reshape(rows * SEGS, TEMB), time_weight, preferred_element_type=F32)
    time_shift = time_shift.reshape(rows, SEGS, model) + time_bias.astype(F32)
    stream = inputs.astype(F32) + jnp.einsum("rsg,rgd->rsd", onehot, time_shift, precision=highest)
    normed1, norm1_back = jax.vjp(layer_norm, stream, norm1_gain.astype(F32), norm1_bias.astype(F32))
    own1, one1, two1, three1 = spread(normed1.astype(BF16))
    near1, far1 = jnp.stack([own1, one1]), jnp.stack([two1, three1])

    qkv_own = pick(qkv_weight.reshape(model, 3, parts, width), me, 2).reshape(model, 3 * width)
    qkv_bias_own = pick(qkv_bias.reshape(3, parts, width), me, 1).reshape(1, 3 * width).astype(F32)
    held = project_qkv(near1, qkv_own, qkv_bias_own, cos_tab, sin_tab, 0, parts)
    q, k, v = project_qkv(far1, qkv_own, qkv_bias_own, cos_tab, sin_tab, 2, parts, held)
    o, lse = attend(act, q, k, v, seg_row, seg_col)
    attended = jnp.concatenate([p.reshape(tokens, width) for p in exchange(o)], axis=1)
    out_blocks = out_weight.reshape(parts, width, model)
    out_own = jnp.concatenate([pick(out_blocks, o_at, 0) for o_at in order], axis=0)
    branch = dot(attended, out_own) + out_bias.astype(F32)
    middle = stream + branch.reshape(rows, shard, model)
    normed2, norm2_back = jax.vjp(layer_norm, middle, norm2_gain.astype(F32), norm2_bias.astype(F32))
    normed2 = normed2.astype(BF16).reshape(tokens, model)

    piece = hidden_width // (2 * dp)
    half = hidden_width // 2
    up_own = pick(up_weight.reshape(model, dp, 2, piece), c_at, 2).reshape(model, half)
    up_bias_own = pick(up_bias.reshape(dp, 2, piece), c_at, 1).reshape(half).astype(F32)
    down_own = pick(down_weight.reshape(dp, 2, piece, model), c_at, 1).reshape(half, model)
    cot = cotangent.reshape(tokens, model)
    cot_both = jnp.concatenate([cot, swap(cot, "c")], axis=0)
    normed2_both = jnp.concatenate([normed2, swap(normed2, "c")], axis=0)
    hidden = dot(normed2_both, up_own) + up_bias_own
    active, gate_back = jax.vjp(functools.partial(jax.nn.gelu, approximate=True), hidden)
    active = active.astype(BF16)
    feed = dot(active, down_own)
    feed = feed[:tokens] + swap(feed[tokens:].astype(BF16), "c").astype(F32)
    output = (middle + (feed + down_bias.astype(F32)).reshape(rows, shard, model)).astype(BF16)
    down_grad = dot(active, cot_both, 0, 0).astype(BF16)
    grad_hidden = gate_back(dot(cot_both, down_own, 1, 1))[0].astype(BF16)
    grad_normed2 = dot(grad_hidden, up_own, 1, 1)
    up_grad = dot(normed2_both, grad_hidden, 0, 0).astype(BF16)
    grad_normed2 = grad_normed2[:tokens] + swap(grad_normed2[tokens:].astype(BF16), "c").astype(F32)
    grad_mid_norm, gain2_grad, shift2_grad = norm2_back(grad_normed2.reshape(rows, shard, model))
    grad_middle = cotangent.astype(F32) + grad_mid_norm
    grad_middle_low = grad_middle.astype(BF16).reshape(tokens, model)

    grad_att = dot(grad_middle_low, out_own, 1, 1).astype(BF16)
    grad_att = jnp.stack(
        [grad_att[:, i * width : (i + 1) * width].reshape(rows, shard, width) for i in range(parts)]
    )
    grad_o = jnp.stack(exchange(grad_att))
    out_grad = dot(attended, grad_middle_low, 0, 0).reshape(parts, width, model)
    out_grad = jnp.concatenate([pick(out_grad, o_at, 0) for o_at in order], axis=0).astype(BF16)
    grad_qkv = attend_back(act, q, k, v, o, grad_o, lse, seg_row, seg_col, cos_tab, sin_tab)
    grad_near = grad_qkv[:2].reshape(2 * tokens, 3 * width)
    grad_far = grad_qkv[2:].reshape(2 * tokens, 3 * width)
    qkv_grad = (
        dot(near1.reshape(2 * tokens, model), grad_near, 0, 0)
        + dot(far1.reshape(2 * tokens, model), grad_far, 0, 0)
    ).astype(BF16)
    part1 = dot(grad_qkv.reshape(4 * tokens, 3 * width), qkv_own, 1, 1).astype(BF16)
    part1 = part1.reshape(4, tokens, model)
    here = part1[0].astype(F32) + swap(part1[1], "c").astype(F32)
    there = part1[2].astype(F32) + swap(part1[3], "c").astype(F32)
    grad_normed1 = here + swap(there.astype(BF16), "y").astype(F32)
    grad_norm, gain1_grad, shift1_grad = norm1_back(grad_normed1.reshape(rows, shard, model))
    grad_stream = grad_middle + grad_norm
    input_grad = grad_stream.astype(BF16)
    grad_shift = jnp.einsum("rsg,rsd->rgd", onehot, grad_stream, precision=highest)
    time_b_grad = jnp.sum(grad_shift, axis=(0, 1))
    time_w_grad = jnp.einsum("rgt,rgd->td", features.astype(F32), grad_shift, precision=highest)

    depth = dp // 2

    def halve(values, axis_name, at, dim):
        shape = values.shape
        split = values.reshape(shape[:dim] + (2, shape[dim] // 2) + shape[dim + 1 :])
        sent = swap(pick(split, 1 - at, dim), axis_name)
        return (pick(split, at, dim).astype(F32) + sent.astype(F32)).astype(BF16)

    def over_x(values):
        split = values.reshape(depth, 2, values.shape[0] // dp, values.shape[1])
        sent = swap(pick(split, 1 - x_at, 1), "x")
        return (pick(split, x_at, 1).astype(F32) + sent.astype(F32)).astype(BF16)

    def over_z(values):
        return lax.psum_scatter(values, "z", scatter_dimension=0, tiled=False)

    def join(values, axis_name, at):
        other = swap(values, axis_name)
        return jnp.where(at == 0, jnp.stack([values, other]), jnp.stack([other, values]))

    down_sum = over_z(halve(over_x(down_grad), "y", y_at, 2))
    up_sum = over_z(over_x(halve(up_grad, "y", y_at, 1)))
    out_sum = over_z(over_x(halve(halve(out_grad, "c", c_at, 1), "y", y_at, 1)))
    qkv_sum = over_z(over_x(qkv_grad))
    down_done = join(jnp.concatenate(list(join(down_sum, "y", y_at)), axis=1), "c", c_at)
    down_done = down_done.reshape(hidden_width // dp, model).astype(F32)
    up_done = join(jnp.concatenate(list(join(up_sum, "y", y_at)), axis=1), "c", c_at)
    up_done = up_done.reshape(2, model // dp, dp, piece).transpose(1, 2, 0, 3)
    up_done = up_done.reshape(model // dp, hidden_width).astype(F32)
    out_done = join(jnp.concatenate(list(join(out_sum, "y", y_at)), axis=1), "c", c_at)
    out_done = jnp.concatenate(list(out_done), axis=1).astype(F32)
    qkv_done = join(join(qkv_sum, "c", c_at), "y", y_at).reshape(parts, model // dp, 3, width)
    qkv_done = qkv_done.transpose(1, 2, 0, 3).reshape(model // dp, 3 * model).astype(F32)

    def total(values):
        return jnp.sum(values.astype(F32), axis=0)

    up_b = total(grad_hidden).reshape(dp, 1, piece)
    up_b = jnp.where(jnp.arange(2)[:, None] == c_at, up_b, 0.0).reshape(hidden_width)
    qkv_b = total(grad_qkv.reshape(4 * tokens, 3 * width)).reshape(3, 1, width)
    qkv_b = jnp.where(jnp.arange(parts)[:, None] == me, qkv_b, 0.0).reshape(3 * model)
    vectors = [
        time_b_grad, gain1_grad, shift1_grad, qkv_b, total(grad_middle_low), gain2_grad, shift2_grad, up_b, total(cot),
    ]
    small = [time_w_grad] + vectors
    small = jnp.concatenate([s.reshape(dp, -1) for s in small], axis=1).astype(BF16)
    small = small.astype(F32) + swap(small, "c").astype(F32)
    small = small + swap(small.astype(BF16), "y").astype(F32)
    small = over_z(over_x(small.astype(BF16)))[0].astype(F32)
    done = []
    start = 0
    for s in [time_w_grad] + vectors:
        done.append(small[start : start + s.size // dp])
        start += s.size // dp
    time_w_done = done[0].reshape(TEMB // dp, model)
    return (
        output, input_grad, time_w_done, done[1], done[2], done[3], qkv_done, done[4], out_done, done[5],
        done[6], done[7], up_done, done[8], down_done, done[9],
    )


def solution(mesh):
    dp, seq = mesh.shape["dp"], mesh.shape["seq"]
    fine = Mesh(mesh.devices.reshape(dp // 2, 2, seq // 2, 2), ("z", "x", "y", "c"))
    rows, seqs = ("z", "x"), ("y", "c")
    placed = (P(rows, seqs, None), P(rows, seqs), P(rows, None)) + (P(),) * 14 + (P(rows, seqs, None),)
    vec, mat = P(rows), P(rows, None)
    return jax.shard_map(
        functools.partial(local, dp=dp),
        mesh=fine,
        in_specs=placed,
        out_specs=(
            P(rows, seqs, None), P(rows, seqs, None), mat, vec, vec, vec, mat, vec, mat, vec, vec, vec, mat, vec, mat, vec,
        ),
        check_vma=False,
    )
```

time: 1510 us -> 724 us (0.48)
  waiting for transfers between devices: 974 us -> 212 us
  matrix products: 273 us -> 104 us
  Pallas kernels: 0 us -> 124 us
  local copies, waits for them, and re-layouts: 69.8 us -> 151 us
  blocking collectives: 48.5 us -> 0 us
  other arithmetic: 118 us -> 94.3 us
  starting transfers between devices: 1.05 us -> 21.9 us
    reduce_scatter x7 -> x4, waiting for transfers between devices: 925 us -> 14.8 us  [over_z(): return lax.psum_scatter(values, 'z', scatter_dimension=0, tiled=False)]
    dot_general x20 -> x14, matrix products: 269 us -> 99.5 us  [the longest x12 98.7 us: dot(): lax.dot_general(left_op, right_op, (((left_dim,), (right_dim,)), ((), ())...]
    ppermute x0 -> x38, waiting for transfers between devices: none -> 160 us  [swap(): return lax.ppermute(value, axis, [(0, 1), (1, 0)])]
    pallas_call x0 -> x4, Pallas kernels: none -> 124 us  [the longest x1 60.3 us: attend_back(): pl.pallas_call(attend_back_body, grid_spec=pltpu.PrefetchScalarGridSpec(n...]
    dynamic_slice x0 -> x13, local copies, waits for them, and re-layouts: none -> 44.6 us  [pick(): return lax.dynamic_index_in_dim(values, index, axis, keepdims=False)]
    all_gather x2 -> x0, waiting for transfers between devices: 41.4 us -> none  [the longest x1 39.6 us: local(): lax.all_gather(keys_flat, 'seq', axis=1, tiled=True)]
    unnamed x131 -> x174, local copies, waits for them, and re-layouts: 14 us -> 53.1 us
    unnamed x10 -> x6, waiting for transfers between devices: 0.16 us -> 37 us
  transfers between devices with their start and end apart: 10 -> 43, of which waited for: 10 -> 13; matrix products, arithmetic and copies ran while one was open for 13% -> 39% of each run, Pallas kernels for 0% -> 9%
where the time goes in v1:
time: 724 us; the launch traced here: 721 us
  waiting for transfers between devices  212 us (29%)
  local copies, waits for them, and re-layouts  151 us (21%)
  Pallas kernels  124 us (17%)
  matrix products  104 us (14%)
  other arithmetic  94.3 us (13%)
  starting transfers between devices  21.9 us (3%)
  between operations  15.3 us (2%)
    ppermute x38, waiting for transfers between devices, swap(): return lax.ppermute(value, axis, [(0, 1), (1, 0)])  160 us
    dot_general x12, matrix products, dot(): lax.dot_general(left_op, right_op, (((left_dim,), (right_dim,)), ((), ())...  98.7 us
    pallas_call x1, Pallas kernels, attend_back(): pl.pallas_call(attend_back_body, grid_spec=pltpu.PrefetchScalarGridSpec(n...  60.3 us
    unnamed x174, local copies, waits for them, and re-layouts  53.1 us
    pallas_call x1, Pallas kernels, attend(): pl.pallas_call(attend_body, grid_spec=pltpu.PrefetchScalarGridSpec(num_sc...  47.7 us
    dynamic_slice x13, local copies, waits for them, and re-layouts, pick(): return lax.dynamic_index_in_dim(values, index, axis, keepdims=False)  44.6 us
    unnamed x6, waiting for transfers between devices  37 us
    ppermute x38, starting transfers between devices, swap(): return lax.ppermute(value, axis, [(0, 1), (1, 0)])  21.7 us
  transfers between devices with their start and end apart: 43, of which 13 were waited for; matrix products, arithmetic and copies ran while one was open for 39% of the time, Pallas kernels for 9%

profile of v1, /device:TPU:0, one launch (start us, length us, event | category | flops | bytes accessed | tf_op | source)
XLA Modules:
  0.0 721.3 jit_solution(7671981340067397207)
XLA Ops:
  20.8 8.8 %copy.241 = bf16[1024,3072]{0,1:T(8,128)(2,1)} copy(bf16[1024,3072]{1,0:T(8,128)(2,1)} %param.25) | data formatting | bytes 12582912 | tf_op args[7]
  31.5 23.5 %collective-permute-done.3 = bf16[3,256,1024]{2,1,0:T(8,128)(2,1)} collective-permute-done((bf16[3,256,1024]{2,1,0:T(8,128)(2,1)}, bf16[3,256,1024]{2,1,0:T(8,128)(2,1)}, u32[]{:S(2)}, u32[]{:S(2)}) %collective-permute-start.3) | collective-permute-done | bytes 1572896 | tf_op jit(solution)/shard_map/ppermute | solution.py:23
  76.4 7.8 %qkv.2 = (bf16[4,3,256,256]{3,2,1,0:T(8,128)(2,1)}, bf16[4,3,256,256]{3,2,1,0:T(8,128)(2,1)}, bf16[4,3,256,256]{3,2,1,0:T(8,128)(2,1)}) custom-call(bf16[2,3,256,1024]{3,2,1,0:T(8,128)(2,1)} %pad_maximum_fusion.1.x_ref, bf16[1024,768]{1,0:T(8,128)(2,1)} %copy.243.w_ref, f32[1,768]{1,0:T(1,128)} %convert.105.b_ref, ...), custom_call_target="tpu_custom_call" | custom-call | flops 2415919104 | bytes 7077888 | tf_op jit(solution)/shard_map/qkv/pallas_call | solution.py:85
  88.0 7.8 %qkv.3 = (bf16[4,3,256,256]{3,2,1,0:T(8,128)(2,1)}, bf16[4,3,256,256]{3,2,1,0:T(8,128)(2,1)}, bf16[4,3,256,256]{3,2,1,0:T(8,128)(2,1)}) custom-call(bf16[2,3,256,1024]{3,2,1,0:T(8,128)(2,1)} %pad_maximum_fusion.x_ref, bf16[1024,768]{1,0:T(8,128)(2,1)} %copy.243.w_ref, ...), custom_call_target="tpu_custom_call", output_to_operand_aliasing={{0}: (5, {}), {1}: (6, {}), {2}: (7, {})} | custom-call | flops 2415919104 | bytes 7077888 | tf_op jit(solution)/shard_map/qkv/pallas_call | solution.py:85
  95.8 47.7 %attend.1 = (bf16[4,3,256,256]{3,2,1,0:T(8,128)(2,1)}, f32[3,4,8,256]{3,2,1,0:T(8,128)}) custom-call(s32[48]{0:T(128)} %reshape.547.act_ref, bf16[4,3,256,256]{3,2,1,0:T(8,128)(2,1)} %get-tuple-element.27.q_ref, bf16[4,3,256,256]{3,2,1,0:T(8,128)(2,1)} %get-tuple-element.28.k_ref, bf16[4,3,256,256]{3,2,1,0:T(8,128)(2,1)} %get-tuple-element.29.v_ref, ...), custom_call_target="tpu_custom_call" | custom-call | flops 6442450944 | bytes 6291456 | tf_op jit(solution)/shard_map/attend/pallas_call | solution.py:162
  148.4 15.8 %collective-permute-done.7 = bf16[2,3,256,256]{3,2,1,0:T(8,128)(2,1)S(1)} collective-permute-done((bf16[2,3,256,256]{3,2,1,0:T(8,128)(2,1)S(1)}, bf16[2,3,256,256]{3,2,1,0:T(8,128)(2,1)S(1)}, u32[]{:S(2)}, u32[]{:S(2)}) %collective-permute-start.7) | collective-permute-done | bytes 786464 | tf_op jit(solution)/shard_map/ppermute | solution.py:23
  175.1 12.0 %copy.245 = bf16[1024,4096]{0,1:T(8,128)(2,1)} copy(bf16[1024,4096]{1,0:T(8,128)(2,1)} %param.31) | data formatting | bytes 16777216 | tf_op args[13]
  200.6 16.2 %multiply_convert_fusion = (bf16[1536,2048]{1,0:T(8,128)(2,1)}, f32[1536,2048]{1,0:T(8,128)}) fusion(f32[2048]{0:T(1024)S(1)} %bitcast.283, bf16[1024,2048]{0,1:T(8,128)(2,1)} %bitcast.242, bf16[768,1024]{1,0:T(8,128)(2,1)} %collective-permute-done.9, bf16[768,1024]{1,0:T(8,128)(2,1)} %bitcast.27), kind=kOutput, calls=%fused_computation.10 | convolution fusion | flops 6480199680 | bytes 26222592 | tf_op jit(solution)/shard_map/dot_general | solution.py:51
  216.9 20.4 %convert_reduce_fusion = (bf16[2048]{0:T(1024)(128)(2,1)}, bf16[1536,2048]{1,0:T(8,128)(2,1)}) fusion(f32[1536,2048]{1,0:T(8,128)} %get-tuple-element.206, f32[2048]{0:T(1024)S(1)} %bitcast.284, bf16[2048,1024]{1,0:T(8,128)(2,1)S(1)} %bitcast.240, bf16[768,1024]{1,0:T(8,128)(2,1)} %collective-permute-done.11, bf16[768,1024]{1,0:T(8,128)(2,1)S(1)} %bitcast.233), kind=kOutput, calls=%fused_computation.9 | convolution fusion | flops 6521092096 | bytes 26226688 | tf_op jit(solution)/shard_map/dot_general | solution.py:51
  237.3 9.0 %fusion.67 = f32[1536,1024]{1,0:T(8,128)S(1)} fusion(bf16[1536,2048]{1,0:T(8,128)(2,1)} %get-tuple-element.210, bf16[1024,2048]{0,1:T(8,128)(2,1)S(1)} %bitcast.243), kind=kOutput, calls=%fused_computation.228 | convolution fusion | flops 6442450944 | bytes 16777216 | tf_op jit(solution)/shard_map/dot_general | solution.py:51
  261.1 10.3 %convolution_convert_fusion.2 = bf16[1024,2048]{1,0:T(8,128)(2,1)} fusion(bf16[1536,2048]{1,0:T(8,128)(2,1)S(1)} %bitcast.290, bf16[768,1024]{1,0:T(8,128)(2,1)} %collective-permute-done.9, bf16[768,1024]{1,0:T(8,128)(2,1)} %bitcast.27), kind=kOutput, calls=%fused_computation.20 | convolution fusion | flops 6450839552 | bytes 13631488 | tf_op jit(solution)/shard_map/dot_general | solution.py:51
  271.4 8.0 %reshape.543 = bf16[1024,2,1024]{2,1,0:T(2,128)(2,1)} reshape(bf16[1024,2048]{1,0:T(8,128)(2,1)} %convolution_convert_fusion.2) | data formatting | bytes 8388608 | tf_op jit(solution)/shard_map/reshape | solution.py:418
  279.3 11.3 %constant_dynamic-slice_fusion.5 = (bf16[1024,1,1024]{2,1,0:T(2,128)(2,1)}, bf16[1024,1,1024]{2,1,0:T(2,128)(2,1)S(1)}) fusion(bf16[1024,2,1024]{2,1,0:T(2,128)(2,1)} %reshape.543, s32[]{:T(128)S(6)} %select_n.179, s32[]{:T(128)S(6)} %select_n.180), kind=kLoop, calls=%fused_computation.165 | loop fusion | bytes 8388616 | tf_op jit(solution)/shard_map/jit(dynamic_index_in_dim)/dynamic_slice | solution.py:315
  330.2 11.3 %convolution_convert_fusion.1 = bf16[2048,1024]{1,0:T(8,128)(2,1)} fusion(bf16[1536,2048]{1,0:T(8,128)(2,1)} %get-tuple-element.205, bf16[768,1024]{1,0:T(8,128)(2,1)} %collective-permute-done.11, bf16[768,1024]{1,0:T(8,128)(2,1)S(1)} %bitcast.234), kind=kOutput, calls=%fused_computation.19 | convolution fusion | flops 6450839552 | bytes 13631488 | tf_op jit(solution)/shard_map/dot_general | solution.py:51
  341.8 16.2 %collective-permute-done.14 = bf16[2,3,256,256]{3,2,1,0:T(8,128)(2,1)} collective-permute-done((bf16[2,3,256,256]{3,2,1,0:T(8,128)(2,1)}, bf16[2,3,256,256]{3,2,1,0:T(8,128)(2,1)}, u32[]{:S(2)}, u32[]{:S(2)}) %collective-permute-start.14) | collective-permute-done | bytes 786464 | tf_op jit(solution)/shard_map/ppermute | solution.py:23
  373.3 60.3 %attend_back.1 = bf16[4,3,256,768]{3,2,1,0:T(8,128)(2,1)} custom-call(s32[48]{0:T(128)} %reshape.547.act_ref, bf16[4,3,256,256]{3,2,1,0:T(8,128)(2,1)} %get-tuple-element.27.q_ref, bf16[4,3,256,256]{3,2,1,0:T(8,128)(2,1)} %get-tuple-element.28.k_ref, bf16[4,3,256,256]{3,2,1,0:T(8,128)(2,1)} %get-tuple-element.29.v_ref, ...), custom_call_target="tpu_custom_call" | custom-call | flops 16106127360 | bytes 12582912 | tf_op jit(solution)/shard_map/attend_back/pallas_call | solution.py:264
  460.3 13.2 %collective-permute-done.27 = bf16[4,128,256]{2,1,0:T(8,128)(2,1)} collective-permute-done((bf16[4,128,256]{2,1,0:T(8,128)(2,1)S(1)}, bf16[4,128,256]{2,1,0:T(8,128)(2,1)}, u32[]{:S(2)}, u32[]{:S(2)}) %collective-permute-start.27) | collective-permute-done | bytes 262176 | tf_op jit(solution)/shard_map/ppermute | solution.py:23
  494.2 24.3 %collective-permute-done.34 = bf16[4,256,1024]{1,2,0:T(8,128)(2,1)} collective-permute-done((bf16[4,256,1024]{1,2,0:T(8,128)(2,1)}, bf16[4,256,1024]{1,2,0:T(8,128)(2,1)}, u32[]{:S(2)}, u32[]{:S(2)}) %collective-permute-start.34) | collective-permute-done | bytes 2097184 | tf_op jit(solution)/shard_map/ppermute | solution.py:23
  522.5 17.8 %collective-permute-done.31 = bf16[4,128,1024]{1,2,0:T(8,128)(2,1)} collective-permute-done((bf16[4,128,1024]{1,2,0:T(8,128)(2,1)}, bf16[4,128,1024]{1,2,0:T(8,128)(2,1)}, u32[]{:S(2)}, u32[]{:S(2)}) %collective-permute-start.31) | collective-permute-done | bytes 1048608 | tf_op jit(solution)/shard_map/ppermute | solution.py:23
  542.8 7.6 %convolution_convert_fusion = bf16[3072,1024]{1,0:T(8,128)(2,1)S(1)} fusion(bf16[3072,768]{1,0:T(8,128)(2,1)} %bitcast.238, bf16[1024,768]{0,1:T(8,128)(2,1)} %bitcast.237), kind=kOutput, calls=%fused_computation.12 | convolution fusion | flops 4834983936 | bytes 12582912 | tf_op jit(solution)/shard_map/dot_general | solution.py:51
  554.9 25.1 %collective-permute-done.35 = bf16[4,256,512]{1,2,0:T(8,128)(2,1)S(1)} collective-permute-done((bf16[4,256,512]{1,2,0:T(8,128)(2,1)S(1)}, bf16[4,256,512]{1,2,0:T(8,128)(2,1)S(1)}, u32[]{:S(2)}, u32[]{:S(2)}) %collective-permute-start.35) | collective-permute-done | bytes 1048608 | tf_op jit(solution)/shard_map/ppermute | solution.py:23
  597.8 14.8 %reduce-scatter.11.cloned.1.call-done = bf16[1,256,512]{1,2,0:T(8,128)(2,1)} async-done(((bf16[4,256,512]{1,2,0:T(8,128)(2,1)}), bf16[1,256,512]{1,2,0:T(8,128)(2,1)}) %reduce-scatter.11.cloned.1.call-update) | async-done | bytes 262160 | tf_op jit(solution)/shard_map/reduce_scatter | solution.py:428
  645.9 9.7 %collective-permute-done.20 = bf16[8,34560]{1,0:T(8,128)(2,1)S(1)} collective-permute-done((bf16[8,34560]{1,0:T(8,128)(2,1)S(1)}, bf16[8,34560]{1,0:T(8,128)(2,1)S(1)}, u32[]{:S(2)}, u32[]{:S(2)}) %collective-permute-start.20) | collective-permute-done | bytes 552992 | tf_op jit(solution)/shard_map/ppermute | solution.py:23
  673.2 36.9 %all-reduce.3.cloned.1.call-done = bf16[4,1,34560]{2,1,0:T(2,128)(2,1)} async-done(((bf16[4,1,34560]{2,1,0:T(2,128)(2,1)}), bf16[4,1,34560]{2,1,0:T(2,128)(2,1)}) %all-reduce.3.cloned.1.call-update) | async-done | bytes 276496
  (409 shorter events, 270.4 us)
Async XLA Ops:
  7.2 576.0 %reduce-scatter.7.cloned.1.call-start = ((), (), s32[]{:S(2)}) async-start(), calls=%async_computation.5 | async-start | bytes 327680 | tf_op jit(solution)/shard_map/reduce_scatter | solution.py:428
  17.3 37.7 %collective-permute-start.3 = (bf16[3,256,1024]{2,1,0:T(8,128)(2,1)}, bf16[3,256,1024]{2,1,0:T(8,128)(2,1)}, u32[]{:S(2)}, u32[]{:S(2)}) collective-permute-start(bf16[3,256,1024]{2,1,0:T(8,128)(2,1)} %add_convert_fusion.3), channel_id=1, source_target_pairs={{0,2},{2,0},{1,3},{3,1},{4,6},{6,4},{5,7},{7,5},{8,10},{10,8},{9,1... | collective-permute-start | bytes 4718600 | tf_op jit(solution)/shard_map/ppermute | solution.py:23
  20.2 41.7 %collective-permute-start.1 = (s32[3,256]{1,0:T(4,128)S(1)}, s32[3,256]{1,0:T(4,128)S(1)}, u32[]{:S(2)}, u32[]{:S(2)}) collective-permute-start(s32[3,256]{1,0:T(4,128)S(1)} %copy-done.43), channel_id=1, source_target_pairs={{0,2},{2,0},{1,3},{3,1},{4,6},{6,4},{5,7},{7,5},{8,10},{10,8},{9,1... | collective-permute-start | bytes 9224 | tf_op jit(solution)/shard_map/ppermute | solution.py:23
  20.3 47.3 %collective-permute-start = (s32[3,256]{1,0:T(4,128)S(1)}, s32[3,256]{1,0:T(4,128)S(1)}, u32[]{:S(2)}, u32[]{:S(2)}) collective-permute-start(s32[3,256]{1,0:T(4,128)S(1)} %copy-done.43), channel_id=1, source_target_pairs={{0,1},{1,0},{2,3},{3,2},{4,5},{5,4},{6,7},{7,6},{8,9},{9,8},{10,11... | collective-permute-start | bytes 9224 | tf_op jit(solution)/shard_map/ppermute | solution.py:23
  20.3 52.4 %collective-permute-start.5 = (bf16[3,256,1024]{2,1,0:T(8,128)(2,1)}, bf16[3,256,1024]{2,1,0:T(8,128)(2,1)}, u32[]{:S(2)}, u32[]{:S(2)}) collective-permute-start(bf16[3,256,1024]{2,1,0:T(8,128)(2,1)} %add_convert_fusion.3), channel_id=1, source_target_pairs={{0,1},{1,0},{2,3},{3,2},{4,5},{5,4},{6,7},{7,6},{8,9},{9,8},{10,11... | collective-permute-start | bytes 4718600 | tf_op jit(solution)/shard_map/ppermute | solution.py:23
  174.6 42.3 %collective-permute-start.11 = (bf16[768,1024]{1,0:T(8,128)(2,1)S(1)}, bf16[768,1024]{1,0:T(8,128)(2,1)}, u32[]{:S(2)}, u32[]{:S(2)}) collective-permute-start(bf16[768,1024]{1,0:T(8,128)(2,1)S(1)} %bitcast.232), channel_id=1, source_target_pairs={{0,1},{1,0},{2,3},{3,2},{4,5},{5,4},{6,7},{7,6},{8,9},{9,8},{10,11... | collective-permute-start | bytes 4718600 | tf_op jit(solution)/shard_map/ppermute | solution.py:23
  247.8 46.7 %collective-permute-start.12 = (bf16[768,1024]{1,0:T(8,128)(2,1)}, bf16[768,1024]{1,0:T(8,128)(2,1)}, u32[]{:S(2)}, u32[]{:S(2)}) collective-permute-start(bf16[768,1024]{1,0:T(8,128)(2,1)} %slice.221), channel_id=1, source_target_pairs={{0,1},{1,0},{2,3},{3,2},{4,5},{5,4},{6,7},{7,6},{8,9},{9,8},{10,11... | collective-permute-start | bytes 4718600 | tf_op jit(solution)/shard_map/ppermute | solution.py:23
  261.1 37.9 %collective-permute-start.10 = (bf16[768,1024]{1,0:T(8,128)(2,1)}, bf16[768,1024]{1,0:T(8,128)(2,1)}, u32[]{:S(2)}, u32[]{:S(2)}) collective-permute-start(bf16[768,1024]{1,0:T(8,128)(2,1)} %slice.222), channel_id=1, source_target_pairs={{0,1},{1,0},{2,3},{3,2},{4,5},{5,4},{6,7},{7,6},{8,9},{9,8},{10,11... | collective-permute-start | bytes 4718600 | tf_op jit(solution)/shard_map/ppermute | solution.py:23
  292.8 187.5 %collective-permute-start.30 = (bf16[1024,1024]{1,0:T(8,128)(2,1)}, bf16[1024,1024]{1,0:T(8,128)(2,1)}, u32[]{:S(2)}, u32[]{:S(2)}) collective-permute-start(bf16[1024,1024]{1,0:T(8,128)(2,1)} %bitcast.217), channel_id=1, source_target_pairs={{0,2},{2,0},{1,3},{3,1},{4,6},{6,4},{5,7},{7,5},{8,10},{10,8},{9,1... | collective-permute-start | bytes 6291464 | tf_op jit(solution)/shard_map/ppermute | solution.py:23
  308.6 49.4 %collective-permute-start.14 = (bf16[2,3,256,256]{3,2,1,0:T(8,128)(2,1)}, bf16[2,3,256,256]{3,2,1,0:T(8,128)(2,1)}, u32[]{:S(2)}, u32[]{:S(2)}) collective-permute-start(bf16[2,3,256,256]{3,2,1,0:T(8,128)(2,1)} %pad_maximum_fusion.13), channel_id=1, source_target_pairs={{0,2},{2,0},{1,3},{3,1},{4,6},{6,4},{5,7},{7,5},{8,10},{10,8},{9,1... | collective-permute-start | bytes 2359304 | tf_op jit(solution)/shard_map/ppermute | solution.py:23
  330.1 30.0 %collective-permute-start.25 = (bf16[1024,512]{1,0:T(8,128)(2,1)S(1)}, bf16[1024,512]{1,0:T(8,128)(2,1)S(1)}, u32[]{:S(2)}, u32[]{:S(2)}) collective-permute-start(bf16[1024,512]{1,0:T(8,128)(2,1)S(1)} %dynamic-slice_bitcast_fusion.1), channel_id=1, source_target_pairs={{0,1},{1,0},{2,3},{3,2},{4,5},{5,4},{6,7},{7,6},{8,9},{9,8},{10,11... | collective-permute-start | bytes 3145736 | tf_op jit(solution)/shard_map/ppermute | solution.py:23
  341.4 29.4 %collective-permute-start.13 = (bf16[3,256,256]{2,1,0:T(8,128)(2,1)}, bf16[3,256,256]{2,1,0:T(8,128)(2,1)}, u32[]{:S(2)}, u32[]{:S(2)}) collective-permute-start(bf16[3,256,256]{2,1,0:T(8,128)(2,1)} %bitcast.38), channel_id=1, source_target_pairs={{0,1},{1,0},{2,3},{3,2},{4,5},{5,4},{6,7},{7,6},{8,9},{9,8},{10,11... | collective-permute-start | bytes 1179656 | tf_op jit(solution)/shard_map/ppermute | solution.py:23
  369.1 78.1 %collective-permute-start.26 = (bf16[1024,256]{1,0:T(8,128)(2,1)}, bf16[1024,256]{1,0:T(8,128)(2,1)}, u32[]{:S(2)}, u32[]{:S(2)}) collective-permute-start(bf16[1024,256]{1,0:T(8,128)(2,1)} %bitcast.218), channel_id=1, source_target_pairs={{0,2},{2,0},{1,3},{3,1},{4,6},{6,4},{5,7},{7,5},{8,10},{10,8},{9,1... | collective-permute-start | bytes 1572872 | tf_op jit(solution)/shard_map/ppermute | solution.py:23
  447.2 30.5 %collective-permute-start.22 = (bf16[4,128,768]{1,2,0:T(8,128)(2,1)}, bf16[4,128,768]{1,2,0:T(8,128)(2,1)}, u32[]{:S(2)}, u32[]{:S(2)}) collective-permute-start(bf16[4,128,768]{1,2,0:T(8,128)(2,1)} %bitcast.271), channel_id=1, source_target_pairs={{0,4},{4,0},{1,5},{5,1},{2,6},{6,2},{3,7},{7,3},{8,12},{12,8},{9,1... | collective-permute-start | bytes 2359304 | tf_op jit(solution)/shard_map/ppermute | solution.py:23
  460.3 58.2 %collective-permute-start.34 = (bf16[4,256,1024]{1,2,0:T(8,128)(2,1)}, bf16[4,256,1024]{1,2,0:T(8,128)(2,1)}, u32[]{:S(2)}, u32[]{:S(2)}) collective-permute-start(bf16[4,256,1024]{1,2,0:T(8,128)(2,1)} %bitcast.251), channel_id=1, source_target_pairs={{0,4},{4,0},{1,5},{5,1},{2,6},{6,2},{3,7},{7,3},{8,12},{12,8},{9,1... | collective-permute-start | bytes 6291464 | tf_op jit(solution)/shard_map/ppermute | solution.py:23
  475.3 120.6 %reduce-scatter.5.cloned.1.call-start = ((), (), s32[]{:S(2)}) async-start(), calls=%async_computation.4 | async-start | bytes 983040 | tf_op jit(solution)/shard_map/reduce_scatter | solution.py:428
  480.2 117.2 %reduce-scatter.9.cloned.1.call-start = ((), (), s32[]{:S(2)}) async-start(), calls=%async_computation.6 | async-start | bytes 1310720 | tf_op jit(solution)/shard_map/reduce_scatter | solution.py:428
  488.0 52.2 %collective-permute-start.31 = (bf16[4,128,1024]{1,2,0:T(8,128)(2,1)}, bf16[4,128,1024]{1,2,0:T(8,128)(2,1)}, u32[]{:S(2)}, u32[]{:S(2)}) collective-permute-start(bf16[4,128,1024]{1,2,0:T(8,128)(2,1)} %bitcast.270), channel_id=1, source_target_pairs={{0,4},{4,0},{1,5},{5,1},{2,6},{6,2},{3,7},{7,3},{8,12},{12,8},{9,1... | collective-permute-start | bytes 3145736 | tf_op jit(solution)/shard_map/ppermute | solution.py:23
  542.7 69.9 %reduce-scatter.11.cloned.1.call-start = ((), (), s32[]{:S(2)}) async-start(), calls=%async_computation.7 | async-start | bytes 1310720 | tf_op jit(solution)/shard_map/reduce_scatter | solution.py:428
  554.3 29.4 %collective-permute-start.17 = (bf16[768,1024]{1,0:T(8,128)(2,1)}, bf16[768,1024]{1,0:T(8,128)(2,1)}, u32[]{:S(2)}, u32[]{:S(2)}) collective-permute-start(bf16[768,1024]{1,0:T(8,128)(2,1)} %get-tuple-element.148), channel_id=1, source_target_pairs={{0,1},{1,0},{2,3},{3,2},{4,5},{5,4},{6,7},{7,6},{8,9},{9,8},{10,11... | collective-permute-start | bytes 4718600 | tf_op jit(solution)/shard_map/ppermute | solution.py:23
  581.3 128.8 %all-reduce.3.cloned.1.call-start = ((), (), s32[]{:S(2)}) async-start(), calls=%async_computation.8 | async-start | bytes 1105920
  583.1 34.9 %collective-permute-start.16 = (bf16[768,1024]{1,0:T(8,128)(2,1)}, bf16[768,1024]{1,0:T(8,128)(2,1)}, u32[]{:S(2)}, u32[]{:S(2)}) collective-permute-start(bf16[768,1024]{1,0:T(8,128)(2,1)} %get-tuple-element.147), channel_id=1, source_target_pairs={{0,1},{1,0},{2,3},{3,2},{4,5},{5,4},{6,7},{7,6},{8,9},{9,8},{10,11... | collective-permute-start | bytes 4718600 | tf_op jit(solution)/shard_map/ppermute | solution.py:23
  587.4 37.6 %collective-permute-start.18 = (bf16[768,1024]{1,0:T(8,128)(2,1)}, bf16[768,1024]{1,0:T(8,128)(2,1)}, u32[]{:S(2)}, u32[]{:S(2)}) collective-permute-start(bf16[768,1024]{1,0:T(8,128)(2,1)} %add_convert_fusion), channel_id=1, source_target_pairs={{0,2},{2,0},{1,3},{3,1},{4,6},{6,4},{5,7},{7,5},{8,10},{10,8},{9,1... | collective-permute-start | bytes 4718600 | tf_op jit(solution)/shard_map/ppermute | solution.py:23
  597.4 39.2 %collective-permute-start.32 = (bf16[128,1024]{0,1:T(8,128)(2,1)}, bf16[128,1024]{0,1:T(8,128)(2,1)}, u32[]{:S(2)}, u32[]{:S(2)}) collective-permute-start(bf16[128,1024]{0,1:T(8,128)(2,1)} %bitcast.275), channel_id=1, source_target_pairs={{0,2},{2,0},{1,3},{3,1},{4,6},{6,4},{5,7},{7,5},{8,10},{10,8},{9,1... | collective-permute-start | bytes 786440 | tf_op jit(solution)/shard_map/ppermute | solution.py:23
  (95 other events, 1181.9 us)
Sparse Core Ops, SparseCore 0:
  475.5 23.6 reduce-scatter.6
  501.5 21.5 reduce-scatter.4
  542.9 31.1 reduce-scatter.8
  581.4 31.1 reduce-scatter.10
  666.3 43.7 all-reduce.2

commit v2 on v1

v2 whole, which is shorter than its diff:
```python
import functools
import math

import jax
import jax.numpy as jnp
from jax import lax
from jax.experimental import pallas as pl
from jax.experimental.pallas import tpu as pltpu
from jax.sharding import Mesh, PartitionSpec as P

HEADS = 16
HEAD_DIM = 64
TEMB = 256
SEGS = 8
EPSILON = 1e-05
F32 = jnp.float32
BF16 = jnp.bfloat16
NEG = -1e30
LOG2E = math.log2(math.e)
GELU_A = math.sqrt(2.0 / math.pi)
GELU_B = GELU_A * 0.044715
BLOCK = 256
VMEM = 60 * 1024 * 1024


def swap(value, axis):
    return lax.ppermute(value, axis, [(0, 1), (1, 0)])


def time_features(doc_times, column, half_size):
    frequency = jnp.exp(-math.log(10000.0) * (column % half_size).astype(F32) / half_size)
    angles = doc_times.astype(F32)[..., None] * frequency
    return jnp.where(column < half_size, jnp.sin(angles), jnp.cos(angles)).astype(BF16)


def rotary_tables(positions, head_size):
    half_size = head_size // 2
    frequency = jnp.exp(-math.log(10000.0) * 2.0 * jnp.arange(half_size, dtype=F32) / head_size)
    angles = positions.astype(F32)[..., None] * frequency
    cos_tab, sin_tab = jnp.cos(angles), jnp.sin(angles)
    return (
        jnp.concatenate([cos_tab] * 4, axis=-1),
        jnp.concatenate([-sin_tab, sin_tab, -sin_tab, sin_tab], axis=-1),
    )


def dot(left_op, right_op, left_dim=1, right_dim=0):
    return lax.dot_general(
        left_op, right_op, (((left_dim,), (right_dim,)), ((), ())), preferred_element_type=F32
    )


def turn(values, cos_tab, sin_tab):
    slabs = []
    lane = lax.broadcasted_iota(jnp.int32, (values.shape[0], 128), 1)
    first = lane % HEAD_DIM < HEAD_DIM // 2
    for start in range(0, values.shape[1], 128):
        slab = values[:, start : start + 128]
        partner = jnp.where(
            first, pltpu.roll(slab, 128 - HEAD_DIM // 2, 1), pltpu.roll(slab, HEAD_DIM // 2, 1)
        )
        slabs.append(slab * cos_tab + partner * sin_tab)
    return jnp.concatenate(slabs, axis=1)


def split_low(values):
    high = values.astype(BF16)
    return jnp.concatenate([high, (values - high.astype(F32)).astype(BF16)], axis=0)


def centre(values):
    scale = 1.0 / values.shape[-1]
    centred = values - jnp.sum(values, axis=-1, keepdims=True) * scale
    spread = jnp.sum(centred * centred, axis=-1, keepdims=True) * scale
    inverse = lax.rsqrt(spread + EPSILON)
    return centred * inverse, inverse


def norm_back(grad, gain, hat, inverse):
    scale = 1.0 / grad.shape[-1]
    scaled = grad * gain
    mean = jnp.sum(scaled, axis=-1, keepdims=True) * scale
    along = jnp.sum(scaled * hat, axis=-1, keepdims=True) * scale
    return inverse * (scaled - mean - hat * along)


def call(body, name, prefetch, grid, ins, outs, scratch=(), deps=(), flops=0, moved=0, trans=0):
    count, held = len(prefetch) + len(ins), len(deps)

    def kernel(*refs):
        body(*refs[:count], *refs[count + held :])

    return pl.pallas_call(
        kernel,
        grid_spec=pltpu.PrefetchScalarGridSpec(
            num_scalar_prefetch=len(prefetch),
            grid=grid,
            in_specs=[spec for _, spec in ins] + [pl.BlockSpec(memory_space=pl.ANY)] * held,
            out_specs=[spec for _, _, spec in outs],
            scratch_shapes=list(scratch),
        ),
        out_shape=[jax.ShapeDtypeStruct(shape, kind) for shape, kind, _ in outs],
        compiler_params=pltpu.CompilerParams(vmem_limit_bytes=VMEM),
        cost_estimate=pl.CostEstimate(flops=flops, bytes_accessed=moved, transcendentals=trans),
        name=name,
    )(*prefetch, *[array for array, _ in ins], *deps)


def fixed(shape):
    return pl.BlockSpec(shape, lambda *_: (0,) * len(shape))


def along(shape, axis=0):
    return pl.BlockSpec(shape, lambda g, *_: tuple(g if n == axis else 0 for n in range(len(shape))))


def norm1_body(x_ref, seg_ref, shift_ref, gain_ref, bias_ref, stream_ref, low_ref):
    slots = lax.broadcasted_iota(jnp.int32, (SEGS, seg_ref.shape[-1]), 0) == seg_ref[0]
    onehot = slots.astype(F32).astype(BF16)
    added = dot(jnp.concatenate([onehot, onehot], axis=0), split_low(shift_ref[0]), 0, 0)
    stream = x_ref[0].astype(F32) + added
    hat, _ = centre(stream)
    stream_ref[0] = stream
    low_ref[0] = (hat * gain_ref[...] + bias_ref[...]).astype(BF16)


def norm1(x, seg, shift, gain, bias):
    rows, shard, model = x.shape
    block = along((1, shard, model))
    return call(
        norm1_body, "norm1", (), (rows,),
        [(x, block), (seg, along((1, 1, shard))), (shift, along((1, SEGS, model))), (gain, fixed((1, model))), (bias, fixed((1, model)))],
        [(x.shape, F32, block), (x.shape, BF16, block)],
        moved=8 * x.size,
    )


def qkv_body(me_ref, a_ref, b_ref, wq_ref, wk_ref, wv_ref, bq_ref, bk_ref, bv_ref, cos_ref, sin_ref, *refs):
    q_ref, k_ref, v_ref, w_ref = refs[-4:]
    rows, shard, model = a_ref.shape
    width = wq_ref.shape[1]

    def run(x_ref):
        x = x_ref[...].reshape(rows * shard, model)
        cos_tab = jnp.concatenate([cos_ref[0]] * rows, axis=0)
        sin_tab = jnp.concatenate([sin_ref[0]] * rows, axis=0)
        q = turn(dot(x, wq_ref[...]) + bq_ref[...].astype(F32), cos_tab, sin_tab)
        q_ref[0] = (q * (LOG2E * HEAD_DIM**-0.5)).astype(BF16).reshape(rows, shard, width)
        k = turn(dot(x, wk_ref[...]) + bk_ref[...].astype(F32), cos_tab, sin_tab)
        k_ref[0] = k.astype(BF16).reshape(rows, shard, width)
        v = dot(x, wv_ref[...]) + bv_ref[...].astype(F32)
        v_ref[0] = v.astype(BF16).reshape(rows, shard, width)

    @pl.when(pl.program_id(0) == 0)
    def _():
        w_ref[:, 0:width] = wq_ref[...]
        w_ref[:, width : 2 * width] = wk_ref[...]
        w_ref[:, 2 * width :] = wv_ref[...]
        run(a_ref)

    @pl.when(pl.program_id(0) == 1)
    def _():
        run(b_ref)


def project_qkv(me, first, second, weight, bias, cos_tab, sin_tab, offset, parts, held=(), deps=()):
    rows, shard, model = first.shape
    width = model // parts
    out = jax.ShapeDtypeStruct((parts, rows, shard, width), BF16)
    place = pl.BlockSpec((1, rows, shard, width), lambda p, m: (p + offset, 0, 0, 0))
    table = pl.BlockSpec((1, shard, 128), lambda p, m: (p + offset, 0, 0))

    def column(part, height):
        return pl.BlockSpec((height, width), lambda p, m: (0, part * parts + m[0]))

    extra = list(held) + list(deps)
    return pl.pallas_call(
        qkv_body,
        grid_spec=pltpu.PrefetchScalarGridSpec(
            num_scalar_prefetch=1,
            grid=(2,),
            in_specs=[fixed(first.shape), fixed(first.shape)]
            + [column(n, model) for n in range(3)]
            + [column(n, 1) for n in range(3)]
            + [table, table]
            + [pl.BlockSpec(memory_space=pl.ANY)] * len(extra),
            out_specs=[place] * 3 + [fixed((model, 3 * width))],
        ),
        out_shape=[out] * 3 + [jax.ShapeDtypeStruct((model, 3 * width), BF16)],
        input_output_aliases={11 + n: n for n in range(len(held))},
        compiler_params=pltpu.CompilerParams(vmem_limit_bytes=VMEM),
        cost_estimate=pl.CostEstimate(
            flops=12 * rows * shard * model * width, bytes_accessed=12 * rows * shard * model, transcendentals=0
        ),
        name="qkv",
    )(me, first, second, weight, weight, weight, bias, bias, bias, cos_tab, sin_tab, *extra)


PLACED = (2, 0, 3, 1)


def seg_columns(segq_all, segk):
    pieces, shard, _ = segk.shape
    for j in range(pieces):
        row = jnp.broadcast_to(segq_all[j:j+1].astype(F32), (128, shard))
        segk[j] = row.T

def attend_body(cnt_ref, idx_ref, q_ref, k_ref, v_ref, seg_ref, o_ref, lse_ref, vt, segk, qmt, acc):
    row = pl.program_id(0)
    pieces, _, shard, width = k_ref.shape
    heads = width // HEAD_DIM

    @pl.when(row == 0)
    def _():
        qmt[...] = jnp.zeros_like(qmt)

    for j in range(pieces):
        vt[j] = v_ref[j, 0].T
    seg_columns(seg_ref[0], segk)

    @pl.loop(0, pieces)
    def _(piece):
        attend_piece(row, piece, cnt_ref, idx_ref, q_ref, k_ref, v_ref, seg_ref, o_ref, lse_ref, vt, segk, qmt, acc)

def attend_piece(row, piece, cnt_ref, idx_ref, q_ref, k_ref, v_ref, seg_ref, o_ref, lse_ref, vt, segk, qmt, acc):
    pieces, _, shard, width = k_ref.shape
    heads = width // HEAD_DIM
    qt = q_ref[piece, 0].T
    for h in range(heads):
        at = slice(h * HEAD_DIM, (h + 1) * HEAD_DIM)
        qmt[at, h * shard : (h + 1) * shard] = qt[at]
    at_q = row * pieces + piece
    seg_q = seg_ref[0, pl.ds(piece, 1)].astype(F32)

    def run(count):
        @pl.when(cnt_ref[at_q] == count)
        def _():
            qm = qmt[...]
            places = [idx_ref[at_q * pieces + t] for t in range(count)]
            top, tot, out = [None] * heads, [None] * heads, [None] * heads
            later = dot(k_ref[places[0], 0], qm)
            for t in range(count):
                s = later
                if t + 1 < count:
                    later = dot(k_ref[places[t + 1], 0], qm)
                col = segk[places[t]]
                same = jnp.concatenate([col] * (shard // 128), axis=1) == seg_q
                for h in range(heads):
                    at = slice(h * HEAD_DIM, (h + 1) * HEAD_DIM)
                    sh = jnp.where(same, s[:, h * shard : (h + 1) * shard], NEG)
                    best = jnp.max(sh, axis=0, keepdims=True)
                    if t:
                        best = jnp.maximum(top[h], best)
                        fade = jnp.exp2(top[h] - best)
                    p = jnp.exp2(sh - best)
                    total = jnp.sum(p, axis=0, keepdims=True)
                    part = dot(vt[places[t], at], p.astype(BF16))
                    if t:
                        total = tot[h] * fade + total
                        part = out[h] * fade + part
                    top[h], tot[h], out[h] = best, total, part
            for h in range(heads):
                acc[h * HEAD_DIM : (h + 1) * HEAD_DIM] = out[h] / tot[h]
                lse_ref[0, piece, h : h + 1] = top[h] + jnp.log2(tot[h])

    for count in range(1, pieces + 1):
        run(count)
    o_ref[piece, 0] = acc[...].T.astype(BF16)

def row_blocks(pieces, shard, width, axis=1):
    return along((pieces, 1, shard, width), axis)


def attend(cnt, idx, q, k, v, seg):
    pieces, rows, shard, width = q.shape
    heads = width // HEAD_DIM
    whole = row_blocks(pieces, shard, width)
    pairs = rows * (pieces * shard) ** 2
    return call(
        attend_body, "attend", (cnt, idx), (rows,),
        [(q, whole), (k, whole), (v, whole), (seg, along((1, pieces, shard)))],
        [(q.shape, BF16, whole), ((rows, pieces, 8, shard), F32, along((1, pieces, 8, shard)))],
        [
            pltpu.VMEM((pieces, width, shard), BF16),
            pltpu.VMEM((pieces, shard, 128), F32),
            pltpu.VMEM((width, heads * shard), BF16),
            pltpu.VMEM((width, shard), F32),
        ],
        flops=16 * pairs * width, moved=8 * q.size, trans=pairs * heads,
    )


def attend_back_body(cnt_ref, idx_ref, q_ref, k_ref, v_ref, o_ref, do_ref, lse_ref, seg_ref, cos_ref, sin_ref,
    g_ref, kt, segk, dk, dv, dqt, qmt, gmt, qst, gst):
    row = pl.program_id(0)
    pieces, _, shard, width = k_ref.shape

    @pl.when(row == 0)
    def _():
        qmt[...] = jnp.zeros_like(qmt)
        gmt[...] = jnp.zeros_like(gmt)

    for j in range(pieces):
        kt[j] = k_ref[j, 0].T
    seg_columns(seg_ref[0], segk)
    dk[...] = jnp.zeros_like(dk)
    dv[...] = jnp.zeros_like(dv)

    @pl.loop(0, pieces)
    def _(piece):
        back_piece(row, piece, cnt_ref, idx_ref, q_ref, k_ref, v_ref, o_ref, do_ref, lse_ref, seg_ref, cos_ref, sin_ref,
            g_ref, kt, segk, dk, dv, dqt, qmt, gmt, qst, gst)

    for j in range(pieces):
        at = PLACED[j]
        g_ref[at, 0, :, width : 2 * width] = turn(dk[j] * (1 / LOG2E), cos_ref[j], -sin_ref[j]).astype(BF16)
        g_ref[at, 0, :, 2 * width :] = dv[j].astype(BF16)

def back_piece(row, piece, cnt_ref, idx_ref, q_ref, k_ref, v_ref, o_ref, do_ref, lse_ref, seg_ref, cos_ref, sin_ref,
            g_ref, kt, segk, dk, dv, dqt, qmt, gmt, qst, gst):
    pieces, _, shard, width = k_ref.shape
    heads = width // HEAD_DIM
    q, do = q_ref[piece, 0], do_ref[piece, 0]
    qt, gt = q.T, do.T
    lane = lax.broadcasted_iota(jnp.int32, q.shape, 1) // HEAD_DIM
    for h in range(heads):
        at = slice(h * HEAD_DIM, (h + 1) * HEAD_DIM)
        qa = slice(h * shard, (h + 1) * shard)
        qmt[at, qa] = qt[at]
        gmt[at, qa] = gt[at]
        qst[qa] = jnp.where(lane == h, q, jnp.zeros_like(q))
        gst[qa] = jnp.where(lane == h, do, jnp.zeros_like(do))
    prod = do.astype(F32) * o_ref[piece, 0].astype(F32)
    prod_hi = prod.astype(BF16)
    prod_lo = (prod - prod_hi.astype(F32)).astype(BF16)
    pick = (lax.broadcasted_iota(jnp.int32, (8, width), 1) // HEAD_DIM == lax.broadcasted_iota(jnp.int32, (8, width), 0)).astype(BF16)
    delta = dot(pick, prod_hi, 1, 1) + dot(pick, prod_lo, 1, 1)
    lse = lse_ref[0, piece]
    at_q = row * pieces + piece
    seg_q = seg_ref[0, pl.ds(piece, 1)].astype(F32)

    def run(count):
        @pl.when(cnt_ref[at_q] == count)
        def _():
            places = [idx_ref[at_q * pieces + t] for t in range(count)]
            qm, gm = qmt[...], gmt[...]
            later = dot(k_ref[places[0], 0], qm), dot(v_ref[places[0], 0], gm)
            out = [None] * heads
            for t in range(count):
                s, dp = later
                j = places[t]
                if t + 1 < count:
                    later = dot(k_ref[places[t + 1], 0], qm), dot(v_ref[places[t + 1], 0], gm)
                col = segk[j]
                same = jnp.concatenate([col] * (shard // 128), axis=1) == seg_q
                ps, dss = [], []
                for h in range(heads):
                    at = slice(h * HEAD_DIM, (h + 1) * HEAD_DIM)
                    qa = slice(h * shard, (h + 1) * shard)
                    p = jnp.exp2(jnp.where(same, s[:, qa] - lse[h : h + 1], NEG))
                    ds = (p * (dp[:, qa] - delta[h : h + 1])).astype(BF16)
                    ps.append(p.astype(BF16))
                    dss.append(ds)
                    part = dot(kt[j, at], ds)
                    out[h] = part if t == 0 else out[h] + part
                dv[j] += dot(jnp.concatenate(ps, axis=1), gst[...])
                dk[j] += dot(jnp.concatenate(dss, axis=1), qst[...])
            for h in range(heads):
                dqt[h * HEAD_DIM : (h + 1) * HEAD_DIM] = out[h]

    for count in range(1, pieces + 1):
        run(count)
    place = jnp.where(piece % 2 == 1, piece // 2, 2 + piece // 2)
    g_ref[place, 0, :, 0:width] = turn(dqt[...].T * HEAD_DIM**-0.5, cos_ref[piece], -sin_ref[piece]).astype(BF16)

def attend_back(cnt, idx, q, k, v, o, do, lse, seg, cos_tab, sin_tab, deps=()):
    pieces, rows, shard, width = q.shape
    heads = width // HEAD_DIM
    whole, table = row_blocks(pieces, shard, width), fixed((pieces, shard, 128))
    pairs = rows * (pieces * shard) ** 2
    return call(
        attend_back_body, "attend_back", (cnt, idx), (rows,),
        [(q, whole), (k, whole), (v, whole), (o, whole), (do, whole), (lse, along((1, pieces, 8, shard)))]
        + [(seg, along((1, pieces, shard))), (cos_tab, table), (sin_tab, table)],
        [((pieces, rows, shard, 3 * width), BF16, row_blocks(pieces, shard, 3 * width))],
        [
            pltpu.VMEM((pieces, width, shard), BF16),
            pltpu.VMEM((pieces, shard, 128), F32),
            pltpu.VMEM((pieces, shard, width), F32),
            pltpu.VMEM((pieces, shard, width), F32),
            pltpu.VMEM((width, shard), F32),
            pltpu.VMEM((width, heads * shard), BF16),
            pltpu.VMEM((width, heads * shard), BF16),
            pltpu.VMEM((heads * shard, width), BF16),
            pltpu.VMEM((heads * shard, width), BF16),
        ],
        deps=deps, flops=40 * pairs * width, moved=16 * q.size, trans=pairs * heads,
    )[0]


def middle_body(order_ref, a0, a1, a2, a3, w0, w1, w2, w3, stream_ref, bias_ref, gain_ref, shift_ref, mid_ref, low_ref):
    total = dot(a0[0], w0[...]) + dot(a1[0], w1[...])
    total = total + (dot(a2[0], w2[...]) + dot(a3[0], w3[...]))
    mid = stream_ref[0] + (total + bias_ref[...])
    hat, _ = centre(mid)
    mid_ref[0] = mid
    low_ref[0] = (hat * gain_ref[...] + shift_ref[...]).astype(BF16)


def out_blocks(weight, parts):
    width = weight.shape[0] // parts

    def block(i):
        return pl.BlockSpec((width, weight.shape[1]), lambda g, o: (o[i], 0))

    return [(weight, block(i)) for i in range(parts)]


def middle_norm(order, attended, weight, stream, bias, gain, shift):
    rows, shard, model = stream.shape
    parts = len(attended)
    width = model // parts
    block, line = along((1, shard, model)), fixed((1, model))
    return call(
        middle_body, "middle", (order,), (rows,),
        [(a, along((1, shard, width))) for a in attended] + out_blocks(weight, parts)
        + [(stream, block), (bias, line), (gain, line), (shift, line)],
        [(stream.shape, F32, block), (stream.shape, BF16, block)],
        flops=2 * rows * shard * model * model, moved=14 * stream.size,
    )


def cot_body(blk_ref, a_ref, b_ref, up_ref, down_ref, g_ref, up_out, down_out):
    tokens = a_ref.shape[0]
    down = down_ref[...]
    g_ref[0:tokens] = dot(a_ref[...], down, 1, 1).astype(BF16)
    g_ref[tokens:] = dot(b_ref[...], down, 1, 1).astype(BF16)
    up_out[...] = up_ref[...]
    down_out[...] = down


def cot_down(blk, own, other, up, down, picked, half):
    tokens, model = own.shape
    steps = half // BLOCK
    column = along((2 * tokens, BLOCK), 1)
    if picked:
        up_at, down_at = along((model, BLOCK), 1), along((BLOCK, model))
    else:
        up_at = pl.BlockSpec((model, BLOCK), lambda g, b: (0, b[g]))
        down_at = pl.BlockSpec((BLOCK, model), lambda g, b: (b[g], 0))
    return call(
        cot_body, "cot_down", (blk,), (steps,),
        [(own, fixed(own.shape)), (other, fixed(own.shape)), (up, up_at), (down, down_at)],
        [
            ((2 * tokens, half), BF16, column),
            ((model, half), BF16, along((model, BLOCK), 1)),
            ((half, model), BF16, along((BLOCK, model))),
        ],
        flops=4 * tokens * model * half, moved=2 * (2 * tokens * (model + half) + 4 * model * half),
    )


def hidden_body(a_ref, b_ref, g_ref, up_ref, bias_ref, act_ref, grad_ref, sum_ref):
    tokens = a_ref.shape[0]
    up, bias = up_ref[...], bias_ref[...]
    chunk = 256 if tokens % 256 == 0 else tokens
    places = [(ref, start, n * tokens + start) for n, ref in enumerate((a_ref, b_ref)) for start in range(0, tokens, chunk)]
    total = 0.0
    later = dot(a_ref[0:chunk], up)
    for n, (ref, start, at) in enumerate(places):
        v = later + bias
        if n + 1 < len(places):
            ref, start, _ = places[n + 1]
            later = dot(ref[start : start + chunk], up)
        square = v * v
        tanh = jnp.tanh(v * (GELU_A + GELU_B * square))
        gate = 0.5 + 0.5 * tanh
        act = v * gate
        slope = gate + act * ((1.0 - tanh) * (GELU_A + 3.0 * GELU_B * square))
        grad = (slope * g_ref[at : at + chunk].astype(F32)).astype(BF16)
        act_ref[at : at + chunk] = act.astype(BF16)
        grad_ref[at : at + chunk] = grad
        total = total + jnp.sum(grad.astype(F32), axis=0, keepdims=True)
    sum_ref[...] = total


def hidden_units(own, other, grads, up, bias):
    tokens, model = own.shape
    half = up.shape[1]
    column, line = along((2 * tokens, BLOCK), 1), along((1, BLOCK), 1)
    return call(
        hidden_body, "hidden", (), (half // BLOCK,),
        [(own, fixed(own.shape)), (other, fixed(own.shape)), (grads, column), (up, along((model, BLOCK), 1)), (bias, line)],
        [(grads.shape, BF16, column), (grads.shape, BF16, column), ((1, half), F32, line)],
        flops=4 * tokens * model * half, moved=2 * (2 * tokens * (model + 3 * half) + model * half), trans=2 * tokens * half,
    )


def middle_back_body(
    order_ref, part_ref, sent_ref, mid_ref, cot_ref, gain_ref, w0, w1, w2, w3, grad_ref, low_ref, att_ref, sums_ref,
):
    grad = part_ref[0].astype(F32) + sent_ref[0].astype(F32)
    hat, inverse = centre(mid_ref[0])
    cot = cot_ref[0].astype(F32)
    total = cot + norm_back(grad, gain_ref[...], hat, inverse)
    low = total.astype(BF16)
    grad_ref[0] = total
    low_ref[0] = low
    for n, w in enumerate((w0, w1, w2, w3)):
        att_ref[n, 0] = dot(low, w[...], 1, 1).astype(BF16)

    @pl.when(pl.program_id(0) == 0)
    def _():
        sums_ref[...] = jnp.zeros_like(sums_ref)

    sums_ref[0:1] += jnp.sum(grad * hat, axis=0, keepdims=True)
    sums_ref[1:2] += jnp.sum(grad, axis=0, keepdims=True)
    sums_ref[2:3] += jnp.sum(low.astype(F32), axis=0, keepdims=True)
    sums_ref[3:4] += jnp.sum(cot, axis=0, keepdims=True)


def middle_back(order, part, sent, mid, cot, gain, weight, parts, deps=()):
    rows, shard, model = mid.shape
    width = model // parts
    block = along((1, shard, model))
    return call(
        middle_back_body, "middle_back", (order,), (rows,),
        [(part, block), (sent, block), (mid, block), (cot, block), (gain, fixed((1, model)))] + out_blocks(weight, parts),
        [
            (mid.shape, F32, block),
            (mid.shape, BF16, block),
            ((parts, rows, shard, width), BF16, along((parts, 1, shard, width), 1)),
            ((8, model), F32, fixed((8, model))),
        ],
        deps=deps, flops=2 * rows * shard * model * model, moved=18 * mid.size,
    )


def norm1_back_body(part_ref, near_ref, far_ref, stream_ref, mid_ref, gain_ref, seg_ref, in_ref, shift_ref, sums_ref):
    grad = part_ref[0].astype(F32) + near_ref[0].astype(F32) + far_ref[0].astype(F32)
    hat, inverse = centre(stream_ref[0])
    total = mid_ref[0] + norm_back(grad, gain_ref[...], hat, inverse)
    in_ref[0] = total.astype(BF16)
    slots = lax.broadcasted_iota(jnp.int32, (SEGS, seg_ref.shape[-1]), 0) == seg_ref[0]
    onehot = slots.astype(F32).astype(BF16)
    shift_ref[0] = dot(jnp.concatenate([onehot, onehot], axis=1), split_low(total))

    @pl.when(pl.program_id(0) == 0)
    def _():
        sums_ref[...] = jnp.zeros_like(sums_ref)

    sums_ref[0:1] += jnp.sum(grad * hat, axis=0, keepdims=True)
    sums_ref[1:2] += jnp.sum(grad, axis=0, keepdims=True)


def norm1_back(part, near, far, stream, mid, gain, seg):
    rows, shard, model = stream.shape
    block = along((1, shard, model))
    return call(
        norm1_back_body, "norm1_back", (), (rows,),
        [(part, block), (near, block), (far, block), (stream, block), (mid, block), (gain, fixed((1, model))), (seg, along((1, 1, shard)))],
        [
            (stream.shape, BF16, block),
            ((rows, SEGS, model), F32, along((1, SEGS, model))),
            ((8, model), F32, fixed((8, model))),
        ],
        moved=16 * stream.size,
    )


def exchange(parts):
    far = swap(parts[2:4], "y")
    return [parts[0], swap(parts[1], "c"), far[0], swap(far[1], "c")]


def cut(values, index, size, axis):
    return lax.dynamic_slice_in_dim(values, index * size, size, axis)


def add_low(kept, sent):
    return (kept.astype(F32) + sent.astype(F32)).astype(BF16)


def ordered(at, own, other, axis):
    return jnp.where(at == 0, jnp.concatenate([own, other], axis), jnp.concatenate([other, own], axis))


def local(
    inputs, segment_ids, doc_times, time_weight, time_bias, norm1_gain, norm1_bias, qkv_weight, qkv_bias,
    out_weight, out_bias, norm2_gain, norm2_bias, up_weight, up_bias, down_weight, down_bias, cotangent,
    *, dp,
):
    rows, shard, model = inputs.shape
    parts = 4
    tokens = rows * shard
    hidden_width = up_weight.shape[1]
    width = model // parts
    depth = dp // 2
    half = hidden_width // 2
    piece = half // dp
    z_at, x_at, y_at, c_at = (lax.axis_index(name) for name in ("z", "x", "y", "c"))
    me = 2 * y_at + c_at
    order = [me ^ i for i in range(parts)]
    order_list = jnp.stack(order).astype(jnp.int32)
    me_list = order_list[:1]

    def line(vector):
        return vector.astype(F32)[None]

    seg = segment_ids[:, None, :]
    features = time_features(doc_times.reshape(rows * SEGS), jnp.arange(TEMB), TEMB // 2)
    time_shift = dot(features, time_weight).reshape(rows, SEGS, model) + time_bias.astype(F32)
    stream, own1 = norm1(inputs, seg, time_shift, line(norm1_gain), line(norm1_bias))
    one1 = swap(own1, "c")
    two1 = swap(own1, "y")

    seg_two = swap(segment_ids, "y")
    segs = jnp.stack([segment_ids, swap(segment_ids, "c"), seg_two, swap(seg_two, "c")], axis=1)
    low_id, high_id = segs.min(axis=2), segs.max(axis=2)
    act = (low_id[:, :, None] <= high_id[:, None, :]) & (low_id[:, None, :] <= high_id[:, :, None])
    places = jnp.arange(parts, dtype=jnp.int32)
    rank = jnp.cumsum(act.astype(jnp.int32), axis=2) - 1
    chosen = act[..., None] & (rank[..., None] == places)
    idx = jnp.sum(jnp.where(chosen, places[:, None], 0), axis=2).astype(jnp.int32).reshape(-1)
    cnt = jnp.sum(act.astype(jnp.int32), axis=2).reshape(-1)
    positions = jnp.stack([o * shard + jnp.arange(shard, dtype=jnp.int32) for o in order])
    cos_tab, sin_tab = rotary_tables(positions, HEAD_DIM)
    all_times = lax.all_gather(doc_times.reshape(rows * SEGS), ("z", "x"))

    cot = cotangent.reshape(tokens, model)
    cot_other = swap(cot, "c")
    turned = jnp.stack([1 - x_at, x_at])
    if piece % BLOCK == 0:
        blk = ((jnp.arange(depth)[None, :] * 2 + turned[:, None]) * 2 + c_at) * (piece // BLOCK)
        blk = (blk[..., None] + jnp.arange(piece // BLOCK)).reshape(-1).astype(jnp.int32)
        up_from, down_from = up_weight, down_weight
    else:
        blk = jnp.zeros((half // BLOCK,), jnp.int32)
        up_from = up_weight.reshape(model, depth, 2, 2, piece)
        up_from = lax.dynamic_index_in_dim(up_from, c_at, 3, keepdims=False)
        up_from = jnp.where(x_at == 1, up_from, up_from[:, :, ::-1]).transpose(0, 2, 1, 3).reshape(model, half)
        down_from = down_weight.reshape(depth, 2, 2, piece, model)
        down_from = lax.dynamic_index_in_dim(down_from, c_at, 2, keepdims=False)
        down_from = jnp.where(x_at == 1, down_from, down_from[:, ::-1]).transpose(1, 0, 2, 3).reshape(half, model)
    grad_act, up_own, down_own = cot_down(blk, cot, cot_other, up_from, down_from, piece % BLOCK != 0, half)
    up_bias_own = lax.dynamic_index_in_dim(up_bias.reshape(depth, 2, 2, piece), c_at, 2, keepdims=False)
    up_bias_own = jnp.where(x_at == 1, up_bias_own, up_bias_own[:, ::-1]).transpose(1, 0, 2).reshape(half)

    bias_line = qkv_bias.reshape(1, 3 * model)
    *held, _ = project_qkv(me_list, own1, one1, qkv_weight, bias_line, cos_tab, sin_tab, 0, parts, (), (grad_act,))
    three1 = swap(two1, "c")
    q, k, v, qkv_own = project_qkv(me_list, two1, three1, qkv_weight, bias_line, cos_tab, sin_tab, 2, parts, held)
    o, lse = attend(cnt, idx, q, k, v, segs)
    attended = exchange(o)
    middle, normed2 = middle_norm(
        order_list, attended, out_weight, stream, line(out_bias), line(norm2_gain), line(norm2_bias)
    )

    normed2 = normed2.reshape(tokens, model)
    normed2_other = swap(normed2, "c")
    active, grad_hidden, up_b = hidden_units(normed2, normed2_other, grad_act, up_own, line(up_bias_own))
    part2_sent = swap(dot(grad_hidden[tokens:], up_own, 1, 1).astype(BF16), "c").reshape(rows, shard, model)
    part2 = dot(grad_hidden[:tokens], up_own, 1, 1).astype(BF16).reshape(rows, shard, model)
    grad_middle, grad_middle_low, grad_att, sums2 = middle_back(
        order_list, part2, part2_sent, middle, cotangent, line(norm2_gain), out_weight, parts
    )
    grad_o = jnp.stack(exchange(grad_att))

    cot_both = jnp.concatenate([cot, cot_other], axis=0)
    normed2_both = jnp.concatenate([normed2, normed2_other], axis=0)
    down_sent = swap(dot(active[:, : half // 2], cot_both, 0, 0).astype(BF16), "x")
    up_grad = dot(normed2_both, grad_hidden, 0, 0).astype(BF16)
    up_z = lax.psum_scatter(up_grad, "z", scatter_dimension=0, tiled=True)
    down_kept = dot(active[:, half // 2 :], cot_both, 0, 0).astype(BF16)
    feed_sent = swap(dot(active[tokens:], down_own).astype(BF16), "c")
    feed = dot(active[:tokens], down_own) + feed_sent.astype(F32) + line(down_bias)
    output = (middle + feed.reshape(rows, shard, model)).astype(BF16)
    attended_all = jnp.concatenate([a.reshape(tokens, width) for a in attended], axis=1)
    out_grad = dot(attended_all, grad_middle_low.reshape(tokens, model), 0, 0).astype(BF16)

    grad_qkv = attend_back(cnt, idx, q, k, v, o, grad_o, lse, segs, cos_tab, sin_tab, (down_kept, up_grad, down_sent))
    part1_out = dot(grad_qkv[:2].reshape(2 * tokens, 3 * width), qkv_own, 1, 1).astype(BF16)
    part1_out = part1_out.reshape(2, rows, shard, model)
    part1 = dot(grad_qkv[2:].reshape(2 * tokens, 3 * width), qkv_own, 1, 1).astype(BF16)
    part1 = part1.reshape(2, rows, shard, model)
    near = swap(part1_out[0], "c")
    there = add_low(part1[1], swap(part1_out[1], "c"))
    far = swap(there, "y")
    normed1_all = jnp.stack([one1, three1, own1, two1]).reshape(parts * tokens, model)
    grad_qkv = grad_qkv.reshape(parts * tokens, 3 * width)
    qkv_grad = dot(normed1_all, grad_qkv, 0, 0).astype(BF16)
    qkv_b = jnp.sum(grad_qkv.astype(F32), axis=0)
    input_grad, grad_shift, sums1 = norm1_back(part1[0], near, far, stream, grad_middle, line(norm1_gain), seg)

    down_x = add_low(down_kept, down_sent)
    down_y = add_low(cut(down_x, y_at, model // 2, 1), swap(cut(down_x, 1 - y_at, model // 2, 1), "y"))
    down_z = lax.psum_scatter(down_y, "z", scatter_dimension=0, tiled=True)
    up_rows = model // dp
    up_sent = swap(cut(up_z, 1 - x_at, up_rows, 0), "x")
    up_sent = jnp.concatenate([up_sent[:, half // 2 :], up_sent[:, : half // 2]], axis=1)
    up_x = add_low(cut(up_z, x_at, up_rows, 0), up_sent)
    up_y = add_low(cut(up_x, y_at, half // 2, 1), swap(cut(up_x, 1 - y_at, half // 2, 1), "y"))
    out_grad = jnp.concatenate([cut(out_grad, o_at, width, 0) for o_at in order], axis=0)
    out_c = add_low(cut(out_grad, c_at, model // 2, 1), swap(cut(out_grad, 1 - c_at, model // 2, 1), "c"))
    out_y = add_low(cut(out_c, y_at, width, 1), swap(cut(out_c, 1 - y_at, width, 1), "y"))
    late = jnp.concatenate([qkv_grad, out_y], axis=1).reshape(depth, 2 * up_rows, model)
    late_x = add_low(cut(late, x_at, up_rows, 1), swap(cut(late, 1 - x_at, up_rows, 1), "x"))
    late_z = lax.psum_scatter(late_x, "z", scatter_dimension=0, tiled=False)

    down_done = ordered(y_at, down_z, swap(down_z, "y"), 1)
    down_done = ordered(c_at, down_done, swap(down_done, "c"), 0).astype(F32)
    up_done = ordered(y_at, up_y, swap(up_y, "y"), 1)
    up_done = ordered(c_at, up_done[None], swap(up_done, "c")[None], 0).reshape(2, up_rows, 2, depth, piece)
    up_done = jnp.where(x_at == 1, up_done, up_done[:, :, ::-1]).transpose(1, 3, 2, 0, 4)
    up_done = up_done.reshape(up_rows, hidden_width).astype(F32)
    late_done = ordered(c_at, late_z[None], swap(late_z, "c")[None], 0)
    late_done = ordered(y_at, late_done[None], swap(late_done, "y")[None], 0).reshape(parts, up_rows, model)
    qkv_done = late_done[:, :, : 3 * width].reshape(parts, up_rows, 3, width).transpose(1, 2, 0, 3)
    qkv_done = qkv_done.reshape(up_rows, 3 * model).astype(F32)
    out_done = late_done[:, :, 3 * width :].reshape(2, 2, up_rows, width).transpose(2, 1, 0, 3)
    out_done = out_done.reshape(up_rows, model).astype(F32)

    up_b = up_b.reshape(2, depth, 1, piece)
    up_b = jnp.where(x_at == 1, up_b, up_b[::-1]).transpose(1, 0, 2, 3)
    up_b = jnp.where(jnp.arange(2)[:, None] == c_at, up_b, 0.0).reshape(-1, model)
    qkv_b = jnp.where(jnp.arange(parts)[:, None] == me, qkv_b.reshape(3, 1, width), 0.0).reshape(3, model)
    small = jnp.concatenate(
        [grad_shift.reshape(rows * SEGS, model), sums1[:2], sums2[:4], qkv_b, up_b], axis=0
    )
    small = add_low(small, swap(small.astype(BF16), "c"))
    small = add_low(small, swap(small, "y"))
    small = lax.all_gather(small, ("z", "x"))
    shifts = small[:, : rows * SEGS].reshape(dp * rows * SEGS, model)
    columns = (2 * z_at + x_at) * (TEMB // dp) + jnp.arange(TEMB // dp)
    wanted = time_features(all_times.reshape(-1), columns, TEMB // 2)
    time_w_done = dot(wanted, shifts, 0, 0)
    sums = jnp.sum(small[:, rows * SEGS :].astype(F32), axis=0)
    dp_at = 2 * z_at + x_at

    def share(vector):
        return cut(vector.reshape(-1), dp_at, vector.size // dp, 0)

    time_b_done = jnp.sum(cut(shifts, dp_at, up_rows, 1).astype(F32), axis=0)
    return (
        output, input_grad, time_w_done, time_b_done, share(sums[0]), share(sums[1]), qkv_done, share(sums[6:9]),
        out_done, share(sums[4]), share(sums[2]), share(sums[3]), up_done, share(sums[9:]), down_done, share(sums[5]),
    )


def solution(mesh):
    dp, seq = mesh.shape["dp"], mesh.shape["seq"]
    fine = Mesh(mesh.devices.reshape(dp // 2, 2, seq // 2, 2), ("z", "x", "y", "c"))
    rows, seqs = ("z", "x"), ("y", "c")
    placed = (P(rows, seqs, None), P(rows, seqs), P(rows, None)) + (P(),) * 14 + (P(rows, seqs, None),)
    vec, mat = P(rows), P(rows, None)
    return jax.shard_map(
        functools.partial(local, dp=dp),
        mesh=fine,
        in_specs=placed,
        out_specs=(
            P(rows, seqs, None), P(rows, seqs, None), mat, vec, vec, vec, mat, vec, mat, vec, vec, vec, mat, vec, mat, vec,
        ),
        check_vma=False,
    )
```

time: 724 us -> 543 us (0.75)
  local copies, waits for them, and re-layouts: 151 us -> 44.9 us
  waiting for transfers between devices: 212 us -> 111 us
  blocking collectives: 0 us -> 94.2 us
  other arithmetic: 94.3 us -> 35.3 us
  matrix products: 104 us -> 67.7 us
  Pallas kernels: 124 us -> 144 us
    all_gather x0 -> x2, blocking collectives: none -> 94.2 us  [the longest x1 60.3 us: local(): all_times = lax.all_gather(doc_times.reshape(rows * SEGS), ('z', 'x'))]
    ppermute x38 -> x34, waiting for transfers between devices: 160 us -> 111 us  [swap(): return lax.ppermute(value, axis, [(0, 1), (1, 0)])]
    unnamed x174 -> x86, local copies, waits for them, and re-layouts: 53.1 us -> 8.97 us
    dynamic_slice x13 -> x16, local copies, waits for them, and re-layouts: 44.6 us -> 7.16 us  [the longest x15 7.14 us: cut(): return lax.dynamic_slice_in_dim(values, index * size, size, axis)]
    unnamed x6 -> x3, waiting for transfers between devices: 37 us -> 0.05 us
    dot_general x12 -> x13, matrix products: 98.7 us -> 67.7 us  [dot(): lax.dot_general(left_op, right_op, (((left_dim,), (right_dim,)), ((), ())...]
    convert_element_type x30 -> x18, other arithmetic: 40.5 us -> 14.4 us  [the longest x8 6.64 us: add_low(): return (kept.astype(F32) + sent.astype(F32)).astype(BF16)]
    pallas_call x4 -> x10, Pallas kernels: 124 us -> 144 us  [the longest x8 129 us: call(): pl.pallas_call(kernel, grid_spec=pltpu.PrefetchScalarGridSpec(num_scalar_...]
  transfers between devices with their start and end apart: 43 -> 37, of which waited for: 13 -> 11; matrix products, arithmetic and copies ran while one was open for 39% -> 21% of each run, Pallas kernels for 9% -> 15%
where the time goes in v2:
time: 543 us; the launch traced here: 534 us
  Pallas kernels  144 us (27%)
  waiting for transfers between devices  111 us (20%)
  blocking collectives  94.2 us (17%)
  matrix products  67.7 us (12%)
  local copies, waits for them, and re-layouts  44.9 us (8%)
  other arithmetic  35.3 us (7%)
  starting transfers between devices  21.8 us (4%)
  between operations  15.2 us (3%)
    pallas_call x8, Pallas kernels, call(): pl.pallas_call(kernel, grid_spec=pltpu.PrefetchScalarGridSpec(num_scalar_...  129 us
    ppermute x34, waiting for transfers between devices, swap(): return lax.ppermute(value, axis, [(0, 1), (1, 0)])  111 us
    dot_general x13, matrix products, dot(): lax.dot_general(left_op, right_op, (((left_dim,), (right_dim,)), ((), ())...  67.7 us
    all_gather x1, blocking collectives, local(): all_times = lax.all_gather(doc_times.reshape(rows * SEGS), ('z', 'x'))  60.3 us
    all_gather x1, blocking collectives, local(): small = lax.all_gather(small, ('z', 'x'))  33.9 us
    ppermute x34, starting transfers between devices, swap(): return lax.ppermute(value, axis, [(0, 1), (1, 0)])  21 us
    pallas_call x2, Pallas kernels, project_qkv(): pl.pallas_call(qkv_body, grid_spec=pltpu.PrefetchScalarGridSpec(num_scala...  15.1 us
  transfers between devices with their start and end apart: 37, of which 11 were waited for; matrix products, arithmetic and copies ran while one was open for 21% of the time, Pallas kernels for 15%

profile of v2, /device:TPU:0, one launch (start us, length us, event | category | flops | bytes accessed | tf_op | source)
XLA Modules:
  0.0 533.7 jit_solution(14598430542196652144)
XLA Ops:
  25.1 30.8 %collective-permute-done.1 = s32[3,256]{1,0:T(4,128)S(1)} collective-permute-done((s32[3,256]{1,0:T(4,128)S(1)}, s32[3,256]{1,0:T(4,128)S(1)}, u32[]{:S(2)}, u32[]{:S(2)}) %collective-permute-start.1) | collective-permute-done | bytes 3104 | tf_op jit(solution)/shard_map/ppermute | solution.py:27
  61.7 14.9 %cot_down.1 = (bf16[1536,2048]{1,0:T(8,128)(2,1)}, bf16[1024,2048]{1,0:T(8,128)(2,1)}, bf16[2048,1024]{1,0:T(8,128)(2,1)}) custom-call(s32[8]{0:T(128)} %add.265.refs_0_, bf16[768,1024]{1,0:T(8,128)(2,1)} %bitcast.145, bf16[768,1024]{1,0:T(8,128)(2,1)} %collective-permute-done.6.refs_2_, bf16[1024,4096]{1,0:T(8,128)(2,1)} %refs_3_.1, bf16[4096,1024]{1,0:T(8,128)(2,1)} %refs_4_.2), custom_call_target="tpu_custom_call" | custom-call | flops 6442450944 | bytes 26214400 | tf_op jit(solution)/shard_map/cot_down/pallas_call | solution.py:93
  77.8 7.5 %qkv.2 = (bf16[4,3,256,256]{3,2,1,0:T(8,128)(2,1)}, bf16[4,3,256,256]{3,2,1,0:T(8,128)(2,1)}, bf16[4,3,256,256]{3,2,1,0:T(8,128)(2,1)}, bf16[1024,768]{1,0:T(8,128)(2,1)}) custom-call(s32[1]{0:T(128)} %bitcast.me_ref, bf16[3,256,1024]{2,1,0:T(8,128)(2,1)} %get-tuple-element.42.a_ref, bf16[3,256,1024]{2,1,0:T(8,128)(2,1)} %copy-done.3, ...), custom_call_target="tpu_custom_call" | custom-call | flops 2415919104 | bytes 9437184 | tf_op jit(solution)/shard_map/qkv/pallas_call | solution.py:177
  85.3 7.6 %qkv.3 = (bf16[4,3,256,256]{3,2,1,0:T(8,128)(2,1)}, bf16[4,3,256,256]{3,2,1,0:T(8,128)(2,1)}, bf16[4,3,256,256]{3,2,1,0:T(8,128)(2,1)}, bf16[1024,768]{1,0:T(8,128)(2,1)}) custom-call(s32[1]{0:T(128)} %bitcast.me_ref, bf16[3,256,1024]{2,1,0:T(8,128)(2,1)} %collective-permute-done.3.a_ref, ...), custom_call_target="tpu_custom_call", output_to_operand_aliasing={{0}: (11, {}), {1}: (12, {}), {2}: (13, {})} | custom-call | flops 2415919104 | bytes 9437184 | tf_op jit(solution)/shard_map/qkv/pallas_call | solution.py:177
  92.9 22.9 %attend.1 = (bf16[4,3,256,256]{3,2,1,0:T(8,128)(2,1)}, f32[3,4,8,256]{3,2,1,0:T(8,128)}) custom-call(s32[12]{0:T(128)} %reshape.425.refs_0_, s32[48]{0:T(128)} %reshape.426.refs_1_, bf16[4,3,256,256]{3,2,1,0:T(8,128)(2,1)} %get-tuple-element.47.refs_2_, bf16[4,3,256,256]{3,2,1,0:T(8,128)(2,1)} %get-tuple-element.48.refs_3_, ...), custom_call_target="tpu_custom_call" | custom-call | flops 12884901888 | bytes 6291456 | tf_op jit(solution)/shard_map/attend/pallas_call | solution.py:93
  119.8 16.9 %collective-permute-done.8 = bf16[2,3,256,256]{3,2,1,0:T(8,128)(2,1)S(1)} collective-permute-done((bf16[2,3,256,256]{3,2,1,0:T(8,128)(2,1)S(1)}, bf16[2,3,256,256]{3,2,1,0:T(8,128)(2,1)S(1)}, u32[]{:S(2)}, u32[]{:S(2)}) %collective-permute-start.8) | collective-permute-done | bytes 786464 | tf_op jit(solution)/shard_map/ppermute | solution.py:27
  140.8 7.8 %middle.1 = (f32[3,256,1024]{2,1,0:T(8,128)}, bf16[3,256,1024]{2,1,0:T(8,128)(2,1)}) custom-call(s32[4]{0:T(128)} %pad_add_fusion.1.refs_0_, bf16[3,256,256]{2,1,0:T(8,128)(2,1)} %get-tuple-element.132.refs_1_, bf16[3,256,256]{2,1,0:T(8,128)(2,1)} %copy-done.11, bf16[3,256,256]{2,1,0:T(8,128)(2,1)} %get-tuple-element.137.refs_3_, ...), custom_call_target="tpu_custom_call" | custom-call | flops 1610612736 | bytes 11010048 | tf_op jit(solution)/shard_map/middle/pallas_call | solution.py:93
  153.5 19.2 %hidden.1 = (bf16[1536,2048]{1,0:T(8,128)(2,1)}, bf16[1536,2048]{1,0:T(8,128)(2,1)}, f32[1,2048]{1,0:T(1,128)}) custom-call(bf16[768,1024]{1,0:T(8,128)(2,1)} %bitcast.177, bf16[768,1024]{1,0:T(8,128)(2,1)} %copy-done.28, bf16[1536,2048]{1,0:T(8,128)(2,1)} %get-tuple-element.43.refs_0_.refs_2_, bf16[1024,2048]{1,0:T(8,128)(2,1)} %get-tuple-element.54.refs_3_, ...), custom_call_target="tpu_custom_call" | custom-call | flops 6442450944 | bytes 26214400 | tf_op jit(solution)/shard_map/hidden/pallas_call | solution.py:93
  172.8 7.2 %fusion.27 = bf16[1024,1024]{1,0:T(8,128)(2,1)} fusion(bf16[768,1024]{1,0:T(8,128)(2,1)} %collective-permute-done.6.refs_2_, bf16[768,1024]{1,0:T(8,128)(2,1)S(1)} %bitcast.146, bf16[1536,2048]{1,0:T(8,128)(2,1)} %get-tuple-element.55), kind=kOutput, calls=%fused_computation.41 | convolution fusion | flops 3228565504 | bytes 8388608 | tf_op jit(solution)/shard_map/dot_general | solution.py:48
  181.2 60.3 %all-gather.1 = s32[8,1,24]{2,1,0:T(1,128)S(1)} all-gather(s32[1,1,24]{2,1,0:T(1,128)S(1)} %reshape.459), channel_id=1, replica_groups=mesh['z'=4,'x'=2,'y'=2,'c'=2] {'z','x'}, dimensions={0}, use_global_device_ids=true | all-gather | bytes 864 | tf_op jit(solution)/shard_map/all_gather | solution.py:628
  241.6 8.0 %add_convert_fusion = (bf16[1024,1024]{1,0:T(8,128)(2,1)S(1)}, bf16[1024,1024]{1,0:T(8,128)(2,1)}) fusion(bf16[1024,1024]{1,0:T(8,128)(2,1)} %collective-permute-done.16.refs_13_, bf16[768,1024]{1,0:T(8,128)(2,1)} %collective-permute-done.6.refs_2_, bf16[768,1024]{1,0:T(8,128)(2,1)S(1)} %bitcast.147, bf16[1536,2048]{1,0:T(8,128)(2,1)} %get-tuple-element.55), kind=kOutput, calls=%fused_computation.9 | convolution fusion | flops 3232759808 | bytes 12582912 | tf_op jit(solution)/shard_map/dot_general | solution.py:48
  255.9 4.6 fusion.38
  261.1 10.7 %collective-permute-done.31 = bf16[1024,512]{1,0:T(8,128)(2,1)S(1)} collective-permute-done((bf16[1024,512]{1,0:T(8,128)(2,1)S(1)}, bf16[1024,512]{1,0:T(8,128)(2,1)S(1)}, u32[]{:S(2)}, u32[]{:S(2)}) %collective-permute-start.31) | collective-permute-done | bytes 1048608 | tf_op jit(solution)/shard_map/ppermute | solution.py:27
  273.7 11.2 %convolution_convert_fusion.refs_12_ = bf16[1024,2048]{1,0:T(8,128)(2,1)} fusion(bf16[1536,2048]{1,0:T(8,128)(2,1)} %get-tuple-element.57, bf16[768,1024]{1,0:T(8,128)(2,1)} %copy-done.28, bf16[768,1024]{1,0:T(8,128)(2,1)} %bitcast.178), kind=kOutput, calls=%fused_computation.10 | convolution fusion | flops 6450839552 | bytes 13631488 | tf_op jit(solution)/shard_map/dot_general | solution.py:48
  286.1 7.8 %fusion.35 = bf16[768,1024]{1,0:T(8,128)(2,1)} fusion(bf16[1024,2048]{1,0:T(8,128)(2,1)} %get-tuple-element.54.refs_3_, bf16[1536,2048]{1,0:T(8,128)(2,1)} %get-tuple-element.57), kind=kOutput, calls=%fused_computation.44 | convolution fusion | flops 3222011904 | bytes 8912896 | tf_op jit(solution)/shard_map/dot_general | solution.py:48
  295.4 9.8 %middle_back.1 = (f32[3,256,1024]{2,1,0:T(8,128)}, bf16[3,256,1024]{2,1,0:T(8,128)(2,1)}, bf16[4,3,256,256]{3,2,1,0:T(8,128)(2,1)}, f32[8,1024]{1,0:T(8,128)}) custom-call(s32[4]{0:T(128)} %pad_add_fusion.1.refs_0_, bf16[3,256,1024]{2,1,0:T(8,128)(2,1)} %bitcast.149, bf16[3,256,1024]{2,1,0:T(8,128)(2,1)} %bitcast.148, ...), custom_call_target="tpu_custom_call" | custom-call | flops 1610612736 | bytes 14155776 | tf_op jit(solution)/shard_map/middle_back/pallas_call | solution.py:93
  314.4 5.9 %add_add_fusion = f32[768,1024]{1,0:T(8,128)} fusion(bf16[768,1024]{1,0:T(8,128)(2,1)} %collective-permute-done.11, f32[1024]{0:T(1024)S(1)} %convert_element_type.271, bf16[2048,1024]{1,0:T(8,128)(2,1)S(1)} %copy-done.30, bf16[1536,2048]{1,0:T(8,128)(2,1)S(1)} %bitcast.181), kind=kOutput, calls=%fused_computation.29 | convolution fusion | flops 3223584768 | bytes 12062720 | tf_op jit(solution)/shard_map/dot_general | solution.py:48
  325.7 41.7 %attend_back.1 = bf16[4,3,256,768]{3,2,1,0:T(8,128)(2,1)} custom-call(s32[12]{0:T(128)} %reshape.425.refs_0_, s32[48]{0:T(128)} %reshape.426.refs_1_, bf16[4,3,256,256]{3,2,1,0:T(8,128)(2,1)} %get-tuple-element.47.refs_2_, bf16[4,3,256,256]{3,2,1,0:T(8,128)(2,1)} %get-tuple-element.48.refs_3_, bf16[4,3,256,256]{3,2,1,0:T(8,128)(2,1)} %get-tuple-element.49.refs_4_, ...), custom_call_target="tpu_custom_call" | custom-call | flops 32212254720 | bytes 12582912 | tf_op jit(solution)/shard_map/attend_back/pallas_call | solution.py:93
  375.7 6.9 %bitcast_convert_fusion = bf16[1024,768]{0,1:T(8,128)(2,1)S(1)} fusion(bf16[4,3,256,768]{3,2,1,0:T(8,128)(2,1)S(1)} %bitcast.126, bf16[1,3,256,1024]{3,2,1,0:T(8,128)(2,1)} %bitcast.43, bf16[1,3,256,1024]{3,2,1,0:T(8,128)(2,1)S(1)} %bitcast.141, bf16[1,3,256,1024]{3,2,1,0:T(8,128)(2,1)} %bitcast.41, bf16[1,3,256,1024]{3,2,1,0:T(8,128)(2,1)S(1)} %bitcast.142), kind=kOutput, calls=%fused_computation.17 | convolution fusion | flops 4842061824 | bytes 12582912 | tf_op jit(solution)/shard_map/dot_general | solution.py:48
  404.2 27.3 %collective-permute-done.32 = bf16[256,512]{1,0:T(8,128)(2,1)S(1)} collective-permute-done((bf16[256,512]{1,0:T(8,128)(2,1)}, bf16[256,512]{1,0:T(8,128)(2,1)S(1)}, u32[]{:S(2)}, u32[]{:S(2)}) %collective-permute-start.32) | collective-permute-done | bytes 262176 | tf_op jit(solution)/shard_map/ppermute | solution.py:27
  431.7 7.7 %norm1_back.1 = (bf16[3,256,1024]{2,1,0:T(8,128)(2,1)}, f32[3,8,1024]{2,1,0:T(8,128)}, f32[8,1024]{1,0:T(8,128)}) custom-call(bf16[3,256,1024]{2,1,0:T(8,128)(2,1)} %bitcast.132, bf16[3,256,1024]{2,1,0:T(8,128)(2,1)} %collective-permute-done.17.refs_1_, bf16[3,256,1024]{2,1,0:T(8,128)(2,1)} %collective-permute-done.19.refs_2_, ...), custom_call_target="tpu_custom_call" | custom-call | bytes 12582912 | tf_op jit(solution)/shard_map/norm1_back/pallas_call | solution.py:93
  449.0 33.9 %all-gather.2 = bf16[8,37,1024]{2,1,0:T(8,128)(2,1)S(1)} all-gather(bf16[1,37,1024]{2,1,0:T(8,128)(2,1)S(1)} %fusion.55), channel_id=2, replica_groups=mesh['z'=4,'x'=2,'y'=2,'c'=2] {'z','x'}, dimensions={0}, use_global_device_ids=true | all-gather | bytes 681984 | tf_op jit(solution)/shard_map/all_gather | solution.py:732
  487.7 7.4 %collective-permute-done.27 = bf16[128,2048]{1,0:T(8,128)(2,1)S(1)} collective-permute-done((bf16[128,2048]{1,0:T(8,128)(2,1)S(1)}, bf16[128,2048]{1,0:T(8,128)(2,1)S(1)}, u32[]{:S(2)}, u32[]{:S(2)}) %collective-permute-start.27) | collective-permute-done | bytes 524320 | tf_op jit(solution)/shard_map/ppermute | solution.py:27
  505.7 5.0 collective-permute-done.26
  (299 shorter events, 135.5 us)
Async XLA Ops:
  7.2 392.9 %reduce-scatter.8.cloned.1.call-start = ((), (), s32[]{:S(2)}) async-start(), calls=%async_computation.5 | async-start | bytes 1310720 | tf_op jit(solution)/shard_map/reduce_scatter | solution.py:697
  18.2 40.3 %collective-permute-start.3 = (bf16[3,256,1024]{2,1,0:T(8,128)(2,1)}, bf16[3,256,1024]{2,1,0:T(8,128)(2,1)}, u32[]{:S(2)}, u32[]{:S(2)}) collective-permute-start(bf16[3,256,1024]{2,1,0:T(8,128)(2,1)} %get-tuple-element.42.a_ref), channel_id=1, source_target_pairs={{0,2},{2,0},{1,3},{3,1},{4,6},{6,4},{5,7},{7,5},{8,10},{10,8},{9,1... | collective-permute-start | bytes 4718600 | tf_op jit(solution)/shard_map/ppermute | solution.py:27
  21.1 34.8 %collective-permute-start.1 = (s32[3,256]{1,0:T(4,128)S(1)}, s32[3,256]{1,0:T(4,128)S(1)}, u32[]{:S(2)}, u32[]{:S(2)}) collective-permute-start(s32[3,256]{1,0:T(4,128)S(1)} %copy-done.22), channel_id=1, source_target_pairs={{0,2},{2,0},{1,3},{3,1},{4,6},{6,4},{5,7},{7,5},{8,10},{10,8},{9,1... | collective-permute-start | bytes 9224 | tf_op jit(solution)/shard_map/ppermute | solution.py:27
  21.2 37.2 %collective-permute-start = (s32[3,256]{1,0:T(4,128)S(1)}, s32[3,256]{1,0:T(4,128)S(1)}, u32[]{:S(2)}, u32[]{:S(2)}) collective-permute-start(s32[3,256]{1,0:T(4,128)S(1)} %copy-done.22), channel_id=1, source_target_pairs={{0,1},{1,0},{2,3},{3,2},{4,5},{5,4},{6,7},{7,6},{8,9},{9,8},{10,11... | collective-permute-start | bytes 9224 | tf_op jit(solution)/shard_map/ppermute | solution.py:27
  21.2 55.4 %collective-permute-start.5 = (bf16[3,256,1024]{2,1,0:T(8,128)(2,1)}, bf16[3,256,1024]{2,1,0:T(8,128)(2,1)S(1)}, u32[]{:S(2)}, u32[]{:S(2)}) collective-permute-start(bf16[3,256,1024]{2,1,0:T(8,128)(2,1)} %get-tuple-element.42.a_ref), channel_id=1, source_target_pairs={{0,1},{1,0},{2,3},{3,2},{4,5},{5,4},{6,7},{7,6},{8,9},{9,8},{10,11... | collective-permute-start | bytes 4718600 | tf_op jit(solution)/shard_map/ppermute | solution.py:27
  21.7 40.0 %collective-permute-start.6 = (bf16[768,1024]{1,0:T(8,128)(2,1)}, bf16[768,1024]{1,0:T(8,128)(2,1)}, u32[]{:S(2)}, u32[]{:S(2)}) collective-permute-start(bf16[768,1024]{1,0:T(8,128)(2,1)} %bitcast.144), channel_id=1, source_target_pairs={{0,1},{1,0},{2,3},{3,2},{4,5},{5,4},{6,7},{7,6},{8,9},{9,8},{10,11... | collective-permute-start | bytes 4718600 | tf_op jit(solution)/shard_map/ppermute | solution.py:27
  58.4 26.9 %collective-permute-start.4 = (bf16[3,256,1024]{2,1,0:T(8,128)(2,1)}, bf16[3,256,1024]{2,1,0:T(8,128)(2,1)}, u32[]{:S(2)}, u32[]{:S(2)}) collective-permute-start(bf16[3,256,1024]{2,1,0:T(8,128)(2,1)} %collective-permute-done.3.a_ref), channel_id=1, source_target_pairs={{0,1},{1,0},{2,3},{3,2},{4,5},{5,4},{6,7},{7,6},{8,9},{9,8},{10,11... | collective-permute-start | bytes 4718600 | tf_op jit(solution)/shard_map/ppermute | solution.py:27
  117.1 19.5 %collective-permute-start.8 = (bf16[2,3,256,256]{3,2,1,0:T(8,128)(2,1)S(1)}, bf16[2,3,256,256]{3,2,1,0:T(8,128)(2,1)S(1)}, u32[]{:S(2)}, u32[]{:S(2)}) collective-permute-start(bf16[2,3,256,256]{3,2,1,0:T(8,128)(2,1)S(1)} %slice.120), channel_id=1, source_target_pairs={{0,2},{2,0},{1,3},{3,1},{4,6},{6,4},{5,7},{7,5},{8,10},{10,8},{9,1... | collective-permute-start | bytes 2359304 | tf_op jit(solution)/shard_map/ppermute | solution.py:27
  119.8 20.1 %collective-permute-start.7 = (bf16[3,256,256]{2,1,0:T(8,128)(2,1)S(1)}, bf16[3,256,256]{2,1,0:T(8,128)(2,1)S(1)}, u32[]{:S(2)}, u32[]{:S(2)}) collective-permute-start(bf16[3,256,256]{2,1,0:T(8,128)(2,1)S(1)} %get-tuple-element.133), channel_id=1, source_target_pairs={{0,1},{1,0},{2,3},{3,2},{4,5},{5,4},{6,7},{7,6},{8,9},{9,8},{10,11... | collective-permute-start | bytes 1179656 | tf_op jit(solution)/shard_map/ppermute | solution.py:27
  179.9 61.6 %collective-permute-start.16 = (bf16[1024,1024]{1,0:T(8,128)(2,1)}, bf16[1024,1024]{1,0:T(8,128)(2,1)}, u32[]{:S(2)}, u32[]{:S(2)}) collective-permute-start(bf16[1024,1024]{1,0:T(8,128)(2,1)} %fusion.27), channel_id=1, source_target_pairs={{0,4},{4,0},{1,5},{5,1},{2,6},{6,2},{3,7},{7,3},{8,12},{12,8},{9,1... | collective-permute-start | bytes 6291464 | tf_op jit(solution)/shard_map/ppermute | solution.py:27
  249.7 22.1 %collective-permute-start.31 = (bf16[1024,512]{1,0:T(8,128)(2,1)S(1)}, bf16[1024,512]{1,0:T(8,128)(2,1)S(1)}, u32[]{:S(2)}, u32[]{:S(2)}) collective-permute-start(bf16[1024,512]{1,0:T(8,128)(2,1)S(1)} %constant_dynamic-slice_fusion.1), channel_id=1, source_target_pairs={{0,2},{2,0},{1,3},{3,1},{4,6},{6,4},{5,7},{7,5},{8,10},{10,8},{9,1... | collective-permute-start | bytes 3145736 | tf_op jit(solution)/shard_map/ppermute | solution.py:27
  255.9 57.2 %collective-permute-start.11 = (bf16[768,1024]{1,0:T(8,128)(2,1)}, bf16[768,1024]{1,0:T(8,128)(2,1)}, u32[]{:S(2)}, u32[]{:S(2)}) collective-permute-start(bf16[768,1024]{1,0:T(8,128)(2,1)} %fusion.32), channel_id=1, source_target_pairs={{0,1},{1,0},{2,3},{3,2},{4,5},{5,4},{6,7},{7,6},{8,9},{9,8},{10,11... | collective-permute-start | bytes 4718600 | tf_op jit(solution)/shard_map/ppermute | solution.py:27
  260.6 33.7 %collective-permute-start.12 = (bf16[768,1024]{1,0:T(8,128)(2,1)}, bf16[768,1024]{1,0:T(8,128)(2,1)S(1)}, u32[]{:S(2)}, u32[]{:S(2)}) collective-permute-start(bf16[768,1024]{1,0:T(8,128)(2,1)} %fusion.38), channel_id=1, source_target_pairs={{0,1},{1,0},{2,3},{3,2},{4,5},{5,4},{6,7},{7,6},{8,9},{9,8},{10,11... | collective-permute-start | bytes 4718600 | tf_op jit(solution)/shard_map/ppermute | solution.py:27
  273.2 211.4 %reduce-scatter.6.cloned.1.call-start = ((), (), s32[]{:S(2)}) async-start(), calls=%async_computation.4 | async-start | bytes 5242880 | tf_op jit(solution)/shard_map/reduce_scatter | solution.py:673
  294.0 193.7 %reduce-scatter.4.cloned.1.call-start = ((), (), s32[]{:S(2)}) async-start(), calls=%async_computation.3 | async-start | bytes 1310720 | tf_op jit(solution)/shard_map/reduce_scatter | solution.py:708
  306.7 15.4 %collective-permute-start.14 = (bf16[2,3,256,256]{3,2,1,0:T(8,128)(2,1)S(1)}, bf16[2,3,256,256]{3,2,1,0:T(8,128)(2,1)S(1)}, u32[]{:S(2)}, u32[]{:S(2)}) collective-permute-start(bf16[2,3,256,256]{3,2,1,0:T(8,128)(2,1)S(1)} %slice.129), channel_id=1, source_target_pairs={{0,2},{2,0},{1,3},{3,1},{4,6},{6,4},{5,7},{7,5},{8,10},{10,8},{9,1... | collective-permute-start | bytes 2359304 | tf_op jit(solution)/shard_map/ppermute | solution.py:27
  308.4 16.0 %collective-permute-start.13 = (bf16[3,256,256]{2,1,0:T(8,128)(2,1)S(1)}, bf16[3,256,256]{2,1,0:T(8,128)(2,1)S(1)}, u32[]{:S(2)}, u32[]{:S(2)}) collective-permute-start(bf16[3,256,256]{2,1,0:T(8,128)(2,1)S(1)} %get-tuple-element.135), channel_id=1, source_target_pairs={{0,1},{1,0},{2,3},{3,2},{4,5},{5,4},{6,7},{7,6},{8,9},{9,8},{10,11... | collective-permute-start | bytes 1179656 | tf_op jit(solution)/shard_map/ppermute | solution.py:27
  322.7 64.3 %collective-permute-start.23 = (bf16[1024,256]{0,1:T(8,128)(2,1)S(1)}, bf16[1024,256]{0,1:T(8,128)(2,1)S(1)}, u32[]{:S(2)}, u32[]{:S(2)}) collective-permute-start(bf16[1024,256]{0,1:T(8,128)(2,1)S(1)} %constant_dynamic-slice_fusion.8), channel_id=1, source_target_pairs={{0,2},{2,0},{1,3},{3,1},{4,6},{6,4},{5,7},{7,5},{8,10},{10,8},{9,1... | collective-permute-start | bytes 1572872 | tf_op jit(solution)/shard_map/ppermute | solution.py:27
  374.7 57.0 %collective-permute-start.17 = (bf16[3,256,1024]{2,1,0:T(8,128)(2,1)}, bf16[3,256,1024]{2,1,0:T(8,128)(2,1)}, u32[]{:S(2)}, u32[]{:S(2)}) collective-permute-start(bf16[3,256,1024]{2,1,0:T(8,128)(2,1)} %bitcast.30), channel_id=1, source_target_pairs={{0,1},{1,0},{2,3},{3,2},{4,5},{5,4},{6,7},{7,6},{8,9},{9,8},{10,11... | collective-permute-start | bytes 4718600 | tf_op jit(solution)/shard_map/ppermute | solution.py:27
  389.1 42.6 %collective-permute-start.19 = (bf16[3,256,1024]{2,1,0:T(8,128)(2,1)}, bf16[3,256,1024]{2,1,0:T(8,128)(2,1)}, u32[]{:S(2)}, u32[]{:S(2)}) collective-permute-start(bf16[3,256,1024]{2,1,0:T(8,128)(2,1)} %fusion.11), channel_id=1, source_target_pairs={{0,2},{2,0},{1,3},{3,1},{4,6},{6,4},{5,7},{7,5},{8,10},{10,8},{9,1... | collective-permute-start | bytes 4718600 | tf_op jit(solution)/shard_map/ppermute | solution.py:27
  395.6 46.2 %collective-permute-start.24 = (bf16[4,128,1024]{2,1,0:T(8,128)(2,1)}, bf16[4,128,1024]{2,1,0:T(8,128)(2,1)}, u32[]{:S(2)}, u32[]{:S(2)}) collective-permute-start(bf16[4,128,1024]{2,1,0:T(8,128)(2,1)} %constant_dynamic-slice_fusion.7), channel_id=1, source_target_pairs={{0,4},{4,0},{1,5},{5,1},{2,6},{6,2},{3,7},{7,3},{8,12},{12,8},{9,1... | collective-permute-start | bytes 3145736 | tf_op jit(solution)/shard_map/ppermute | solution.py:27
  400.2 31.3 %collective-permute-start.32 = (bf16[256,512]{1,0:T(8,128)(2,1)}, bf16[256,512]{1,0:T(8,128)(2,1)S(1)}, u32[]{:S(2)}, u32[]{:S(2)}) collective-permute-start(bf16[256,512]{1,0:T(8,128)(2,1)} %reduce-scatter.8.cloned.1.call-done), channel_id=1, source_target_pairs={{0,2},{2,0},{1,3},{3,1},{4,6},{6,4},{5,7},{7,5},{8,10},{10,8},{9,1... | collective-permute-start | bytes 786440 | tf_op jit(solution)/shard_map/ppermute | solution.py:27
  431.6 13.9 %collective-permute-start.33 = (bf16[256,1024]{1,0:T(8,128)(2,1)S(1)}, bf16[256,1024]{1,0:T(8,128)(2,1)S(1)}, u32[]{:S(2)}, u32[]{:S(2)}) collective-permute-start(bf16[256,1024]{1,0:T(8,128)(2,1)S(1)} %maximum_select_fusion.7), channel_id=1, source_target_pairs={{0,1},{1,0},{2,3},{3,2},{4,5},{5,4},{6,7},{7,6},{8,9},{9,8},{10,11... | collective-permute-start | bytes 1572872 | tf_op jit(solution)/shard_map/ppermute | solution.py:27
  496.3 14.4 %collective-permute-start.26 = (bf16[2,128,1024]{2,1,0:T(8,128)(2,1)S(1)}, bf16[2,128,1024]{2,1,0:T(8,128)(2,1)S(1)}, u32[]{:S(2)}, u32[]{:S(2)}) collective-permute-start(bf16[2,128,1024]{2,1,0:T(8,128)(2,1)S(1)} %maximum_select_fusion.4), channel_id=1, source_target_pairs={{0,2},{2,0},{1,3},{3,1},{4,6},{6,4},{5,7},{7,5},{8,10},{10,8},{9,1... | collective-permute-start | bytes 1572872 | tf_op jit(solution)/shard_map/ppermute | solution.py:27
  (52 other events, 440.8 us)
Sparse Core Ops, SparseCore 0:
  273.3 24.4 reduce-scatter.7
  300.2 75.4 reduce-scatter.5
  444.5 28.1 reduce-scatter.3

commit v3 on v2

v3 whole, which is shorter than its diff:
```python
import functools
import math

import jax
import jax.numpy as jnp
from jax import lax
from jax.experimental import pallas as pl
from jax.experimental.pallas import tpu as pltpu
from jax.sharding import Mesh, PartitionSpec as P

HEADS = 16
HEAD_DIM = 64
TEMB = 256
SEGS = 8
EPSILON = 1e-05
F32 = jnp.float32
BF16 = jnp.bfloat16
NEG = -1e30
LOG2E = math.log2(math.e)
GELU_A = math.sqrt(2.0 / math.pi)
GELU_B = GELU_A * 0.044715
BLOCK = 256
VMEM = 60 * 1024 * 1024


def swap(value, axis):
    return lax.ppermute(value, axis, [(0, 1), (1, 0)])


def time_features(doc_times, column, half_size):
    frequency = jnp.exp(-math.log(10000.0) * (column % half_size).astype(F32) / half_size)
    angles = doc_times.astype(F32)[..., None] * frequency
    return jnp.where(column < half_size, jnp.sin(angles), jnp.cos(angles)).astype(BF16)


def rotary_tables(positions, head_size):
    half_size = head_size // 2
    frequency = jnp.exp(-math.log(10000.0) * 2.0 * jnp.arange(half_size, dtype=F32) / head_size)
    angles = positions.astype(F32)[..., None] * frequency
    cos_tab, sin_tab = jnp.cos(angles), jnp.sin(angles)
    return (
        jnp.concatenate([cos_tab] * 4, axis=-1),
        jnp.concatenate([-sin_tab, sin_tab, -sin_tab, sin_tab], axis=-1),
    )


def dot(left_op, right_op, left_dim=1, right_dim=0):
    return lax.dot_general(
        left_op, right_op, (((left_dim,), (right_dim,)), ((), ())), preferred_element_type=F32
    )


def turn(values, cos_tab, sin_tab):
    slabs = []
    lane = lax.broadcasted_iota(jnp.int32, (values.shape[0], 128), 1)
    first = lane % HEAD_DIM < HEAD_DIM // 2
    for start in range(0, values.shape[1], 128):
        slab = values[:, start : start + 128]
        partner = jnp.where(
            first, pltpu.roll(slab, 128 - HEAD_DIM // 2, 1), pltpu.roll(slab, HEAD_DIM // 2, 1)
        )
        slabs.append(slab * cos_tab + partner * sin_tab)
    return jnp.concatenate(slabs, axis=1)


def split_low(values):
    high = values.astype(BF16)
    return jnp.concatenate([high, (values - high.astype(F32)).astype(BF16)], axis=0)


def centre(values):
    scale = 1.0 / values.shape[-1]
    centred = values - jnp.sum(values, axis=-1, keepdims=True) * scale
    spread = jnp.sum(centred * centred, axis=-1, keepdims=True) * scale
    inverse = lax.rsqrt(spread + EPSILON)
    return centred * inverse, inverse


def norm_back(grad, gain, hat, inverse):
    scale = 1.0 / grad.shape[-1]
    scaled = grad * gain
    mean = jnp.sum(scaled, axis=-1, keepdims=True) * scale
    along = jnp.sum(scaled * hat, axis=-1, keepdims=True) * scale
    return inverse * (scaled - mean - hat * along)


def call(body, name, prefetch, grid, ins, outs, scratch=(), deps=(), held=(), flops=0, moved=0, trans=0):
    count = len(prefetch) + len(ins)
    extra = [array for array, _ in held] + list(deps)

    def kernel(*refs):
        body(*refs[:count], *refs[count + len(extra) :])

    return pl.pallas_call(
        kernel,
        grid_spec=pltpu.PrefetchScalarGridSpec(
            num_scalar_prefetch=len(prefetch),
            grid=grid,
            in_specs=[spec for _, spec in ins] + [pl.BlockSpec(memory_space=pl.ANY)] * len(extra),
            out_specs=[spec for _, _, spec in outs],
            scratch_shapes=list(scratch),
        ),
        out_shape=[jax.ShapeDtypeStruct(shape, kind) for shape, kind, _ in outs],
        input_output_aliases={count + n: out for n, (_, out) in enumerate(held)},
        compiler_params=pltpu.CompilerParams(vmem_limit_bytes=VMEM),
        cost_estimate=pl.CostEstimate(flops=flops, bytes_accessed=moved, transcendentals=trans),
        name=name,
    )(*prefetch, *[array for array, _ in ins], *extra)


def fixed(shape):
    return pl.BlockSpec(shape, lambda *_: (0,) * len(shape))


def part(shape, row):
    return pl.BlockSpec(shape, lambda *_: (row,) + (0,) * (len(shape) - 1))


def along(shape, axis=0):
    return pl.BlockSpec(shape, lambda g, *_: tuple(g if n == axis else 0 for n in range(len(shape))))


def norm1_body(x_ref, seg_ref, shift_ref, gain_ref, bias_ref, stream_ref, low_ref):
    slots = lax.broadcasted_iota(jnp.int32, (SEGS, seg_ref.shape[-1]), 0) == seg_ref[0]
    onehot = slots.astype(F32).astype(BF16)
    added = dot(jnp.concatenate([onehot, onehot], axis=0), split_low(shift_ref[0]), 0, 0)
    stream = x_ref[0].astype(F32) + added
    hat, _ = centre(stream)
    stream_ref[...] = stream
    low_ref[...] = (hat * gain_ref[...] + bias_ref[...]).astype(BF16)


def norm1(row, x, seg, shift, gain, bias):
    _, shard, model = x.shape
    whole = fixed((shard, model))
    return call(
        norm1_body, "norm1", (), (1,),
        [(x, part((1, shard, model), row)), (seg, part((1, 1, shard), row)), (shift, part((1, SEGS, model), row))]
        + [(gain, fixed((1, model))), (bias, fixed((1, model)))],
        [((shard, model), F32, whole), ((shard, model), BF16, whole)],
        moved=8 * shard * model,
    )


def qkv_body(me_ref, x0, x1, x2, x3, w_ref, b_ref, cos_ref, sin_ref, out_ref, all_ref, own_ref):
    pieces, shard, _ = cos_ref.shape
    refs = (x0, x1, x2, x3)
    step = pl.program_id(0)

    @pl.when(step == 0)
    def _():
        for n, x_ref in enumerate(refs):
            all_ref[0, n] = x_ref[...]

    def run(turned):
        w = w_ref[...]
        later = dot(x0[...], w)
        for n in range(pieces):
            full = later + b_ref[...].astype(F32)
            if n + 1 < pieces:
                later = dot(refs[n + 1][...], w)
            if turned:
                full = turn(full, cos_ref[n], sin_ref[n]) * jnp.where(step == 0, LOG2E * HEAD_DIM**-0.5, 1.0)
            out_ref[0, n] = full.astype(BF16)

    own_ref[...] = w_ref[...].T

    @pl.when(step < 2)
    def _():
        run(True)

    @pl.when(step == 2)
    def _():
        run(False)


def project_qkv(row, rows, me, pieces, weight, bias, cos_tab, sin_tab, held=(), deps=()):
    shard, model = pieces[0].shape
    parts = len(pieces)
    width = model // parts
    return call(
        qkv_body, "qkv", (me,), (3,),
        [(x, fixed((shard, model))) for x in pieces]
        + [
            (weight, pl.BlockSpec((model, width), lambda g, m: (0, g * parts + m[0]))),
            (bias, pl.BlockSpec((1, width), lambda g, m: (0, g * parts + m[0]))),
            (cos_tab, fixed(cos_tab.shape)),
            (sin_tab, fixed(cos_tab.shape)),
        ],
        [
            ((3, parts, shard, width), BF16, along((1, parts, shard, width))),
            ((rows, parts, shard, model), BF16, part((1, parts, shard, model), row)),
            ((3 * width, model), BF16, along((width, model))),
        ],
        held=[(array, 1) for array in held], deps=deps,
        flops=6 * parts * shard * model * width, moved=2 * (3 * model * width + 2 * parts * shard * model),
    )


def seg_columns(segq_all, segk):
    pieces, shard, _ = segk.shape
    for j in range(pieces):
        row = jnp.broadcast_to(segq_all[j:j+1].astype(F32), (128, shard))
        segk[j] = row.T

def attend_body(cnt_ref, idx_ref, qkv_ref, seg_ref, o_ref, one_ref, far_ref, lse_ref, vt, segk, qmt, acc):
    _, pieces, shard, width = qkv_ref.shape
    q_ref, k_ref, v_ref = (qkv_ref.at[n] for n in range(3))
    qmt[...] = jnp.zeros_like(qmt)
    for j in range(pieces):
        vt[j] = v_ref[j].T
    seg_columns(seg_ref[0], segk)

    @pl.loop(0, pieces)
    def _(piece):
        attend_piece(piece, cnt_ref, idx_ref, q_ref, k_ref, seg_ref, o_ref, lse_ref, vt, segk, qmt, acc)

    one_ref[...] = o_ref[1]
    far_ref[...] = o_ref[2:]


def attend_piece(piece, cnt_ref, idx_ref, q_ref, k_ref, seg_ref, o_ref, lse_ref, vt, segk, qmt, acc):
    pieces, shard, width = k_ref.shape
    heads = width // HEAD_DIM
    qt = q_ref[piece].T
    for h in range(heads):
        at = slice(h * HEAD_DIM, (h + 1) * HEAD_DIM)
        qmt[at, h * shard : (h + 1) * shard] = qt[at]
    seg_q = seg_ref[0, pl.ds(piece, 1)].astype(F32)

    def run(count):
        @pl.when(cnt_ref[piece] == count)
        def _():
            qm = qmt[...]
            places = [idx_ref[piece * pieces + t] for t in range(count)]
            top, tot, out = [None] * heads, [None] * heads, [None] * heads
            later = dot(k_ref[places[0]], qm)
            for t in range(count):
                s = later
                if t + 1 < count:
                    later = dot(k_ref[places[t + 1]], qm)
                col = segk[places[t]]
                same = jnp.concatenate([col] * (shard // 128), axis=1) == seg_q
                for h in range(heads):
                    at = slice(h * HEAD_DIM, (h + 1) * HEAD_DIM)
                    sh = jnp.where(same, s[:, h * shard : (h + 1) * shard], NEG)
                    best = jnp.max(sh, axis=0, keepdims=True)
                    if t:
                        best = jnp.maximum(top[h], best)
                        fade = jnp.exp2(top[h] - best)
                    p = jnp.exp2(sh - best)
                    total = jnp.sum(p, axis=0, keepdims=True)
                    part = dot(vt[places[t], at], p.astype(BF16))
                    if t:
                        total = tot[h] * fade + total
                        part = out[h] * fade + part
                    top[h], tot[h], out[h] = best, total, part
            for h in range(heads):
                acc[h * HEAD_DIM : (h + 1) * HEAD_DIM] = out[h] / tot[h]
                lse_ref[piece, h : h + 1] = top[h] + jnp.log2(tot[h])

    for count in range(1, pieces + 1):
        run(count)
    o_ref[piece] = acc[...].T.astype(BF16)

def attend(row, cnt, idx, qkv, seg):
    _, pieces, shard, width = qkv.shape
    heads = width // HEAD_DIM
    pairs = (pieces * shard) ** 2
    shape, shape_lse = (pieces, shard, width), (pieces, 8, shard)
    return call(
        attend_body, "attend", (cnt, idx), (1,),
        [(qkv, fixed(qkv.shape)), (seg, part((1, pieces, shard), row))],
        [
            (shape, BF16, fixed(shape)),
            (shape[1:], BF16, fixed(shape[1:])),
            ((2,) + shape[1:], BF16, fixed((2,) + shape[1:])),
            (shape_lse, F32, fixed(shape_lse)),
        ],
        [
            pltpu.VMEM((pieces, width, shard), BF16),
            pltpu.VMEM((pieces, shard, 128), F32),
            pltpu.VMEM((width, heads * shard), BF16),
            pltpu.VMEM((width, shard), F32),
        ],
        flops=16 * pairs * width, moved=2 * qkv.size, trans=pairs * heads,
    )


def attend_back_body(
    cnt_ref, idx_ref, qkv_ref, o_ref, do0, do1, do2, do3, lse_ref, seg_ref, cos_ref, sin_ref, w_ref,
    g_ref, p0_ref, p1_ref, p2_ref, p3_ref, kt, segk, dk, dv, dq, dqt, qmt, gmt, qst, gst, do_ref,
):
    _, pieces, shard, width = qkv_ref.shape
    q_ref, k_ref, v_ref = (qkv_ref.at[n] for n in range(3))
    qmt[...] = jnp.zeros_like(qmt)
    gmt[...] = jnp.zeros_like(gmt)
    for j, ref in enumerate((do0, do1, do2, do3)):
        kt[j] = k_ref[j].T
        do_ref[j] = ref[...].reshape(shard, width)
    seg_columns(seg_ref[0], segk)
    dk[...] = jnp.zeros_like(dk)
    dv[...] = jnp.zeros_like(dv)

    @pl.loop(0, pieces)
    def _(piece):
        back_piece(
            piece, cnt_ref, idx_ref, q_ref, k_ref, v_ref, o_ref, do_ref, lse_ref, seg_ref, cos_ref, sin_ref,
            kt, segk, dk, dv, dq, dqt, qmt, gmt, qst, gst,
        )

    for j, ref in ((1, p1_ref), (3, p3_ref), (0, p0_ref), (2, p2_ref)):
        grad_k = turn(dk[j] * (1 / LOG2E), cos_ref[j], -sin_ref[j]).astype(BF16)
        grad = jnp.concatenate([dq[j], grad_k, dv[j].astype(BF16)], axis=1)
        g_ref[0, j] = grad
        ref[...] = dot(grad, w_ref[...]).astype(BF16)


def back_piece(
    piece, cnt_ref, idx_ref, q_ref, k_ref, v_ref, o_ref, do_ref, lse_ref, seg_ref, cos_ref, sin_ref,
    kt, segk, dk, dv, dq, dqt, qmt, gmt, qst, gst,
):
    pieces, shard, width = k_ref.shape
    heads = width // HEAD_DIM
    q, do = q_ref[piece], do_ref[piece]
    qt, gt = q.T, do.T
    lane = lax.broadcasted_iota(jnp.int32, q.shape, 1) // HEAD_DIM
    for h in range(heads):
        at = slice(h * HEAD_DIM, (h + 1) * HEAD_DIM)
        qa = slice(h * shard, (h + 1) * shard)
        qmt[at, qa] = qt[at]
        gmt[at, qa] = gt[at]
        qst[qa] = jnp.where(lane == h, q, jnp.zeros_like(q))
        gst[qa] = jnp.where(lane == h, do, jnp.zeros_like(do))
    prod = do.astype(F32) * o_ref[piece].astype(F32)
    prod_hi = prod.astype(BF16)
    prod_lo = (prod - prod_hi.astype(F32)).astype(BF16)
    pick = (lax.broadcasted_iota(jnp.int32, (8, width), 1) // HEAD_DIM == lax.broadcasted_iota(jnp.int32, (8, width), 0)).astype(BF16)
    delta = dot(pick, prod_hi, 1, 1) + dot(pick, prod_lo, 1, 1)
    lse = lse_ref[piece]
    seg_q = seg_ref[0, pl.ds(piece, 1)].astype(F32)

    def run(count):
        @pl.when(cnt_ref[piece] == count)
        def _():
            places = [idx_ref[piece * pieces + t] for t in range(count)]
            qm, gm = qmt[...], gmt[...]
            later = dot(k_ref[places[0]], qm), dot(v_ref[places[0]], gm)
            out = [None] * heads
            for t in range(count):
                s, dp = later
                j = places[t]
                if t + 1 < count:
                    later = dot(k_ref[places[t + 1]], qm), dot(v_ref[places[t + 1]], gm)
                col = segk[j]
                same = jnp.concatenate([col] * (shard // 128), axis=1) == seg_q
                ps, dss = [], []
                for h in range(heads):
                    at = slice(h * HEAD_DIM, (h + 1) * HEAD_DIM)
                    qa = slice(h * shard, (h + 1) * shard)
                    p = jnp.exp2(jnp.where(same, s[:, qa] - lse[h : h + 1], NEG))
                    ds = (p * (dp[:, qa] - delta[h : h + 1])).astype(BF16)
                    ps.append(p.astype(BF16))
                    dss.append(ds)
                    part = dot(kt[j, at], ds)
                    out[h] = part if t == 0 else out[h] + part
                dv[j] += dot(jnp.concatenate(ps, axis=1), gst[...])
                dk[j] += dot(jnp.concatenate(dss, axis=1), qst[...])
            for h in range(heads):
                dqt[h * HEAD_DIM : (h + 1) * HEAD_DIM] = out[h]

    for count in range(1, pieces + 1):
        run(count)
    dq[piece] = turn(dqt[...].T * HEAD_DIM**-0.5, cos_ref[piece], -sin_ref[piece]).astype(BF16)


def attend_back(row, rows, cnt, idx, qkv, o, do, lse, seg, cos_tab, sin_tab, weight, held=(), deps=()):
    _, pieces, shard, width = qkv.shape
    model = weight.shape[1]
    heads = width // HEAD_DIM
    table = fixed((pieces, shard, 128))
    pairs = (pieces * shard) ** 2
    square, wide = (width, heads * shard), (pieces, shard, width)
    far = [part((1, shard, width), n) for n in range(2)]
    return call(
        attend_back_body, "attend_back", (cnt, idx), (1,),
        [(qkv, fixed(qkv.shape)), (o, fixed(o.shape)), (do[0], fixed((shard, width))), (do[1], fixed((shard, width)))]
        + [(do[2], far[0]), (do[3], fixed((shard, width))), (lse, fixed(lse.shape)), (seg, part((1, pieces, shard), row))]
        + [(cos_tab, table), (sin_tab, table), (weight, fixed(weight.shape))],
        [((rows, pieces, shard, 3 * width), BF16, part((1, pieces, shard, 3 * width), row))]
        + [((shard, model), BF16, fixed((shard, model)))] * pieces,
        [
            pltpu.VMEM((pieces, width, shard), BF16),
            pltpu.VMEM((pieces, shard, 128), F32),
            pltpu.VMEM(wide, F32),
            pltpu.VMEM(wide, F32),
            pltpu.VMEM(wide, BF16),
            pltpu.VMEM((width, shard), F32),
            pltpu.VMEM(square, BF16),
            pltpu.VMEM(square, BF16),
            pltpu.VMEM(square[::-1], BF16),
            pltpu.VMEM(square[::-1], BF16),
            pltpu.VMEM(wide, BF16),
        ],
        held=[(array, 0) for array in held], deps=deps,
        flops=40 * pairs * width, moved=16 * qkv.size, trans=pairs * heads,
    )


def middle_body(
    order_ref, a0, a1, a2, a3, w0, w1, w2, w3, stream_ref, bias_ref, gain_ref, shift_ref, mid_ref, low_ref, all_ref,
):
    shard, model = stream_ref.shape
    total = 0.0
    for n, (a, w) in enumerate(((a0, w0), (a1, w1), (a2, w2), (a3, w3))):
        values = a[...].reshape(shard, a.shape[-1])
        total = total + dot(values, w[...])
        all_ref[0, :, n * a.shape[-1] : (n + 1) * a.shape[-1]] = values
    mid = stream_ref[...] + (total + bias_ref[...])
    hat, _ = centre(mid)
    mid_ref[...] = mid
    low_ref[...] = (hat * gain_ref[...] + shift_ref[...]).astype(BF16)


def out_blocks(weight, parts):
    width = weight.shape[0] // parts

    def block(i):
        return pl.BlockSpec((width, weight.shape[1]), lambda g, o: (o[i], 0))

    return [(weight, block(i)) for i in range(parts)]


def middle_norm(row, rows, order, attended, weight, stream, bias, gain, shift, held=()):
    shard, model = stream.shape
    parts = len(attended)
    width = model // parts
    block, line = fixed((shard, model)), fixed((1, model))
    first = [part((1, shard, width), 0), fixed((shard, width)), part((1, shard, width), 0), fixed((shard, width))]
    return call(
        middle_body, "middle", (order,), (1,),
        list(zip(attended, first)) + out_blocks(weight, parts) + [(stream, block), (bias, line), (gain, line), (shift, line)],
        [
            (stream.shape, F32, block),
            (stream.shape, BF16, block),
            ((rows, shard, model), BF16, part((1, shard, model), row)),
        ],
        held=[(array, 2) for array in held], flops=2 * shard * model * model, moved=14 * stream.size,
    )


def cot_body(blk_ref, a_ref, b_ref, up_ref, down_ref, g_ref, up_out, down_out, both_ref):
    tokens = a_ref.shape[0]
    down = down_ref[...]

    @pl.when(pl.program_id(0) == 0)
    def _():
        both_ref[0:tokens] = a_ref[...]
        both_ref[tokens:] = b_ref[...]

    g_ref[0:tokens] = dot(a_ref[...], down, 1, 1).astype(BF16)
    g_ref[tokens:] = dot(b_ref[...], down, 1, 1).astype(BF16)
    up_out[...] = up_ref[...]
    down_out[...] = down


def cot_down(blk, own, other, up, down, picked, half):
    tokens, model = own.shape
    steps = half // BLOCK
    column = along((2 * tokens, BLOCK), 1)
    if picked:
        up_at, down_at = along((model, BLOCK), 1), along((BLOCK, model))
    else:
        up_at = pl.BlockSpec((model, BLOCK), lambda g, b: (0, b[g]))
        down_at = pl.BlockSpec((BLOCK, model), lambda g, b: (b[g], 0))
    return call(
        cot_body, "cot_down", (blk,), (steps,),
        [(own, fixed(own.shape)), (other, fixed(own.shape)), (up, up_at), (down, down_at)],
        [
            ((2 * tokens, half), BF16, column),
            ((model, half), BF16, along((model, BLOCK), 1)),
            ((half, model), BF16, along((BLOCK, model))),
            ((2 * tokens, model), BF16, fixed((2 * tokens, model))),
        ],
        flops=4 * tokens * model * half, moved=2 * (2 * tokens * (model + half) + 4 * model * half),
    )


def hidden_body(*refs):
    pieces, (g_ref, up_ref, bias_ref, act_ref, grad_ref, sum_ref, both_ref) = refs[:-7], refs[-7:]
    chunk = pieces[0].shape[0]

    @pl.when(pl.program_id(0) == 0)
    def _():
        for n, ref in enumerate(pieces):
            both_ref[n * chunk : (n + 1) * chunk] = ref[...]

    up, bias = up_ref[...], bias_ref[...]
    total = 0.0
    later = dot(pieces[0][...], up)
    for n in range(len(pieces)):
        at = slice(n * chunk, (n + 1) * chunk)
        v = later + bias
        if n + 1 < len(pieces):
            later = dot(pieces[n + 1][...], up)
        square = v * v
        tanh = jnp.tanh(v * (GELU_A + GELU_B * square))
        gate = 0.5 + 0.5 * tanh
        act = v * gate
        slope = gate + act * ((1.0 - tanh) * (GELU_A + 3.0 * GELU_B * square))
        grad = (slope * g_ref[at].astype(F32)).astype(BF16)
        act_ref[at] = act.astype(BF16)
        grad_ref[at] = grad
        total = total + jnp.sum(grad.astype(F32), axis=0, keepdims=True)
    sum_ref[...] = total


def hidden_units(pieces, grads, up, bias):
    chunk, model = pieces[0].shape
    tokens, half = grads.shape
    column, line = along((tokens, BLOCK), 1), along((1, BLOCK), 1)
    return call(
        hidden_body, "hidden", (), (half // BLOCK,),
        [(piece, fixed((chunk, model))) for piece in pieces]
        + [(grads, column), (up, along((model, BLOCK), 1)), (bias, line)],
        [
            (grads.shape, BF16, column),
            (grads.shape, BF16, column),
            ((1, half), F32, line),
            ((tokens, model), BF16, fixed((tokens, model))),
        ],
        flops=2 * tokens * model * half, moved=2 * (tokens * (2 * model + 3 * half) + model * half), trans=tokens * half,
    )


def middle_back_body(
    order_ref, part_ref, sent_ref, mid_ref, cot_ref, gain_ref, w0, w1, w2, w3,
    grad_ref, low_ref, att0_ref, att1_ref, far_ref, sums_ref,
):
    grad = part_ref[...].astype(F32) + sent_ref[...].astype(F32)
    hat, inverse = centre(mid_ref[...])
    cot = cot_ref[0].astype(F32)
    total = cot + norm_back(grad, gain_ref[...], hat, inverse)
    low = total.astype(BF16)
    grad_ref[...] = total
    low_ref[0] = low
    far_ref[0] = dot(low, w2[...], 1, 1).astype(BF16)
    far_ref[1] = dot(low, w3[...], 1, 1).astype(BF16)
    att1_ref[...] = dot(low, w1[...], 1, 1).astype(BF16)
    att0_ref[...] = dot(low, w0[...], 1, 1).astype(BF16)
    sums_ref[0:1] = jnp.sum(grad * hat, axis=0, keepdims=True)
    sums_ref[1:2] = jnp.sum(grad, axis=0, keepdims=True)
    sums_ref[2:3] = jnp.sum(low.astype(F32), axis=0, keepdims=True)
    sums_ref[3:4] = jnp.sum(cot, axis=0, keepdims=True)


def middle_back(row, rows, order, own, sent, mid, cot, gain, weight, parts, held=(), deps=()):
    shard, model = mid.shape
    width = model // parts
    block, place = fixed((shard, model)), part((1, shard, model), row)
    flat = pl.BlockSpec((shard, model), lambda *_: (row, 0))
    return call(
        middle_back_body, "middle_back", (order,), (1,),
        [(own, flat), (sent, flat), (mid, block), (cot, place), (gain, fixed((1, model)))] + out_blocks(weight, parts),
        [
            (mid.shape, F32, block),
            ((rows, shard, model), BF16, place),
            ((shard, width), BF16, fixed((shard, width))),
            ((shard, width), BF16, fixed((shard, width))),
            ((2, shard, width), BF16, fixed((2, shard, width))),
            ((8, model), F32, fixed((8, model))),
        ],
        held=[(array, 1) for array in held], deps=deps, flops=2 * shard * model * model, moved=18 * mid.size,
    )


def norm1_back_body(part_ref, near_ref, far_ref, stream_ref, mid_ref, gain_ref, seg_ref, in_ref, shift_ref, sums_ref):
    grad = part_ref[...].astype(F32) + near_ref[...].astype(F32) + far_ref[...].astype(F32)
    hat, inverse = centre(stream_ref[...])
    total = mid_ref[...] + norm_back(grad, gain_ref[...], hat, inverse)
    in_ref[0] = total.astype(BF16)
    slots = lax.broadcasted_iota(jnp.int32, (SEGS, seg_ref.shape[-1]), 0) == seg_ref[0]
    onehot = slots.astype(F32).astype(BF16)
    shift_ref[...] = dot(jnp.concatenate([onehot, onehot], axis=1), split_low(total))
    sums_ref[0:1] = jnp.sum(grad * hat, axis=0, keepdims=True)
    sums_ref[1:2] = jnp.sum(grad, axis=0, keepdims=True)


def norm1_back(row, rows, own, near, far, stream, mid, gain, seg, held=(), deps=()):
    shard, model = stream.shape
    block = fixed((shard, model))
    return call(
        norm1_back_body, "norm1_back", (), (1,),
        [(own, block), (near, block), (far, block), (stream, block), (mid, block), (gain, fixed((1, model)))]
        + [(seg, part((1, 1, shard), row))],
        [
            ((rows, shard, model), BF16, part((1, shard, model), row)),
            ((SEGS, model), F32, fixed((SEGS, model))),
            ((8, model), F32, fixed((8, model))),
        ],
        held=[(array, 0) for array in held], deps=deps, moved=16 * stream.size,
    )


def exchange(own, one, far):
    far = swap(far, "y")
    return [own, swap(one, "c"), far, swap(far[1], "c")]


def after(value, *others):
    return lax.optimization_barrier((value,) + others)[0]


def cut(values, index, size, axis):
    return lax.dynamic_slice_in_dim(values, index * size, size, axis)


def add_low(kept, sent):
    return (kept.astype(F32) + sent.astype(F32)).astype(BF16)


def ordered(at, own, other, axis):
    return jnp.where(at == 0, jnp.concatenate([own, other], axis), jnp.concatenate([other, own], axis))


def local(
    inputs, segment_ids, doc_times, time_weight, time_bias, norm1_gain, norm1_bias, qkv_weight, qkv_bias,
    out_weight, out_bias, norm2_gain, norm2_bias, up_weight, up_bias, down_weight, down_bias, cotangent,
    *, dp,
):
    rows, shard, model = inputs.shape
    parts = 4
    tokens = rows * shard
    hidden_width = up_weight.shape[1]
    width = model // parts
    depth = dp // 2
    half = hidden_width // 2
    piece = half // dp
    z_at, x_at, y_at, c_at = (lax.axis_index(name) for name in ("z", "x", "y", "c"))
    me = 2 * y_at + c_at
    order = [me ^ i for i in range(parts)]
    order_list = jnp.stack(order).astype(jnp.int32)
    me_list = order_list[:1]

    def line(vector):
        return vector.astype(F32)[None]

    seg = segment_ids[:, None, :]
    features = time_features(doc_times.reshape(rows * SEGS), jnp.arange(TEMB), TEMB // 2)
    time_shift = dot(features, time_weight).reshape(rows, SEGS, model) + time_bias.astype(F32)
    stream, own1, one1, two1 = [], [], [], []
    for r in range(rows):
        values, low = norm1(r, inputs, seg, time_shift, line(norm1_gain), line(norm1_bias))
        stream.append(values)
        own1.append(low)
        two1.append(swap(low, "y"))
        one1.append(swap(low, "c"))

    seg_two = swap(segment_ids, "y")
    segs = jnp.stack([segment_ids, swap(segment_ids, "c"), seg_two, swap(seg_two, "c")], axis=1)
    low_id, high_id = segs.min(axis=2), segs.max(axis=2)
    act = (low_id[:, :, None] <= high_id[:, None, :]) & (low_id[:, None, :] <= high_id[:, :, None])
    places = jnp.arange(parts, dtype=jnp.int32)
    rank = jnp.cumsum(act.astype(jnp.int32), axis=2) - 1
    chosen = act[..., None] & (rank[..., None] == places)
    idx = jnp.sum(jnp.where(chosen, places[:, None], 0), axis=2).astype(jnp.int32).reshape(rows, -1)
    cnt = jnp.sum(act.astype(jnp.int32), axis=2)
    positions = jnp.stack([o * shard + jnp.arange(shard, dtype=jnp.int32) for o in order])
    cos_tab, sin_tab = rotary_tables(positions, HEAD_DIM)

    cot = cotangent.reshape(tokens, model)
    cot_other = swap(cot, "c")
    turned = jnp.stack([1 - x_at, x_at])
    if piece % BLOCK == 0:
        blk = ((jnp.arange(depth)[None, :] * 2 + turned[:, None]) * 2 + c_at) * (piece // BLOCK)
        blk = (blk[..., None] + jnp.arange(piece // BLOCK)).reshape(-1).astype(jnp.int32)
        up_from, down_from = up_weight, down_weight
    else:
        blk = jnp.zeros((half // BLOCK,), jnp.int32)
        up_from = up_weight.reshape(model, depth, 2, 2, piece)
        up_from = lax.dynamic_index_in_dim(up_from, c_at, 3, keepdims=False)
        up_from = jnp.where(x_at == 1, up_from, up_from[:, :, ::-1]).transpose(0, 2, 1, 3).reshape(model, half)
        down_from = down_weight.reshape(depth, 2, 2, piece, model)
        down_from = lax.dynamic_index_in_dim(down_from, c_at, 2, keepdims=False)
        down_from = jnp.where(x_at == 1, down_from, down_from[:, ::-1]).transpose(1, 0, 2, 3).reshape(half, model)
    grad_act, up_own, down_own, cot_both = cot_down(
        blk, cot, cot_other, up_from, down_from, piece % BLOCK != 0, half
    )
    up_bias_own = lax.dynamic_index_in_dim(up_bias.reshape(depth, 2, 2, piece), c_at, 2, keepdims=False)
    up_bias_own = jnp.where(x_at == 1, up_bias_own, up_bias_own[:, ::-1]).transpose(1, 0, 2).reshape(half)

    bias_line = qkv_bias.reshape(1, 3 * model)
    qkv, o, lse, attended, middle, normed2, normed2_other = [], [], [], [], [], [], []
    normed1_all, attended_all = (), ()
    for r in range(rows):
        deps = (grad_act,) if r == 0 else ()
        taken = (own1[r], one1[r], two1[r], swap(two1[r], "c"))
        found, normed1_all, qkv_own = project_qkv(
            r, rows, me_list, taken, qkv_weight, bias_line, cos_tab, sin_tab, normed1_all, deps
        )
        normed1_all = (normed1_all,)
        qkv.append(found)
        out, out_one, out_far, scale = attend(r, cnt[r], idx[r], found, segs)
        o.append(out)
        lse.append(scale)
        attended.append(exchange(out, out_one, out_far))
    for r in range(rows):
        values, low, attended_all = middle_norm(
            r, rows, order_list, attended[r], out_weight, stream[r], line(out_bias), line(norm2_gain), line(norm2_bias),
            attended_all,
        )
        attended_all = (attended_all,)
        middle.append(values)
        normed2.append(low)
        normed2_other.append(swap(low, "c"))

    active, grad_hidden, up_b, normed2_both = hidden_units(
        normed2 + normed2_other, grad_act, up_own, line(up_bias_own)
    )
    down_out = dot(active[:, : half // 2], cot_both, 0, 0).astype(BF16)
    down_sent = swap(down_out, "x")
    up_grad = dot(normed2_both, grad_hidden, 0, 0).astype(BF16)
    up_z = lax.psum_scatter(up_grad, "z", scatter_dimension=0, tiled=True)
    grad_hidden = after(grad_hidden, down_out, up_grad)
    part2_sent = swap(dot(grad_hidden[tokens:], up_own, 1, 1).astype(BF16), "c")
    part2 = dot(grad_hidden[:tokens], up_own, 1, 1).astype(BF16)
    grad_middle, grad_o, sums2 = [], [], 0.0
    grad_middle_low = ()
    for r in range(rows):
        values, grad_middle_low, att0, att1, far, found = middle_back(
            r, rows, order_list, part2, part2_sent, middle[r], cotangent, line(norm2_gain), out_weight, parts,
            grad_middle_low,
        )
        grad_middle_low = (grad_middle_low,)
        grad_middle.append(values)
        grad_o.append(exchange(att0, att1, far))
        sums2 = sums2 + found[:4]
    (grad_middle_low,) = grad_middle_low

    active_late = after(active, grad_middle_low)
    down_kept = dot(active_late[:, half // 2 :], cot_both, 0, 0).astype(BF16)
    feed_sent = swap(dot(active_late[tokens:], down_own).astype(BF16), "c")
    feed = dot(active_late[:tokens], down_own) + feed_sent.astype(F32) + line(down_bias)
    output = (jnp.stack(middle) + feed.reshape(rows, shard, model)).astype(BF16)
    out_grad = dot(
        attended_all[0].reshape(tokens, model), grad_middle_low.reshape(tokens, model), 0, 0
    ).astype(BF16)

    grad_qkv, back = (), []
    for r in range(rows):
        deps = (down_kept, output, out_grad) if r == 0 else ()
        grad_qkv, own, one, two, three = attend_back(
            r, rows, cnt[r], idx[r], qkv[r], o[r], grad_o[r], lse[r], segs, cos_tab, sin_tab, qkv_own, grad_qkv, deps
        )
        grad_qkv = (grad_qkv,)
        back.append((own, swap(one, "c"), swap(add_low(two, swap(three, "c")), "y")))
    grad_qkv = grad_qkv[0].reshape(parts * tokens, 3 * width)
    qkv_grad = dot(normed1_all[0].reshape(parts * tokens, model), grad_qkv, 0, 0).astype(BF16)
    qkv_b = jnp.sum(grad_qkv.astype(F32), axis=0)
    input_grad, grad_shift, sums1 = (), [], 0.0
    for r in range(rows):
        input_grad, found, sums = norm1_back(
            r, rows, *back[r], stream[r], grad_middle[r], line(norm1_gain), seg, input_grad
        )
        input_grad = (input_grad,)
        grad_shift.append(found)
        sums1 = sums1 + sums[:2]
    (input_grad,) = input_grad

    down_x = add_low(down_kept, down_sent)
    down_y = add_low(cut(down_x, y_at, model // 2, 1), swap(cut(down_x, 1 - y_at, model // 2, 1), "y"))
    down_z = lax.psum_scatter(down_y, "z", scatter_dimension=0, tiled=True)
    up_rows = model // dp
    up_sent = swap(cut(up_z, 1 - x_at, up_rows, 0), "x")
    up_sent = jnp.concatenate([up_sent[:, half // 2 :], up_sent[:, : half // 2]], axis=1)
    up_x = add_low(cut(up_z, x_at, up_rows, 0), up_sent)
    up_y = add_low(cut(up_x, y_at, half // 2, 1), swap(cut(up_x, 1 - y_at, half // 2, 1), "y"))
    out_grad = jnp.concatenate([cut(out_grad, o_at, width, 0) for o_at in order], axis=0)
    out_c = add_low(cut(out_grad, c_at, model // 2, 1), swap(cut(out_grad, 1 - c_at, model // 2, 1), "c"))
    out_y = add_low(cut(out_c, y_at, width, 1), swap(cut(out_c, 1 - y_at, width, 1), "y"))
    late = jnp.concatenate([qkv_grad, out_y], axis=1).reshape(depth, 2 * up_rows, model)
    late_x = add_low(cut(late, x_at, up_rows, 1), swap(cut(late, 1 - x_at, up_rows, 1), "x"))
    late_z = lax.psum_scatter(late_x, "z", scatter_dimension=0, tiled=False)

    down_done = ordered(y_at, down_z, swap(down_z, "y"), 1)
    down_done = ordered(c_at, down_done, swap(down_done, "c"), 0).astype(F32)
    up_done = ordered(y_at, up_y, swap(up_y, "y"), 1)
    up_done = ordered(c_at, up_done[None], swap(up_done, "c")[None], 0).reshape(2, up_rows, 2, depth, piece)
    up_done = jnp.where(x_at == 1, up_done, up_done[:, :, ::-1]).transpose(1, 3, 2, 0, 4)
    up_done = up_done.reshape(up_rows, hidden_width).astype(F32)
    late_done = ordered(c_at, late_z[None], swap(late_z, "c")[None], 0)
    late_done = ordered(y_at, late_done[None], swap(late_done, "y")[None], 0).reshape(parts, up_rows, model)
    qkv_done = late_done[:, :, : 3 * width].reshape(parts, up_rows, 3, width).transpose(1, 2, 0, 3)
    qkv_done = qkv_done.reshape(up_rows, 3 * model).astype(F32)
    out_done = late_done[:, :, 3 * width :].reshape(2, 2, up_rows, width).transpose(2, 1, 0, 3)
    out_done = out_done.reshape(up_rows, model).astype(F32)

    up_b = up_b.reshape(2, depth, 1, piece)
    up_b = jnp.where(x_at == 1, up_b, up_b[::-1]).transpose(1, 0, 2, 3)
    up_b = jnp.where(jnp.arange(2)[:, None] == c_at, up_b, 0.0).reshape(-1, model)
    qkv_b = jnp.where(jnp.arange(parts)[:, None] == me, qkv_b.reshape(3, 1, width), 0.0).reshape(3, model)
    times = doc_times.reshape(1, rows * SEGS)
    times = jnp.concatenate([times // 32, times % 32], axis=1).astype(F32)
    times = jnp.pad(times, ((0, 0), (0, model - times.shape[1])))
    small = jnp.concatenate(grad_shift + [sums1, sums2, qkv_b, up_b, times], axis=0)
    small = add_low(small, swap(small.astype(BF16), "c"))
    small = add_low(small, swap(small, "y"))
    small = ordered(x_at, small[None], swap(small, "x")[None], 0)
    if depth == 4:
        others = [lax.ppermute(small, "z", [(i, i ^ n) for i in range(depth)]) for n in range(1, depth)]
        small = jnp.stack([small] + others)
        small = jnp.stack([lax.dynamic_index_in_dim(small, z_at ^ n, 0, keepdims=False) for n in range(depth)])
    else:
        small = lax.all_gather(small, "z")
    small = small.reshape(dp, small.shape[2], model)
    all_times = small[:, -1, : 2 * rows * SEGS].astype(F32) * 0.25
    all_times = all_times[:, : rows * SEGS] * 32.0 + all_times[:, rows * SEGS :]
    shifts = small[:, : rows * SEGS].reshape(dp * rows * SEGS, model)
    columns = (2 * z_at + x_at) * (TEMB // dp) + jnp.arange(TEMB // dp)
    wanted = time_features(all_times.reshape(-1), columns, TEMB // 2)
    time_w_done = dot(wanted, shifts, 0, 0)
    sums = jnp.sum(small[:, rows * SEGS :].astype(F32), axis=0)
    dp_at = 2 * z_at + x_at

    def share(vector):
        return cut(vector.reshape(-1), dp_at, vector.size // dp, 0)

    time_b_done = jnp.sum(cut(shifts, dp_at, up_rows, 1).astype(F32), axis=0)
    return (
        output, input_grad, time_w_done, time_b_done, share(sums[0]), share(sums[1]), qkv_done, share(sums[6:9]),
        out_done, share(sums[4]), share(sums[2]), share(sums[3]), up_done, share(sums[9:-1]), down_done, share(sums[5]),
    )


def solution(mesh):
    dp, seq = mesh.shape["dp"], mesh.shape["seq"]
    fine = Mesh(mesh.devices.reshape(dp // 2, 2, seq // 2, 2), ("z", "x", "y", "c"))
    rows, seqs = ("z", "x"), ("y", "c")
    placed = (P(rows, seqs, None), P(rows, seqs), P(rows, None)) + (P(),) * 14 + (P(rows, seqs, None),)
    vec, mat = P(rows), P(rows, None)
    return jax.shard_map(
        functools.partial(local, dp=dp),
        mesh=fine,
        in_specs=placed,
        out_specs=(
            P(rows, seqs, None), P(rows, seqs, None), mat, vec, vec, vec, mat, vec, mat, vec, vec, vec, mat, vec, mat, vec,
        ),
        check_vma=False,
    )
```

time: 543 us -> 510 us (0.939)
  blocking collectives: 94.2 us -> 0 us
  Pallas kernels: 144 us -> 191 us
  starting transfers between devices: 21.8 us -> 48.2 us
  matrix products: 67.7 us -> 60 us
  waiting for transfers between devices: 111 us -> 104 us
    all_gather x2 -> x0, blocking collectives: 94.2 us -> none  [the longest x1 60.3 us: local(): all_times = lax.all_gather(doc_times.reshape(rows * SEGS), ('z', 'x'))]
    pallas_call x8 -> x23, Pallas kernels: 129 us -> 191 us  [call(): pl.pallas_call(kernel, grid_spec=pltpu.PrefetchScalarGridSpec(num_scalar_...]
    ppermute x34 -> x61, starting transfers between devices: 21 us -> 43.4 us  [swap(): return lax.ppermute(value, axis, [(0, 1), (1, 0)])]
    ppermute x34 -> x61, waiting for transfers between devices: 111 us -> 91.4 us  [swap(): return lax.ppermute(value, axis, [(0, 1), (1, 0)])]
    pallas_call x2 -> x0, Pallas kernels: 15.1 us -> none  [project_qkv(): pl.pallas_call(qkv_body, grid_spec=pltpu.PrefetchScalarGridSpec(num_scala...]
    slice x11 -> x1, local copies, waits for them, and re-layouts: 11 us -> 0.01 us  [local(): out, out_one, out_far, scale = attend(r, cnt[r], idx[r], found, segs)]
    dot_general x13 -> x11, matrix products: 67.7 us -> 60 us  [dot(): lax.dot_general(left_op, right_op, (((left_dim,), (right_dim,)), ((), ())...]
    ppermute x0 -> x3, waiting for transfers between devices: none -> 7.31 us  [local(): lax.ppermute(small, 'z', [(i, i ^ n) for i in range(depth)])]
  transfers between devices with their start and end apart: 37 -> 67, of which waited for: 11 -> 23; matrix products, arithmetic and copies ran while one was open for 21% -> 19% of each run, Pallas kernels for 15% -> 30%
where the time goes in v3:
time: 510 us; the launch traced here: 501 us
  Pallas kernels  191 us (37%)
  waiting for transfers between devices  104 us (20%)
  matrix products  60 us (12%)
  starting transfers between devices  48.2 us (9%)
  local copies, waits for them, and re-layouts  41.6 us (8%)
  other arithmetic  40.5 us (8%)
  between operations  15.3 us (3%)
    pallas_call x23, Pallas kernels, call(): pl.pallas_call(kernel, grid_spec=pltpu.PrefetchScalarGridSpec(num_scalar_...  191 us
    ppermute x61, waiting for transfers between devices, swap(): return lax.ppermute(value, axis, [(0, 1), (1, 0)])  91.4 us
    dot_general x11, matrix products, dot(): lax.dot_general(left_op, right_op, (((left_dim,), (right_dim,)), ((), ())...  60 us
    ppermute x61, starting transfers between devices, swap(): return lax.ppermute(value, axis, [(0, 1), (1, 0)])  43.4 us
    convert_element_type x12, other arithmetic, add_low(): return (kept.astype(F32) + sent.astype(F32)).astype(BF16)  13 us
    unnamed x151, local copies, waits for them, and re-layouts  12.4 us
  transfers between devices with their start and end apart: 67, of which 23 were waited for; matrix products, arithmetic and copies ran while one was open for 19% of the time, Pallas kernels for 30%

profile of v3, /device:TPU:0, one launch (start us, length us, event | category | flops | bytes accessed | tf_op | source)
XLA Modules:
  0.0 501.0 jit_solution(17354280899568525572)
XLA Ops:
  23.1 8.2 %collective-permute-done.1 = s32[3,256]{1,0:T(4,128)S(1)} collective-permute-done((s32[3,256]{1,0:T(4,128)}, s32[3,256]{1,0:T(4,128)S(1)}, u32[]{:S(2)}, u32[]{:S(2)}) %collective-permute-start.1) | collective-permute-done | bytes 3104 | tf_op jit(solution)/shard_map/ppermute | solution.py:27
  45.5 8.2 %collective-permute-done.11.refs_3_ = bf16[256,1024]{1,0:T(8,128)(2,1)S(1)} collective-permute-done((bf16[256,1024]{1,0:T(8,128)(2,1)}, bf16[256,1024]{1,0:T(8,128)(2,1)S(1)}, u32[]{:S(2)}, u32[]{:S(2)}) %collective-permute-start.11) | collective-permute-done | bytes 524320 | tf_op jit(solution)/shard_map/ppermute | solution.py:27
  53.8 10.9 %collective-permute-done.17.refs_3_ = bf16[256,1024]{1,0:T(8,128)(2,1)S(1)} collective-permute-done((bf16[256,1024]{1,0:T(8,128)(2,1)}, bf16[256,1024]{1,0:T(8,128)(2,1)S(1)}, u32[]{:S(2)}, u32[]{:S(2)}) %collective-permute-start.17) | collective-permute-done | bytes 524320 | tf_op jit(solution)/shard_map/ppermute | solution.py:27
  65.1 15.8 %cot_down.1 = (bf16[1536,2048]{1,0:T(8,128)(2,1)}, bf16[1024,2048]{1,0:T(8,128)(2,1)}, bf16[2048,1024]{1,0:T(8,128)(2,1)}, bf16[1536,1024]{1,0:T(8,128)(2,1)}) custom-call(s32[8]{0:T(128)} %add.326.refs_0_, bf16[768,1024]{1,0:T(8,128)(2,1)} %bitcast.127, bf16[768,1024]{1,0:T(8,128)(2,1)} %collective-permute-done.6.refs_2_, bf16[1024,4096]{1,0:T(8,128)(2,1)} %refs_3_.1, ...), custom_call_target="tpu_custom_call" | custom-call | flops 6442450944 | bytes 26214400 | tf_op jit(solution)/shard_map/cot_down/pallas_call | solution.py:94
  81.0 7.4 %qkv.3 = (bf16[3,4,256,256]{3,2,1,0:T(8,128)(2,1)}, bf16[3,4,256,1024]{3,2,1,0:T(8,128)(2,1)}, bf16[768,1024]{1,0:T(8,128)(2,1)}) custom-call(s32[1]{0:T(128)} %bitcast.refs_0_, bf16[256,1024]{1,0:T(8,128)(2,1)} %get-tuple-element.102.refs_1_, bf16[256,1024]{1,0:T(8,128)(2,1)} %copy-done.18, bf16[256,1024]{1,0:T(8,128)(2,1)} %copy-done.17, ...), custom_call_target="tpu_custom_call" | custom-call | flops 1610612736 | bytes 5767168 | tf_op jit(solution)/shard_map/qkv/pallas_call | solution.py:94
  89.1 7.3 %qkv.4 = (bf16[3,4,256,256]{3,2,1,0:T(8,128)(2,1)}, bf16[3,4,256,1024]{3,2,1,0:T(8,128)(2,1)}, bf16[768,1024]{1,0:T(8,128)(2,1)}) custom-call(s32[1]{0:T(128)} %bitcast.refs_0_, bf16[256,1024]{1,0:T(8,128)(2,1)} %get-tuple-element.110.refs_1_, bf16[256,1024]{1,0:T(8,128)(2,1)} %copy-done.27, ...), custom_call_target="tpu_custom_call", output_to_operand_aliasing={{1}: (9, {})} | custom-call | flops 1610612736 | bytes 5767168 | tf_op jit(solution)/shard_map/qkv/pallas_call | solution.py:94
  97.5 7.4 %qkv.5 = (bf16[3,4,256,256]{3,2,1,0:T(8,128)(2,1)}, bf16[3,4,256,1024]{3,2,1,0:T(8,128)(2,1)}, bf16[768,1024]{1,0:T(8,128)(2,1)}) custom-call(s32[1]{0:T(128)} %bitcast.refs_0_, bf16[256,1024]{1,0:T(8,128)(2,1)} %get-tuple-element.119.refs_1_, bf16[256,1024]{1,0:T(8,128)(2,1)} %copy-done.25, ...), custom_call_target="tpu_custom_call", output_to_operand_aliasing={{1}: (9, {})} | custom-call | flops 1610612736 | bytes 5767168 | tf_op jit(solution)/shard_map/qkv/pallas_call | solution.py:94
  104.9 8.5 %attend.5 = (bf16[4,256,256]{2,1,0:T(8,128)(2,1)}, bf16[256,256]{1,0:T(8,128)(2,1)}, bf16[2,256,256]{2,1,0:T(8,128)(2,1)}, f32[4,8,256]{2,1,0:T(8,128)}) custom-call(s32[4]{0:T(128)} %get-tuple-element.247.refs_0_, s32[16]{0:T(128)} %squeeze.65.refs_1_, bf16[3,4,256,256]{3,2,1,0:T(8,128)(2,1)} %get-tuple-element.121.refs_2_, ...), custom_call_target="tpu_custom_call" | custom-call | flops 4294967296 | bytes 1572864 | tf_op jit(solution)/shard_map/attend/pallas_call | solution.py:94
  115.1 8.8 %attend.3 = (bf16[4,256,256]{2,1,0:T(8,128)(2,1)}, bf16[256,256]{1,0:T(8,128)(2,1)}, bf16[2,256,256]{2,1,0:T(8,128)(2,1)}, f32[4,8,256]{2,1,0:T(8,128)}) custom-call(s32[4]{0:T(128)} %get-tuple-element.249.refs_0_, s32[16]{0:T(128)} %squeeze.59.refs_1_, bf16[3,4,256,256]{3,2,1,0:T(8,128)(2,1)} %get-tuple-element.104.refs_2_, ...), custom_call_target="tpu_custom_call" | custom-call | flops 4294967296 | bytes 1572864 | tf_op jit(solution)/shard_map/attend/pallas_call | solution.py:94
  124.2 11.0 %attend.4 = (bf16[4,256,256]{2,1,0:T(8,128)(2,1)}, bf16[256,256]{1,0:T(8,128)(2,1)}, bf16[2,256,256]{2,1,0:T(8,128)(2,1)}, f32[4,8,256]{2,1,0:T(8,128)}) custom-call(s32[4]{0:T(128)} %get-tuple-element.248.refs_0_, s32[16]{0:T(128)} %squeeze.62.refs_1_, bf16[3,4,256,256]{3,2,1,0:T(8,128)(2,1)} %get-tuple-element.112.refs_2_, ...), custom_call_target="tpu_custom_call" | custom-call | flops 4294967296 | bytes 1572864 | tf_op jit(solution)/shard_map/attend/pallas_call | solution.py:94
  137.6 6.2 %collective-permute-done.14.refs_3_ = bf16[2,256,256]{2,1,0:T(8,128)(2,1)S(1)} collective-permute-done((bf16[2,256,256]{2,1,0:T(8,128)(2,1)}, bf16[2,256,256]{2,1,0:T(8,128)(2,1)S(1)}, u32[]{:S(2)}, u32[]{:S(2)}) %collective-permute-start.14) | collective-permute-done | bytes 262176 | tf_op jit(solution)/shard_map/ppermute | solution.py:27
  167.6 19.9 %hidden.1 = (bf16[1536,2048]{1,0:T(8,128)(2,1)}, bf16[1536,2048]{1,0:T(8,128)(2,1)}, f32[1,2048]{1,0:T(1,128)}, bf16[1536,1024]{1,0:T(8,128)(2,1)}) custom-call(bf16[256,1024]{1,0:T(8,128)(2,1)} %get-tuple-element.128.refs_0_, bf16[256,1024]{1,0:T(8,128)(2,1)} %get-tuple-element.129.refs_1_, bf16[256,1024]{1,0:T(8,128)(2,1)} %get-tuple-element.130.refs_2_, ...), custom_call_target="tpu_custom_call" | custom-call | flops 6442450944 | bytes 29360128 | tf_op jit(solution)/shard_map/hidden/pallas_call | solution.py:94
  187.5 11.3 %convolution_convert_fusion = bf16[1024,2048]{1,0:T(8,128)(2,1)} fusion(bf16[1536,1024]{1,0:T(8,128)(2,1)} %get-tuple-element.135, bf16[1536,2048]{1,0:T(8,128)(2,1)} %get-tuple-element.136), kind=kOutput, calls=%fused_computation.3 | convolution fusion | flops 6444548096 | bytes 13631488 | tf_op jit(solution)/shard_map/dot_general | solution.py:48
  198.8 7.8 %fusion.13 = bf16[1024,1024]{1,0:T(8,128)(2,1)} fusion(bf16[1536,1024]{1,0:T(8,128)(2,1)} %get-tuple-element.134, bf16[1536,2048]{1,0:T(8,128)(2,1)} %get-tuple-element.140), kind=kOutput, calls=%fused_computation.26 | convolution fusion | flops 3222274048 | bytes 8388608 | tf_op jit(solution)/shard_map/dot_general | solution.py:48
  216.4 7.7 %fusion.19.refs_1_ = bf16[768,1024]{1,0:T(8,128)(2,1)} fusion(bf16[1024,2048]{1,0:T(8,128)(2,1)} %get-tuple-element.131.refs_7_, bf16[1536,2048]{1,0:T(8,128)(2,1)} %get-tuple-element.136), kind=kOutput, calls=%fused_computation.28 | convolution fusion | flops 3222011904 | bytes 8912896 | tf_op jit(solution)/shard_map/dot_general | solution.py:48
  245.1 6.1 %fusion.25 = bf16[768,1024]{1,0:T(8,128)(2,1)S(1)} fusion(bf16[2048,1024]{1,0:T(8,128)(2,1)S(1)} %copy-done.66, bf16[1536,2048]{1,0:T(8,128)(2,1)} %get-tuple-element.140), kind=kOutput, calls=%fused_computation.30 | convolution fusion | flops 3222011904 | bytes 8912896 | tf_op jit(solution)/shard_map/dot_general | solution.py:48
  284.4 17.1 %attend_back.3 = (bf16[3,4,256,768]{3,2,1,0:T(8,128)(2,1)}, bf16[256,1024]{1,0:T(8,128)(2,1)}, bf16[256,1024]{1,0:T(8,128)(2,1)}, bf16[256,1024]{1,0:T(8,128)(2,1)}, bf16[256,1024]{1,0:T(8,128)(2,1)}) custom-call(s32[4]{0:T(128)} %get-tuple-element.249.refs_0_, s32[16]{0:T(128)} %squeeze.59.refs_1_, bf16[3,4,256,256]{3,2,1,0:T(8,128)(2,1)} %get-tuple-element.104.refs_2_, ...), custom_call_target="tpu_custom_call" | custom-call | flops 10737418240 | bytes 12582912 | tf_op jit(solution)/shard_map/attend_back/pallas_call | solution.py:94
  302.7 21.1 %attend_back.4 = (bf16[3,4,256,768]{3,2,1,0:T(8,128)(2,1)}, bf16[256,1024]{1,0:T(8,128)(2,1)}, bf16[256,1024]{1,0:T(8,128)(2,1)}, bf16[256,1024]{1,0:T(8,128)(2,1)}, bf16[256,1024]{1,0:T(8,128)(2,1)}) custom-call(s32[4]{0:T(128)} %get-tuple-element.248.refs_0_, s32[16]{0:T(128)} %squeeze.62.refs_1_, ...), custom_call_target="tpu_custom_call", output_to_operand_aliasing={{0}: (13, {})} | custom-call | flops 10737418240 | bytes 12582912 | tf_op jit(solution)/shard_map/attend_back/pallas_call | solution.py:94
  324.5 17.2 %attend_back.5 = (bf16[3,4,256,768]{3,2,1,0:T(8,128)(2,1)}, bf16[256,1024]{1,0:T(8,128)(2,1)}, bf16[256,1024]{1,0:T(8,128)(2,1)}, bf16[256,1024]{1,0:T(8,128)(2,1)}, bf16[256,1024]{1,0:T(8,128)(2,1)}) custom-call(s32[4]{0:T(128)} %get-tuple-element.247.refs_0_, s32[16]{0:T(128)} %squeeze.65.refs_1_, ...), custom_call_target="tpu_custom_call", output_to_operand_aliasing={{0}: (13, {})} | custom-call | flops 10737418240 | bytes 12582912 | tf_op jit(solution)/shard_map/attend_back/pallas_call | solution.py:94
  341.7 9.6 %bitcast_convert_fusion.1 = bf16[1024,768]{0,1:T(8,128)(2,1)} fusion(bf16[3,4,256,1024]{3,2,1,0:T(8,128)(2,1)} %get-tuple-element.187, bf16[3,4,256,768]{3,2,1,0:T(8,128)(2,1)} %get-tuple-element.185), kind=kOutput, calls=%fused_computation.6 | convolution fusion | flops 4832624640 | bytes 12582912 | tf_op jit(solution)/shard_map/dot_general | solution.py:48
  375.4 6.8 %collective-permute-done.44.refs_2_ = bf16[256,1024]{1,0:T(8,128)(2,1)S(1)} collective-permute-done((bf16[256,1024]{1,0:T(8,128)(2,1)S(1)}, bf16[256,1024]{1,0:T(8,128)(2,1)S(1)}, u32[]{:S(2)}, u32[]{:S(2)}) %collective-permute-start.44) | collective-permute-done | bytes 524320 | tf_op jit(solution)/shard_map/ppermute | solution.py:27
  397.3 6.6 %collective-permute-done.38.refs_2_ = bf16[256,1024]{1,0:T(8,128)(2,1)S(1)} collective-permute-done((bf16[256,1024]{1,0:T(8,128)(2,1)S(1)}, bf16[256,1024]{1,0:T(8,128)(2,1)S(1)}, u32[]{:S(2)}, u32[]{:S(2)}) %collective-permute-start.38) | collective-permute-done | bytes 524320 | tf_op jit(solution)/shard_map/ppermute | solution.py:27
  429.4 6.5 %collective-permute-done.49 = bf16[2,38,1024]{2,1,0:T(8,128)(2,1)S(1)} collective-permute-done((bf16[2,38,1024]{2,1,0:T(8,128)(2,1)S(1)}, bf16[2,38,1024]{2,1,0:T(8,128)(2,1)S(1)}, u32[]{:S(2)}, u32[]{:S(2)}) %collective-permute-start.49) | collective-permute-done | bytes 155680 | tf_op jit(solution)/shard_map/ppermute | solution.py:810
  466.4 9.5 %collective-permute-done.55 = bf16[2,128,1024]{2,1,0:T(8,128)(2,1)S(1)} collective-permute-done((bf16[2,128,1024]{2,1,0:T(8,128)(2,1)S(1)}, bf16[2,128,1024]{2,1,0:T(8,128)(2,1)S(1)}, u32[]{:S(2)}, u32[]{:S(2)}) %collective-permute-start.55) | collective-permute-done | bytes 524320 | tf_op jit(solution)/shard_map/ppermute | solution.py:27
  (442 shorter events, 238.8 us)
Async XLA Ops:
  7.2 431.2 %reduce-scatter.6.cloned.1.call-start = ((), (), s32[]{:S(2)}) async-start(), calls=%async_computation.4 | async-start | bytes 5242880 | tf_op jit(solution)/shard_map/reduce_scatter | solution.py:723
  16.1 28.9 %collective-permute-start.4 = (bf16[256,1024]{1,0:T(8,128)(2,1)}, bf16[256,1024]{1,0:T(8,128)(2,1)S(1)}, u32[]{:S(2)}, u32[]{:S(2)}) collective-permute-start(bf16[256,1024]{1,0:T(8,128)(2,1)} %get-tuple-element.102.refs_1_), channel_id=1, source_target_pairs={{0,2},{2,0},{1,3},{3,1},{4,6},{6,4},{5,7},{7,5},{8,10},{10,8},{9,1... | collective-permute-start | bytes 1572872 | tf_op jit(solution)/shard_map/ppermute | solution.py:27
  19.1 26.0 %collective-permute-start.3 = (bf16[256,1024]{1,0:T(8,128)(2,1)}, bf16[256,1024]{1,0:T(8,128)(2,1)S(1)}, u32[]{:S(2)}, u32[]{:S(2)}) collective-permute-start(bf16[256,1024]{1,0:T(8,128)(2,1)} %get-tuple-element.102.refs_1_), channel_id=1, source_target_pairs={{0,1},{1,0},{2,3},{3,2},{4,5},{5,4},{6,7},{7,6},{8,9},{9,8},{10,11... | collective-permute-start | bytes 1572872 | tf_op jit(solution)/shard_map/ppermute | solution.py:27
  19.6 45.0 %collective-permute-start.6 = (bf16[768,1024]{1,0:T(8,128)(2,1)}, bf16[768,1024]{1,0:T(8,128)(2,1)}, u32[]{:S(2)}, u32[]{:S(2)}) collective-permute-start(bf16[768,1024]{1,0:T(8,128)(2,1)} %bitcast.126), channel_id=1, source_target_pairs={{0,1},{1,0},{2,3},{3,2},{4,5},{5,4},{6,7},{7,6},{8,9},{9,8},{10,11... | collective-permute-start | bytes 4718600 | tf_op jit(solution)/shard_map/ppermute | solution.py:27
  40.6 24.0 %collective-permute-start.17 = (bf16[256,1024]{1,0:T(8,128)(2,1)}, bf16[256,1024]{1,0:T(8,128)(2,1)S(1)}, u32[]{:S(2)}, u32[]{:S(2)}) collective-permute-start(bf16[256,1024]{1,0:T(8,128)(2,1)} %get-tuple-element.119.refs_1_), channel_id=1, source_target_pairs={{0,2},{2,0},{1,3},{3,1},{4,6},{6,4},{5,7},{7,5},{8,10},{10,8},{9,1... | collective-permute-start | bytes 1572872 | tf_op jit(solution)/shard_map/ppermute | solution.py:27
  45.0 43.3 %collective-permute-start.10 = (bf16[256,1024]{1,0:T(8,128)(2,1)}, bf16[256,1024]{1,0:T(8,128)(2,1)S(1)}, u32[]{:S(2)}, u32[]{:S(2)}) collective-permute-start(bf16[256,1024]{1,0:T(8,128)(2,1)} %get-tuple-element.110.refs_1_), channel_id=1, source_target_pairs={{0,1},{1,0},{2,3},{3,2},{4,5},{5,4},{6,7},{7,6},{8,9},{9,8},{10,11... | collective-permute-start | bytes 1572872 | tf_op jit(solution)/shard_map/ppermute | solution.py:27
  45.0 51.5 %collective-permute-start.16 = (bf16[256,1024]{1,0:T(8,128)(2,1)}, bf16[256,1024]{1,0:T(8,128)(2,1)S(1)}, u32[]{:S(2)}, u32[]{:S(2)}) collective-permute-start(bf16[256,1024]{1,0:T(8,128)(2,1)} %get-tuple-element.119.refs_1_), channel_id=1, source_target_pairs={{0,1},{1,0},{2,3},{3,2},{4,5},{5,4},{6,7},{7,6},{8,9},{9,8},{10,11... | collective-permute-start | bytes 1572872 | tf_op jit(solution)/shard_map/ppermute | solution.py:27
  53.8 27.2 %collective-permute-start.5 = (bf16[256,1024]{1,0:T(8,128)(2,1)S(1)}, bf16[256,1024]{1,0:T(8,128)(2,1)}, u32[]{:S(2)}, u32[]{:S(2)}) collective-permute-start(bf16[256,1024]{1,0:T(8,128)(2,1)S(1)} %collective-permute-done.4.refs_3_), channel_id=1, source_target_pairs={{0,1},{1,0},{2,3},{3,2},{4,5},{5,4},{6,7},{7,6},{8,9},{9,8},{10,11... | collective-permute-start | bytes 1572872 | tf_op jit(solution)/shard_map/ppermute | solution.py:27
  64.6 31.9 %collective-permute-start.18 = (bf16[256,1024]{1,0:T(8,128)(2,1)S(1)}, bf16[256,1024]{1,0:T(8,128)(2,1)S(1)}, u32[]{:S(2)}, u32[]{:S(2)}) collective-permute-start(bf16[256,1024]{1,0:T(8,128)(2,1)S(1)} %collective-permute-done.17.refs_3_), channel_id=1, source_target_pairs={{0,1},{1,0},{2,3},{3,2},{4,5},{5,4},{6,7},{7,6},{8,9},{9,8},{10,11... | collective-permute-start | bytes 1572872 | tf_op jit(solution)/shard_map/ppermute | solution.py:27
  115.1 42.6 %collective-permute-start.19 = (bf16[256,256]{1,0:T(8,128)(2,1)}, bf16[256,256]{1,0:T(8,128)(2,1)S(1)}, u32[]{:S(2)}, u32[]{:S(2)}) collective-permute-start(bf16[256,256]{1,0:T(8,128)(2,1)} %get-tuple-element.123), channel_id=1, source_target_pairs={{0,1},{1,0},{2,3},{3,2},{4,5},{5,4},{6,7},{7,6},{8,9},{9,8},{10,11... | collective-permute-start | bytes 393224 | tf_op jit(solution)/shard_map/ppermute | solution.py:27
  211.6 59.7 %collective-permute-start.60 = (bf16[1024,1024]{1,0:T(8,128)(2,1)}, bf16[1024,1024]{1,0:T(8,128)(2,1)}, u32[]{:S(2)}, u32[]{:S(2)}) collective-permute-start(bf16[1024,1024]{1,0:T(8,128)(2,1)} %fusion.13), channel_id=1, source_target_pairs={{0,4},{4,0},{1,5},{5,1},{2,6},{6,2},{3,7},{7,3},{8,12},{12,8},{9,1... | collective-permute-start | bytes 6291464 | tf_op jit(solution)/shard_map/ppermute | solution.py:27
  214.9 227.0 %reduce-scatter.8.cloned.1.call-start = ((), (), s32[]{:S(2)}) async-start(), calls=%async_computation.5 | async-start | bytes 1310720 | tf_op jit(solution)/shard_map/reduce_scatter | solution.py:772
  251.3 25.8 %collective-permute-start.26 = (bf16[768,1024]{1,0:T(8,128)(2,1)S(1)}, bf16[768,1024]{1,0:T(8,128)(2,1)S(1)}, u32[]{:S(2)}, u32[]{:S(2)}) collective-permute-start(bf16[768,1024]{1,0:T(8,128)(2,1)S(1)} %fusion.25), channel_id=1, source_target_pairs={{0,1},{1,0},{2,3},{3,2},{4,5},{5,4},{6,7},{7,6},{8,9},{9,8},{10,11... | collective-permute-start | bytes 4718600 | tf_op jit(solution)/shard_map/ppermute | solution.py:27
  271.3 30.1 %collective-permute-start.30 = (bf16[256,256]{1,0:T(8,128)(2,1)}, bf16[256,256]{1,0:T(8,128)(2,1)}, u32[]{:S(2)}, u32[]{:S(2)}) collective-permute-start(bf16[256,256]{1,0:T(8,128)(2,1)} %get-tuple-element.148), channel_id=1, source_target_pairs={{0,1},{1,0},{2,3},{3,2},{4,5},{5,4},{6,7},{7,6},{8,9},{9,8},{10,11... | collective-permute-start | bytes 393224 | tf_op jit(solution)/shard_map/ppermute | solution.py:27
  271.3 52.5 %collective-permute-start.27 = (bf16[256,256]{1,0:T(8,128)(2,1)}, bf16[256,256]{1,0:T(8,128)(2,1)}, u32[]{:S(2)}, u32[]{:S(2)}) collective-permute-start(bf16[256,256]{1,0:T(8,128)(2,1)} %get-tuple-element.143), channel_id=1, source_target_pairs={{0,1},{1,0},{2,3},{3,2},{4,5},{5,4},{6,7},{7,6},{8,9},{9,8},{10,11... | collective-permute-start | bytes 393224 | tf_op jit(solution)/shard_map/ppermute | solution.py:27
  277.1 25.0 %collective-permute-start.32 = (bf16[256,256]{1,0:T(8,128)(2,1)S(1)}, bf16[256,256]{1,0:T(8,128)(2,1)S(1)}, u32[]{:S(2)}, u32[]{:S(2)}) collective-permute-start(bf16[256,256]{1,0:T(8,128)(2,1)S(1)} %slice_bitcast_fusion.1), channel_id=1, source_target_pairs={{0,1},{1,0},{2,3},{3,2},{4,5},{5,4},{6,7},{7,6},{8,9},{9,8},{10,11... | collective-permute-start | bytes 393224 | tf_op jit(solution)/shard_map/ppermute | solution.py:27
  282.7 41.1 %collective-permute-start.29 = (bf16[256,256]{1,0:T(8,128)(2,1)S(1)}, bf16[256,256]{1,0:T(8,128)(2,1)S(1)}, u32[]{:S(2)}, u32[]{:S(2)}) collective-permute-start(bf16[256,256]{1,0:T(8,128)(2,1)S(1)} %slice_bitcast_fusion.2), channel_id=1, source_target_pairs={{0,1},{1,0},{2,3},{3,2},{4,5},{5,4},{6,7},{7,6},{8,9},{9,8},{10,11... | collective-permute-start | bytes 393224 | tf_op jit(solution)/shard_map/ppermute | solution.py:27
  282.8 80.0 %collective-permute-start.61 = (bf16[1024,512]{1,0:T(8,128)(2,1)}, bf16[1024,512]{1,0:T(8,128)(2,1)}, u32[]{:S(2)}, u32[]{:S(2)}) collective-permute-start(bf16[1024,512]{1,0:T(8,128)(2,1)} %constant_dynamic-slice_fusion.1), channel_id=1, source_target_pairs={{0,2},{2,0},{1,3},{3,1},{4,6},{6,4},{5,7},{7,5},{8,10},{10,8},{9,1... | collective-permute-start | bytes 3145736 | tf_op jit(solution)/shard_map/ppermute | solution.py:27
  301.5 49.8 %collective-permute-start.52 = (bf16[1024,256]{1,0:T(8,128)(2,1)S(1)}, bf16[1024,256]{1,0:T(8,128)(2,1)S(1)}, u32[]{:S(2)}, u32[]{:S(2)}) collective-permute-start(bf16[1024,256]{1,0:T(8,128)(2,1)S(1)} %constant_dynamic-slice_fusion.8), channel_id=1, source_target_pairs={{0,2},{2,0},{1,3},{3,1},{4,6},{6,4},{5,7},{7,5},{8,10},{10,8},{9,1... | collective-permute-start | bytes 1572872 | tf_op jit(solution)/shard_map/ppermute | solution.py:27
  359.4 30.1 %collective-permute-start.39 = (bf16[256,1024]{1,0:T(8,128)(2,1)}, bf16[256,1024]{1,0:T(8,128)(2,1)}, u32[]{:S(2)}, u32[]{:S(2)}) collective-permute-start(bf16[256,1024]{1,0:T(8,128)(2,1)} %get-tuple-element.164), channel_id=1, source_target_pairs={{0,1},{1,0},{2,3},{3,2},{4,5},{5,4},{6,7},{7,6},{8,9},{9,8},{10,11... | collective-permute-start | bytes 1572872 | tf_op jit(solution)/shard_map/ppermute | solution.py:27
  365.7 89.7 %reduce-scatter.4.cloned.1.call-start = ((), (), s32[]{:S(2)}) async-start(), calls=%async_computation.3 | async-start | bytes 1310720 | tf_op jit(solution)/shard_map/reduce_scatter | solution.py:783
  365.7 31.6 %collective-permute-start.36 = (bf16[256,1024]{1,0:T(8,128)(2,1)}, bf16[256,1024]{1,0:T(8,128)(2,1)S(1)}, u32[]{:S(2)}, u32[]{:S(2)}) collective-permute-start(bf16[256,1024]{1,0:T(8,128)(2,1)} %get-tuple-element.159), channel_id=1, source_target_pairs={{0,1},{1,0},{2,3},{3,2},{4,5},{5,4},{6,7},{7,6},{8,9},{9,8},{10,11... | collective-permute-start | bytes 1572872 | tf_op jit(solution)/shard_map/ppermute | solution.py:27
  372.7 31.2 %collective-permute-start.38 = (bf16[256,1024]{1,0:T(8,128)(2,1)S(1)}, bf16[256,1024]{1,0:T(8,128)(2,1)S(1)}, u32[]{:S(2)}, u32[]{:S(2)}) collective-permute-start(bf16[256,1024]{1,0:T(8,128)(2,1)S(1)} %add_convert_fusion.8), channel_id=1, source_target_pairs={{0,2},{2,0},{1,3},{3,1},{4,6},{6,4},{5,7},{7,5},{8,10},{10,8},{9,1... | collective-permute-start | bytes 1572872 | tf_op jit(solution)/shard_map/ppermute | solution.py:27
  383.0 43.0 %collective-permute-start.53 = (bf16[4,128,1024]{2,1,0:T(8,128)(2,1)}, bf16[4,128,1024]{2,1,0:T(8,128)(2,1)}, u32[]{:S(2)}, u32[]{:S(2)}) collective-permute-start(bf16[4,128,1024]{2,1,0:T(8,128)(2,1)} %constant_dynamic-slice_fusion.7), channel_id=1, source_target_pairs={{0,4},{4,0},{1,5},{5,1},{2,6},{6,2},{3,7},{7,3},{8,12},{12,8},{9,1... | collective-permute-start | bytes 3145736 | tf_op jit(solution)/shard_map/ppermute | solution.py:27
  (115 other events, 1032.2 us)
Sparse Core Ops, SparseCore 0:
  215.0 76.2 reduce-scatter.5
  365.8 27.2 reduce-scatter.7
  428.7 26.6 reduce-scatter.3

commit v4 on v3

v4 whole, which is shorter than its diff:
```python
import functools
import math

import jax
import jax.numpy as jnp
from jax import lax
from jax.experimental import pallas as pl
from jax.experimental.pallas import tpu as pltpu
from jax.sharding import Mesh, PartitionSpec as P

HEADS = 16
HEAD_DIM = 64
TEMB = 256
SEGS = 8
EPSILON = 1e-05
F32 = jnp.float32
BF16 = jnp.bfloat16
NEG = -1e30
LOG2E = math.log2(math.e)
GELU_A = math.sqrt(2.0 / math.pi)
GELU_B = GELU_A * 0.044715
BLOCK = 256
VMEM = 60 * 1024 * 1024


def swap(value, axis):
    return lax.ppermute(value, axis, [(0, 1), (1, 0)])


def time_features(doc_times, column, half_size):
    frequency = jnp.exp(-math.log(10000.0) * (column % half_size).astype(F32) / half_size)
    angles = doc_times.astype(F32)[..., None] * frequency
    return jnp.where(column < half_size, jnp.sin(angles), jnp.cos(angles)).astype(BF16)


def rotary_tables(positions, head_size):
    half_size = head_size // 2
    frequency = jnp.exp(-math.log(10000.0) * 2.0 * jnp.arange(half_size, dtype=F32) / head_size)
    angles = positions.astype(F32)[..., None] * frequency
    cos_tab, sin_tab = jnp.cos(angles), jnp.sin(angles)
    return (
        jnp.concatenate([cos_tab] * 4, axis=-1),
        jnp.concatenate([-sin_tab, sin_tab, -sin_tab, sin_tab], axis=-1),
    )


def dot(left_op, right_op, left_dim=1, right_dim=0):
    return lax.dot_general(
        left_op, right_op, (((left_dim,), (right_dim,)), ((), ())), preferred_element_type=F32
    )


def turn(values, cos_tab, sin_tab):
    slabs = []
    lane = lax.broadcasted_iota(jnp.int32, (values.shape[0], 128), 1)
    first = lane % HEAD_DIM < HEAD_DIM // 2
    for start in range(0, values.shape[1], 128):
        slab = values[:, start : start + 128]
        partner = jnp.where(
            first, pltpu.roll(slab, 128 - HEAD_DIM // 2, 1), pltpu.roll(slab, HEAD_DIM // 2, 1)
        )
        slabs.append(slab * cos_tab + partner * sin_tab)
    return jnp.concatenate(slabs, axis=1)


def split_low(values):
    high = values.astype(BF16)
    return jnp.concatenate([high, (values - high.astype(F32)).astype(BF16)], axis=0)


def centre(values):
    scale = 1.0 / values.shape[-1]
    centred = values - jnp.sum(values, axis=-1, keepdims=True) * scale
    spread = jnp.sum(centred * centred, axis=-1, keepdims=True) * scale
    inverse = lax.rsqrt(spread + EPSILON)
    return centred * inverse, inverse


def norm_back(grad, gain, hat, inverse):
    scale = 1.0 / grad.shape[-1]
    scaled = grad * gain
    mean = jnp.sum(scaled, axis=-1, keepdims=True) * scale
    along = jnp.sum(scaled * hat, axis=-1, keepdims=True) * scale
    return inverse * (scaled - mean - hat * along)


def call(body, name, prefetch, grid, ins, outs, scratch=(), deps=(), held=(), flops=0, moved=0, trans=0):
    count = len(prefetch) + len(ins)
    extra = [array for array, _ in held] + list(deps)

    def kernel(*refs):
        body(*refs[:count], *refs[count + len(extra) :])

    return pl.pallas_call(
        kernel,
        grid_spec=pltpu.PrefetchScalarGridSpec(
            num_scalar_prefetch=len(prefetch),
            grid=grid,
            in_specs=[spec for _, spec in ins] + [pl.BlockSpec(memory_space=pl.ANY)] * len(extra),
            out_specs=[spec for _, _, spec in outs],
            scratch_shapes=list(scratch),
        ),
        out_shape=[jax.ShapeDtypeStruct(shape, kind) for shape, kind, _ in outs],
        input_output_aliases={count + n: out for n, (_, out) in enumerate(held)},
        compiler_params=pltpu.CompilerParams(vmem_limit_bytes=VMEM),
        cost_estimate=pl.CostEstimate(flops=flops, bytes_accessed=moved, transcendentals=trans),
        name=name,
    )(*prefetch, *[array for array, _ in ins], *extra)


def fixed(shape):
    return pl.BlockSpec(shape, lambda *_: (0,) * len(shape))


def along(shape, axis=0, start=0):
    return pl.BlockSpec(shape, lambda g, *_: tuple(start + g if n == axis else 0 for n in range(len(shape))))


def norm1_body(x_ref, seg_ref, shift_ref, gain_ref, bias_ref, stream_ref, low_ref):
    slots = lax.broadcasted_iota(jnp.int32, (SEGS, seg_ref.shape[-1]), 0) == seg_ref[0]
    onehot = slots.astype(F32).astype(BF16)
    added = dot(jnp.concatenate([onehot, onehot], axis=0), split_low(shift_ref[0]), 0, 0)
    stream = x_ref[0].astype(F32) + added
    hat, _ = centre(stream)
    stream_ref[0] = stream
    low_ref[0] = (hat * gain_ref[...] + bias_ref[...]).astype(BF16)


def norm1(x, seg, shift, gain, bias):
    rows, shard, model = x.shape
    block = along((1, shard, model))
    return call(
        norm1_body, "norm1", (), (rows,),
        [(x, block), (seg, along((1, 1, shard))), (shift, along((1, SEGS, model))), (gain, fixed((1, model))), (bias, fixed((1, model)))],
        [(x.shape, F32, block), (x.shape, BF16, block)],
        moved=8 * x.size,
    )


def qkv_body(me_ref, a_ref, b_ref, w_ref, bias_ref, cos_ref, sin_ref, out_ref, all_ref, own_ref):
    rows, shard, model = a_ref.shape
    width = w_ref.shape[1]
    refs = (a_ref, b_ref)
    step = pl.program_id(0)

    @pl.when(step == 0)
    def _():
        for n, x_ref in enumerate(refs):
            all_ref[n] = x_ref[...]

    def run(turned):
        w, bias = w_ref[...], bias_ref[...].astype(F32)
        found = [dot(x_ref[...].reshape(rows * shard, model), w) for x_ref in refs]
        for n, full in enumerate(found):
            for r in range(rows):
                values = full[r * shard : (r + 1) * shard] + bias
                if turned:
                    values = turn(values, cos_ref[n], sin_ref[n]) * jnp.where(step == 0, LOG2E * HEAD_DIM**-0.5, 1.0)
                out_ref[0, n, r] = values.astype(BF16)

    own_ref[...] = w_ref[...].T

    @pl.when(step < 2)
    def _():
        run(True)

    @pl.when(step == 2)
    def _():
        run(False)


def project_qkv(pair, parts, me, first, second, weight, bias, cos_tab, sin_tab, held=(), deps=()):
    rows, shard, model = first.shape
    width = model // parts
    return call(
        qkv_body, "qkv", (me,), (3,),
        [(first, fixed(first.shape)), (second, fixed(first.shape))]
        + [
            (weight, pl.BlockSpec((model, width), lambda g, m: (0, g * parts + m[0]))),
            (bias, pl.BlockSpec((1, width), lambda g, m: (0, g * parts + m[0]))),
            (cos_tab, pl.BlockSpec((2, shard, 128), lambda g, m: (pair, 0, 0))),
            (sin_tab, pl.BlockSpec((2, shard, 128), lambda g, m: (pair, 0, 0))),
        ],
        [
            ((3, parts, rows, shard, width), BF16, pl.BlockSpec((1, 2, rows, shard, width), lambda g, m: (g, pair, 0, 0, 0))),
            ((parts, rows, shard, model), BF16, pl.BlockSpec((2, rows, shard, model), lambda g, m: (pair, 0, 0, 0))),
            ((3 * width, model), BF16, along((width, model))),
        ],
        held=[(array, n) for n, array in enumerate(held)], deps=deps,
        flops=12 * rows * shard * model * width, moved=2 * (3 * model * width + 4 * rows * shard * model),
    )


def seg_columns(segq_all, segk):
    pieces, shard, _ = segk.shape
    for j in range(pieces):
        row = jnp.broadcast_to(segq_all[j:j+1].astype(F32), (128, shard))
        segk[j] = row.T

def attend_body(start, cnt_ref, idx_ref, qkv_ref, seg_ref, o_ref, one_ref, far_ref, lse_ref, vt, segk, qmt, acc):
    row = pl.program_id(0) + start
    _, pieces, _, shard, width = qkv_ref.shape
    heads = width // HEAD_DIM

    @pl.when(pl.program_id(0) == 0)
    def _():
        qmt[...] = jnp.zeros_like(qmt)

    for j in range(pieces):
        vt[j] = qkv_ref[2, j, 0].T
        qt = qkv_ref[0, j, 0].T
        for h in range(heads):
            at = slice(h * HEAD_DIM, (h + 1) * HEAD_DIM)
            qmt[j, at, h * shard : (h + 1) * shard] = qt[at]
    seg_columns(seg_ref[0], segk)

    @pl.loop(0, pieces)
    def _(piece):
        attend_piece(row * pieces + piece, piece, cnt_ref, idx_ref, qkv_ref.at[1], seg_ref, lse_ref, vt, segk, qmt, acc)

    for j in range(pieces):
        o_ref[j, 0] = acc[j].T.astype(BF16)
    one_ref[0] = o_ref[1, 0]
    far_ref[:, 0] = o_ref[2:, 0]


def attend_piece(at_q, piece, cnt_ref, idx_ref, k_ref, seg_ref, lse_ref, vt, segk, qmt, acc):
    pieces, _, shard, width = k_ref.shape
    heads = width // HEAD_DIM
    seg_q = seg_ref[0, pl.ds(piece, 1)].astype(F32)

    def run(count):
        @pl.when(cnt_ref[at_q] == count)
        def _():
            qm = qmt[piece]
            places = [idx_ref[at_q * pieces + t] for t in range(count)]
            top, tot, out = [None] * heads, [None] * heads, [None] * heads
            later = dot(k_ref[places[0], 0], qm)
            for t in range(count):
                s = later
                if t + 1 < count:
                    later = dot(k_ref[places[t + 1], 0], qm)
                col = segk[places[t]]
                same = jnp.concatenate([col] * (shard // 128), axis=1) == seg_q
                for h in range(heads):
                    at = slice(h * HEAD_DIM, (h + 1) * HEAD_DIM)
                    sh = jnp.where(same, s[:, h * shard : (h + 1) * shard], NEG)
                    best = jnp.max(sh, axis=0, keepdims=True)
                    if t:
                        best = jnp.maximum(top[h], best)
                        fade = jnp.exp2(top[h] - best)
                    p = jnp.exp2(sh - best)
                    total = jnp.sum(p, axis=0, keepdims=True)
                    found = dot(vt[places[t], at], p.astype(BF16))
                    if t:
                        total = tot[h] * fade + total
                        found = out[h] * fade + found
                    top[h], tot[h], out[h] = best, total, found
            for h in range(heads):
                acc[piece, h * HEAD_DIM : (h + 1) * HEAD_DIM] = out[h] / tot[h]
                lse_ref[0, piece, h : h + 1] = top[h] + jnp.log2(tot[h])

    for count in range(1, pieces + 1):
        run(count)


def attend(start, count, cnt, idx, qkv, seg, held=()):
    _, pieces, rows, shard, width = qkv.shape
    heads = width // HEAD_DIM
    pairs = count * (pieces * shard) ** 2
    return call(
        functools.partial(attend_body, start), "attend", (cnt, idx), (count,),
        [(qkv, along((3, pieces, 1, shard, width), 2, start)), (seg, along((1, pieces, shard), 0, start))],
        [
            ((pieces, rows, shard, width), BF16, along((pieces, 1, shard, width), 1, start)),
            ((count, shard, width), BF16, along((1, shard, width))),
            ((2, count, shard, width), BF16, along((2, 1, shard, width), 1)),
            ((rows, pieces, 8, shard), F32, along((1, pieces, 8, shard), 0, start)),
        ],
        [
            pltpu.VMEM((pieces, width, shard), BF16),
            pltpu.VMEM((pieces, shard, 128), F32),
            pltpu.VMEM((pieces, width, heads * shard), BF16),
            pltpu.VMEM((pieces, width, shard), F32),
        ],
        held=list(zip(held, (0, 3))), flops=16 * pairs * width, moved=8 * count * pieces * shard * width, trans=pairs * heads,
    )


def attend_back_body(
    start, cnt_ref, idx_ref, qkv_ref, o_ref, do0, do1, do2, do3, lse_ref, seg_ref, cos_ref, sin_ref, w_ref,
    g_ref, p0_ref, p1_ref, p2_ref, p3_ref, kt, segk, dk, dv, dqt, qmt, gmt, qst, gst, low,
):
    row = pl.program_id(0) + start
    _, pieces, _, shard, width = qkv_ref.shape
    heads = width // HEAD_DIM

    @pl.when(pl.program_id(0) == 0)
    def _():
        qmt[...] = jnp.zeros_like(qmt)
        gmt[...] = jnp.zeros_like(gmt)

    seg_columns(seg_ref[0], segk)
    dk[...] = jnp.zeros_like(dk)
    dv[...] = jnp.zeros_like(dv)
    lane = lax.broadcasted_iota(jnp.int32, (shard, width), 1) // HEAD_DIM
    chosen = lax.broadcasted_iota(jnp.int32, (8, width), 1) // HEAD_DIM
    chosen = (chosen == lax.broadcasted_iota(jnp.int32, (8, width), 0)).astype(BF16)
    for j, do_ref in enumerate((do0, do1, do2, do3)):
        kt[j] = qkv_ref[1, j, 0].T
        q, do = qkv_ref[0, j, 0], do_ref[...].reshape(shard, width)
        qt, gt = q.T, do.T
        for h in range(heads):
            at, qa = slice(h * HEAD_DIM, (h + 1) * HEAD_DIM), slice(h * shard, (h + 1) * shard)
            qmt[j, at, qa] = qt[at]
            gmt[j, at, qa] = gt[at]
            qst[j, qa] = jnp.where(lane == h, q, jnp.zeros_like(q))
            gst[j, qa] = jnp.where(lane == h, do, jnp.zeros_like(do))
        prod = do.astype(F32) * o_ref[j, 0].astype(F32)
        high = prod.astype(BF16)
        low[j] = dot(chosen, high, 1, 1) + dot(chosen, (prod - high.astype(F32)).astype(BF16), 1, 1)

    @pl.loop(0, pieces)
    def _(piece):
        back_piece(
            row * pieces + piece, piece, cnt_ref, idx_ref, qkv_ref.at[1], qkv_ref.at[2], lse_ref, seg_ref,
            kt, segk, dk, dv, dqt, qmt, gmt, qst, gst, low,
        )

    for j, ref in ((1, p1_ref), (3, p3_ref), (0, p0_ref), (2, p2_ref)):
        grad_q = turn(dqt[j].T * HEAD_DIM**-0.5, cos_ref[j], -sin_ref[j]).astype(BF16)
        grad_k = turn(dk[j] * (1 / LOG2E), cos_ref[j], -sin_ref[j]).astype(BF16)
        grad = jnp.concatenate([grad_q, grad_k, dv[j].astype(BF16)], axis=1)
        g_ref[j, 0] = grad
        ref[0] = dot(grad, w_ref[...]).astype(BF16)


def back_piece(
    at_q, piece, cnt_ref, idx_ref, k_ref, v_ref, lse_ref, seg_ref, kt, segk, dk, dv, dqt, qmt, gmt, qst, gst, low
):
    pieces, _, shard, width = k_ref.shape
    heads = width // HEAD_DIM
    lse, delta = lse_ref[0, piece], low[piece]
    seg_q = seg_ref[0, pl.ds(piece, 1)].astype(F32)

    def run(count):
        @pl.when(cnt_ref[at_q] == count)
        def _():
            places = [idx_ref[at_q * pieces + t] for t in range(count)]
            qm, gm = qmt[piece], gmt[piece]
            later = dot(k_ref[places[0], 0], qm), dot(v_ref[places[0], 0], gm)
            out = [None] * heads
            for t in range(count):
                s, dp = later
                j = places[t]
                if t + 1 < count:
                    later = dot(k_ref[places[t + 1], 0], qm), dot(v_ref[places[t + 1], 0], gm)
                col = segk[j]
                same = jnp.concatenate([col] * (shard // 128), axis=1) == seg_q
                ps, dss = [], []
                for h in range(heads):
                    at, qa = slice(h * HEAD_DIM, (h + 1) * HEAD_DIM), slice(h * shard, (h + 1) * shard)
                    p = jnp.exp2(jnp.where(same, s[:, qa] - lse[h : h + 1], NEG))
                    ds = (p * (dp[:, qa] - delta[h : h + 1])).astype(BF16)
                    ps.append(p.astype(BF16))
                    dss.append(ds)
                    found = dot(kt[j, at], ds)
                    out[h] = found if t == 0 else out[h] + found
                dv[j] += dot(jnp.concatenate(ps, axis=1), gst[piece])
                dk[j] += dot(jnp.concatenate(dss, axis=1), qst[piece])
            for h in range(heads):
                dqt[piece, h * HEAD_DIM : (h + 1) * HEAD_DIM] = out[h]

    for count in range(1, pieces + 1):
        run(count)


def attend_back(start, count, cnt, idx, qkv, o, do, lse, seg, cos_tab, sin_tab, weight, held=(), deps=()):
    _, pieces, rows, shard, width = qkv.shape
    model = weight.shape[1]
    heads = width // HEAD_DIM
    table = fixed((pieces, shard, 128))
    pairs = count * (pieces * shard) ** 2
    square, wide = (pieces, width, heads * shard), (pieces, shard, width)
    one = along((1, shard, width), 0, start)
    return call(
        functools.partial(attend_back_body, start), "attend_back", (cnt, idx), (count,),
        [(qkv, along((3, pieces, 1, shard, width), 2, start)), (o, along((pieces, 1, shard, width), 1, start))]
        + [(do[0], one), (do[1], one), (do[2], along((1, 1, shard, width), 1, start)), (do[3], one)]
        + [(lse, along((1, pieces, 8, shard), 0, start)), (seg, along((1, pieces, shard), 0, start))]
        + [(cos_tab, table), (sin_tab, table), (weight, fixed(weight.shape))],
        [((pieces, rows, shard, 3 * width), BF16, along((pieces, 1, shard, 3 * width), 1, start))]
        + [((count, shard, model), BF16, along((1, shard, model)))] * pieces,
        [
            pltpu.VMEM((pieces, width, shard), BF16),
            pltpu.VMEM((pieces, shard, 128), F32),
            pltpu.VMEM(wide, F32),
            pltpu.VMEM(wide, F32),
            pltpu.VMEM((pieces, width, shard), F32),
            pltpu.VMEM(square, BF16),
            pltpu.VMEM(square, BF16),
            pltpu.VMEM((pieces, heads * shard, width), BF16),
            pltpu.VMEM((pieces, heads * shard, width), BF16),
            pltpu.VMEM((pieces, 8, shard), F32),
        ],
        held=[(array, 0) for array in held], deps=deps,
        flops=40 * pairs * width, moved=16 * count * pieces * shard * width, trans=pairs * heads,
    )


def middle_body(
    order_ref, a0, a1, a2, a3, w0, w1, w2, w3, stream_ref, bias_ref, gain_ref, shift_ref, mid_ref, low_ref, all_ref,
):
    _, shard, model = stream_ref.shape
    total = 0.0
    for n, (a, w) in enumerate(((a0, w0), (a1, w1), (a2, w2), (a3, w3))):
        values = a[...].reshape(shard, a.shape[-1])
        total = total + dot(values, w[...])
        all_ref[0, :, n * a.shape[-1] : (n + 1) * a.shape[-1]] = values
    mid = stream_ref[0] + (total + bias_ref[...])
    hat, _ = centre(mid)
    mid_ref[0] = mid
    low_ref[0] = (hat * gain_ref[...] + shift_ref[...]).astype(BF16)


def out_blocks(weight, parts):
    width = weight.shape[0] // parts

    def block(i):
        return pl.BlockSpec((width, weight.shape[1]), lambda g, o: (o[i], 0))

    return [(weight, block(i)) for i in range(parts)]


def middle_norm(start, count, order, attended, weight, stream, bias, gain, shift, held=()):
    rows, shard, model = stream.shape
    parts = len(attended)
    width = model // parts
    block, line, one = along((1, shard, model), 0, start), fixed((1, model)), along((1, shard, width))
    first = [along((1, 1, shard, width), 1, start), one, along((1, 1, shard, width), 1), one]
    return call(
        middle_body, "middle", (order,), (count,),
        list(zip(attended, first)) + out_blocks(weight, parts) + [(stream, block), (bias, line), (gain, line), (shift, line)],
        [
            (stream.shape, F32, block),
            ((count, shard, model), BF16, along((1, shard, model))),
            (stream.shape, BF16, block),
        ],
        held=list(zip(held, (0, 2))), flops=2 * count * shard * model * model, moved=14 * count * shard * model,
    )


def cot_body(blk_ref, a_ref, b_ref, up_ref, down_ref, g_ref, up_out, down_out, both_ref):
    tokens = a_ref.shape[0]
    down = down_ref[...]

    @pl.when(pl.program_id(0) == 0)
    def _():
        both_ref[0:tokens] = a_ref[...]
        both_ref[tokens:] = b_ref[...]

    g_ref[0:tokens] = dot(a_ref[...], down, 1, 1).astype(BF16)
    g_ref[tokens:] = dot(b_ref[...], down, 1, 1).astype(BF16)
    up_out[...] = up_ref[...]
    down_out[...] = down


def cot_down(blk, own, other, up, down, picked, half):
    tokens, model = own.shape
    steps = half // BLOCK
    column = along((2 * tokens, BLOCK), 1)
    if picked:
        up_at, down_at = along((model, BLOCK), 1), along((BLOCK, model))
    else:
        up_at = pl.BlockSpec((model, BLOCK), lambda g, b: (0, b[g]))
        down_at = pl.BlockSpec((BLOCK, model), lambda g, b: (b[g], 0))
    return call(
        cot_body, "cot_down", (blk,), (steps,),
        [(own, fixed(own.shape)), (other, fixed(own.shape)), (up, up_at), (down, down_at)],
        [
            ((2 * tokens, half), BF16, column),
            ((model, half), BF16, along((model, BLOCK), 1)),
            ((half, model), BF16, along((BLOCK, model))),
            ((2 * tokens, model), BF16, fixed((2 * tokens, model))),
        ],
        flops=4 * tokens * model * half, moved=2 * (2 * tokens * (model + half) + 4 * model * half),
    )


def hidden_body(blocks, *refs):
    pieces, refs = refs[:-10], refs[-10:]
    g_ref, up_ref, row_ref, bias_ref, act_ref, grad_ref, sum_ref, both_ref, part_ref, held = refs
    sizes = [ref.shape[0] * ref.shape[1] for ref in pieces]
    starts = [sum(sizes[:n]) for n in range(len(sizes))]
    step = pl.program_id(0)

    @pl.when(step == 0)
    def _():
        for ref, at, size in zip(pieces, starts, sizes):
            both_ref[at : at + size] = ref[...].reshape(size, ref.shape[2])

    @pl.when(step < blocks)
    def _():
        up, bias = up_ref[...], bias_ref[...]
        total = 0.0
        later = dot(pieces[0][...].reshape(sizes[0], -1), up)
        for n, (start, size) in enumerate(zip(starts, sizes)):
            at = slice(start, start + size)
            v = later + bias
            if n + 1 < len(pieces):
                later = dot(pieces[n + 1][...].reshape(sizes[n + 1], -1), up)
            square = v * v
            tanh = jnp.tanh(v * (GELU_A + GELU_B * square))
            gate = 0.5 + 0.5 * tanh
            act = v * gate
            slope = gate + act * ((1.0 - tanh) * (GELU_A + 3.0 * GELU_B * square))
            grad = (slope * g_ref[at].astype(F32)).astype(BF16)
            act_ref[at] = act.astype(BF16)
            grad_ref[at] = grad
            held[step, at] = grad
            total = total + jnp.sum(grad.astype(F32), axis=0, keepdims=True)
        sum_ref[...] = total

    @pl.when(step >= blocks)
    def _():
        grad = jnp.concatenate([held[n] for n in range(blocks)], axis=1)
        part_ref[...] = dot(grad, row_ref[...], 1, 1).astype(BF16)


def hidden_units(pieces, grads, up, bias):
    model = pieces[0].shape[2]
    tokens, half = grads.shape
    blocks, more = half // BLOCK, model // BLOCK

    def first(g):
        return jnp.minimum(g, blocks - 1)

    def second(g):
        return jnp.maximum(g - blocks, 0)

    column, line = pl.BlockSpec((tokens, BLOCK), lambda g: (0, first(g))), pl.BlockSpec((1, BLOCK), lambda g: (0, first(g)))
    return call(
        functools.partial(hidden_body, blocks), "hidden", (), (blocks + more,),
        [(piece, fixed(piece.shape)) for piece in pieces]
        + [
            (grads, column),
            (up, pl.BlockSpec((model, BLOCK), lambda g: (0, first(g)))),
            (up, pl.BlockSpec((BLOCK, half), lambda g: (second(g), 0))),
            (bias, line),
        ],
        [
            (grads.shape, BF16, column),
            (grads.shape, BF16, column),
            ((1, half), F32, line),
            ((tokens, model), BF16, fixed((tokens, model))),
            ((tokens, model), BF16, pl.BlockSpec((tokens, BLOCK), lambda g: (0, second(g)))),
        ],
        [pltpu.VMEM((blocks, tokens, BLOCK), BF16)],
        flops=4 * tokens * model * half, moved=2 * (tokens * (3 * model + 3 * half) + 2 * model * half), trans=tokens * half,
    )


def middle_back_body(
    order_ref, part_ref, sent_ref, mid_ref, cot_ref, gain_ref, w0, w1, w2, w3,
    grad_ref, low_ref, att0_ref, att1_ref, far_ref, sums_ref,
):
    grad = part_ref[...].astype(F32) + sent_ref[...].astype(F32)
    hat, inverse = centre(mid_ref[0])
    cot = cot_ref[0].astype(F32)
    total = cot + norm_back(grad, gain_ref[...], hat, inverse)
    low = total.astype(BF16)
    grad_ref[0] = total
    low_ref[0] = low
    far_ref[0, 0] = dot(low, w2[...], 1, 1).astype(BF16)
    far_ref[1, 0] = dot(low, w3[...], 1, 1).astype(BF16)
    att1_ref[0] = dot(low, w1[...], 1, 1).astype(BF16)
    att0_ref[0] = dot(low, w0[...], 1, 1).astype(BF16)

    @pl.when(pl.program_id(0) == 0)
    def _():
        sums_ref[...] = jnp.zeros_like(sums_ref)

    sums_ref[0:1] += jnp.sum(grad * hat, axis=0, keepdims=True)
    sums_ref[1:2] += jnp.sum(grad, axis=0, keepdims=True)
    sums_ref[2:3] += jnp.sum(low.astype(F32), axis=0, keepdims=True)
    sums_ref[3:4] += jnp.sum(cot, axis=0, keepdims=True)


def middle_back(order, both, sent, mid, cot, gain, weight, parts, deps=()):
    rows, shard, model = mid.shape
    width = model // parts
    block, one = along((1, shard, model)), along((1, shard, width))
    flat = pl.BlockSpec((shard, model), lambda g, o: (g, 0))
    return call(
        middle_back_body, "middle_back", (order,), (rows,),
        [(both, flat), (sent, flat), (mid, block), (cot, block), (gain, fixed((1, model)))] + out_blocks(weight, parts),
        [
            (mid.shape, F32, block),
            (mid.shape, BF16, block),
            ((rows, shard, width), BF16, one),
            ((rows, shard, width), BF16, one),
            ((2, rows, shard, width), BF16, along((2, 1, shard, width), 1)),
            ((8, model), F32, fixed((8, model))),
        ],
        deps=deps, flops=2 * rows * shard * model * model, moved=18 * mid.size,
    )


def norm1_back_body(part_ref, near_ref, far_ref, stream_ref, mid_ref, gain_ref, seg_ref, in_ref, shift_ref, sums_ref):
    grad = part_ref[0].astype(F32) + near_ref[0].astype(F32) + far_ref[0].astype(F32)
    hat, inverse = centre(stream_ref[0])
    total = mid_ref[0] + norm_back(grad, gain_ref[...], hat, inverse)
    in_ref[0] = total.astype(BF16)
    slots = lax.broadcasted_iota(jnp.int32, (SEGS, seg_ref.shape[-1]), 0) == seg_ref[0]
    onehot = slots.astype(F32).astype(BF16)
    shift_ref[0] = dot(jnp.concatenate([onehot, onehot], axis=1), split_low(total))

    @pl.when(pl.program_id(0) == 0)
    def _():
        sums_ref[...] = jnp.zeros_like(sums_ref)

    sums_ref[0:1] += jnp.sum(grad * hat, axis=0, keepdims=True)
    sums_ref[1:2] += jnp.sum(grad, axis=0, keepdims=True)


def norm1_back(start, count, own, near, far, stream, mid, gain, seg, held=(), deps=()):
    rows, shard, model = stream.shape
    block, own_block = along((1, shard, model), 0, start), along((1, shard, model))
    return call(
        norm1_back_body, "norm1_back", (), (count,),
        [(own, own_block), (near, own_block), (far, own_block), (stream, block), (mid, block), (gain, fixed((1, model)))]
        + [(seg, along((1, 1, shard), 0, start))],
        [
            (stream.shape, BF16, block),
            ((count, SEGS, model), F32, along((1, SEGS, model))),
            ((8, model), F32, fixed((8, model))),
        ],
        held=[(array, 0) for array in held], deps=deps, moved=16 * count * shard * model,
    )


def exchange(own, one, far):
    far = swap(far, "y")
    return [own, swap(one, "c"), far, swap(far[1], "c")]


def after(value, *others):
    return lax.optimization_barrier((value,) + others)[0]


def cut(values, index, size, axis):
    return lax.dynamic_slice_in_dim(values, index * size, size, axis)


def add_low(kept, sent):
    return (kept.astype(F32) + sent.astype(F32)).astype(BF16)


def ordered(at, own, other, axis):
    return jnp.where(at == 0, jnp.concatenate([own, other], axis), jnp.concatenate([other, own], axis))


def local(
    inputs, segment_ids, doc_times, time_weight, time_bias, norm1_gain, norm1_bias, qkv_weight, qkv_bias,
    out_weight, out_bias, norm2_gain, norm2_bias, up_weight, up_bias, down_weight, down_bias, cotangent,
    *, dp,
):
    rows, shard, model = inputs.shape
    parts = 4
    tokens = rows * shard
    hidden_width = up_weight.shape[1]
    width = model // parts
    depth = dp // 2
    half = hidden_width // 2
    piece = half // dp
    z_at, x_at, y_at, c_at = (lax.axis_index(name) for name in ("z", "x", "y", "c"))
    me = 2 * y_at + c_at
    order = [me ^ i for i in range(parts)]
    order_list = jnp.stack(order).astype(jnp.int32)
    me_list = order_list[:1]

    def line(vector):
        return vector.astype(F32)[None]

    groups = [(0, rows - 1), (rows - 1, 1)] if rows > 1 else [(0, 1)]
    seg = segment_ids[:, None, :]
    features = time_features(doc_times.reshape(rows * SEGS), jnp.arange(TEMB), TEMB // 2)
    time_shift = dot(features, time_weight).reshape(rows, SEGS, model) + time_bias.astype(F32)
    stream, own1 = norm1(inputs, seg, time_shift, line(norm1_gain), line(norm1_bias))
    two1 = swap(own1, "y")
    one1 = swap(own1, "c")

    seg_two = swap(segment_ids, "y")
    segs = jnp.stack([segment_ids, swap(segment_ids, "c"), seg_two, swap(seg_two, "c")], axis=1)
    low_id, high_id = segs.min(axis=2), segs.max(axis=2)
    act = (low_id[:, :, None] <= high_id[:, None, :]) & (low_id[:, None, :] <= high_id[:, :, None])
    places = jnp.arange(parts, dtype=jnp.int32)
    rank = jnp.cumsum(act.astype(jnp.int32), axis=2) - 1
    chosen = act[..., None] & (rank[..., None] == places)
    idx = jnp.sum(jnp.where(chosen, places[:, None], 0), axis=2).astype(jnp.int32).reshape(-1)
    cnt = jnp.sum(act.astype(jnp.int32), axis=2).reshape(-1)
    positions = jnp.stack([o * shard + jnp.arange(shard, dtype=jnp.int32) for o in order])
    cos_tab, sin_tab = rotary_tables(positions, HEAD_DIM)

    cot = cotangent.reshape(tokens, model)
    cot_other = swap(cot, "c")
    turned = jnp.stack([1 - x_at, x_at])
    if piece % BLOCK == 0:
        blk = ((jnp.arange(depth)[None, :] * 2 + turned[:, None]) * 2 + c_at) * (piece // BLOCK)
        blk = (blk[..., None] + jnp.arange(piece // BLOCK)).reshape(-1).astype(jnp.int32)
        up_from, down_from = up_weight, down_weight
    else:
        blk = jnp.zeros((half // BLOCK,), jnp.int32)
        up_from = up_weight.reshape(model, depth, 2, 2, piece)
        up_from = lax.dynamic_index_in_dim(up_from, c_at, 3, keepdims=False)
        up_from = jnp.where(x_at == 1, up_from, up_from[:, :, ::-1]).transpose(0, 2, 1, 3).reshape(model, half)
        down_from = down_weight.reshape(depth, 2, 2, piece, model)
        down_from = lax.dynamic_index_in_dim(down_from, c_at, 2, keepdims=False)
        down_from = jnp.where(x_at == 1, down_from, down_from[:, ::-1]).transpose(1, 0, 2, 3).reshape(half, model)
    grad_act, up_own, down_own, cot_both = cot_down(
        blk, cot, cot_other, up_from, down_from, piece % BLOCK != 0, half
    )
    up_bias_own = lax.dynamic_index_in_dim(up_bias.reshape(depth, 2, 2, piece), c_at, 2, keepdims=False)
    up_bias_own = jnp.where(x_at == 1, up_bias_own, up_bias_own[:, ::-1]).transpose(1, 0, 2).reshape(half)

    bias_line = qkv_bias.reshape(1, 3 * model)
    qkv, normed1_all, qkv_own = project_qkv(
        0, parts, me_list, own1, one1, qkv_weight, bias_line, cos_tab, sin_tab, (), (grad_act,)
    )
    two1 = after(two1, qkv)
    qkv, normed1_all, _ = project_qkv(
        1, parts, me_list, two1, swap(two1, "c"), qkv_weight, bias_line, cos_tab, sin_tab, (qkv, normed1_all)
    )
    o, lse, attended = None, None, []
    for start, count in groups:
        held = () if o is None else (o, lse)
        o, out_one, out_far, lse = attend(start, count, cnt, idx, qkv, segs, held)
        attended.append(exchange(o, out_one, out_far))
    held, normed2, normed2_other = (), [], []
    for (start, count), values in zip(groups, attended):
        values = [o] + values[1:]
        middle, low, attended_all = middle_norm(
            start, count, order_list, values, out_weight, stream, line(out_bias), line(norm2_gain), line(norm2_bias), held
        )
        held = (middle, attended_all)
        normed2.append(low)
        normed2_other.append(swap(low, "c"))

    active, grad_hidden, up_b, normed2_both, part2 = hidden_units(
        normed2 + normed2_other, grad_act, up_own, line(up_bias_own)
    )
    part2_sent = swap(part2[tokens:], "c")
    grad_middle, grad_middle_low, att0, att1, far, sums2 = middle_back(
        order_list, part2, part2_sent, middle, cotangent, line(norm2_gain), out_weight, parts
    )
    grad_o = exchange(att0, att1, far)
    sums2 = sums2[:4]

    active_late, grad_hidden_late = lax.optimization_barrier((active, grad_hidden, far))[:2]
    up_grad = dot(normed2_both, grad_hidden_late, 0, 0).astype(BF16)
    up_z = lax.psum_scatter(up_grad, "z", scatter_dimension=0, tiled=True)
    down_out = dot(active_late[:, : half // 2], cot_both, 0, 0).astype(BF16)
    down_sent = swap(down_out, "x")
    active_late = after(active_late, down_out, up_grad)
    down_kept = dot(active_late[:, half // 2 :], cot_both, 0, 0).astype(BF16)
    feed_sent = swap(dot(active_late[tokens:], down_own).astype(BF16), "c")
    feed = dot(active_late[:tokens], down_own) + feed_sent.astype(F32) + line(down_bias)
    output = (middle + feed.reshape(rows, shard, model)).astype(BF16)
    out_grad = dot(
        attended_all.reshape(tokens, model), grad_middle_low.reshape(tokens, model), 0, 0
    ).astype(BF16)

    grad_qkv, back = (), []
    deps = (down_kept, output, out_grad)
    for start, count in groups:
        grad_qkv, own, one, two, three = attend_back(
            start, count, cnt, idx, qkv, o, grad_o, lse, segs, cos_tab, sin_tab, qkv_own, grad_qkv, deps
        )
        grad_qkv = (grad_qkv,)
        there = add_low(two, swap(three, "c"))
        deps = (there,)
        back.append((own, swap(one, "c"), swap(there, "y")))
    grad_qkv = after(grad_qkv[0], there).reshape(parts * tokens, 3 * width)
    qkv_grad = dot(normed1_all.reshape(parts * tokens, model), grad_qkv, 0, 0).astype(BF16)
    qkv_b = jnp.sum(grad_qkv.astype(F32), axis=0)
    held, grad_shift, sums1 = (), [], 0.0
    for (start, count), values in zip(groups, back):
        input_grad, found, sums = norm1_back(
            start, count, *values, stream, grad_middle, line(norm1_gain), seg, held, (qkv_grad,)
        )
        held = (input_grad,)
        grad_shift.append(found.reshape(count * SEGS, model))
        sums1 = sums1 + sums[:2]

    down_x = add_low(down_kept, down_sent)
    down_y = add_low(cut(down_x, y_at, model // 2, 1), swap(cut(down_x, 1 - y_at, model // 2, 1), "y"))
    down_z = lax.psum_scatter(down_y, "z", scatter_dimension=0, tiled=True)
    up_rows = model // dp
    up_sent = swap(cut(up_z, 1 - x_at, up_rows, 0), "x")
    up_sent = jnp.concatenate([up_sent[:, half // 2 :], up_sent[:, : half // 2]], axis=1)
    up_x = add_low(cut(up_z, x_at, up_rows, 0), up_sent)
    up_y = add_low(cut(up_x, y_at, half // 2, 1), swap(cut(up_x, 1 - y_at, half // 2, 1), "y"))
    out_grad = jnp.concatenate([cut(out_grad, o_at, width, 0) for o_at in order], axis=0)
    out_c = add_low(cut(out_grad, c_at, model // 2, 1), swap(cut(out_grad, 1 - c_at, model // 2, 1), "c"))
    out_y = add_low(cut(out_c, y_at, width, 1), swap(cut(out_c, 1 - y_at, width, 1), "y"))
    late = jnp.concatenate([qkv_grad, out_y], axis=1).reshape(depth, 2 * up_rows, model)
    late_x = add_low(cut(late, x_at, up_rows, 1), swap(cut(late, 1 - x_at, up_rows, 1), "x"))
    late_z = lax.psum_scatter(late_x, "z", scatter_dimension=0, tiled=False)

    down_done = ordered(y_at, down_z, swap(down_z, "y"), 1)
    down_done = ordered(c_at, down_done, swap(down_done, "c"), 0).astype(F32)
    up_done = ordered(y_at, up_y, swap(up_y, "y"), 1)
    up_done = ordered(c_at, up_done[None], swap(up_done, "c")[None], 0).reshape(2, up_rows, 2, depth, piece)
    up_done = jnp.where(x_at == 1, up_done, up_done[:, :, ::-1]).transpose(1, 3, 2, 0, 4)
    up_done = up_done.reshape(up_rows, hidden_width).astype(F32)
    late_done = ordered(c_at, late_z[None], swap(late_z, "c")[None], 0)
    late_done = ordered(y_at, late_done[None], swap(late_done, "y")[None], 0).reshape(parts, up_rows, model)
    qkv_done = late_done[:, :, : 3 * width].reshape(parts, up_rows, 3, width).transpose(1, 2, 0, 3)
    qkv_done = qkv_done.reshape(up_rows, 3 * model).astype(F32)
    out_done = late_done[:, :, 3 * width :].reshape(2, 2, up_rows, width).transpose(2, 1, 0, 3)
    out_done = out_done.reshape(up_rows, model).astype(F32)

    up_b = up_b.reshape(2, depth, 1, piece)
    up_b = jnp.where(x_at == 1, up_b, up_b[::-1]).transpose(1, 0, 2, 3)
    up_b = jnp.where(jnp.arange(2)[:, None] == c_at, up_b, 0.0).reshape(-1, model)
    qkv_b = jnp.where(jnp.arange(parts)[:, None] == me, qkv_b.reshape(3, 1, width), 0.0).reshape(3, model)
    times = doc_times.reshape(1, rows * SEGS)
    times = jnp.concatenate([times // 32, times % 32], axis=1).astype(F32)
    times = jnp.pad(times, ((0, 0), (0, model - times.shape[1])))
    small = jnp.concatenate(grad_shift + [sums1, sums2, qkv_b, up_b, times], axis=0)
    small = add_low(small, swap(small.astype(BF16), "c"))
    small = add_low(small, swap(small, "y"))
    small = ordered(x_at, small[None], swap(small, "x")[None], 0)
    if depth == 4:
        others = [lax.ppermute(small, "z", [(i, i ^ n) for i in range(depth)]) for n in range(1, depth)]
        small = jnp.stack([small] + others)
        small = jnp.stack([lax.dynamic_index_in_dim(small, z_at ^ n, 0, keepdims=False) for n in range(depth)])
    else:
        small = lax.all_gather(small, "z")
    small = small.reshape(dp, small.shape[2], model)
    all_times = small[:, -1, : 2 * rows * SEGS].astype(F32) * 0.25
    all_times = all_times[:, : rows * SEGS] * 32.0 + all_times[:, rows * SEGS :]
    shifts = small[:, : rows * SEGS].reshape(dp * rows * SEGS, model)
    columns = (2 * z_at + x_at) * (TEMB // dp) + jnp.arange(TEMB // dp)
    wanted = time_features(all_times.reshape(-1), columns, TEMB // 2)
    time_w_done = dot(wanted, shifts, 0, 0)
    sums = jnp.sum(small[:, rows * SEGS :].astype(F32), axis=0)
    dp_at = 2 * z_at + x_at

    def share(vector):
        return cut(vector.reshape(-1), dp_at, vector.size // dp, 0)

    time_b_done = jnp.sum(cut(shifts, dp_at, up_rows, 1).astype(F32), axis=0)
    return (
        output, input_grad, time_w_done, time_b_done, share(sums[0]), share(sums[1]), qkv_done, share(sums[6:9]),
        out_done, share(sums[4]), share(sums[2]), share(sums[3]), up_done, share(sums[9:-1]), down_done, share(sums[5]),
    )


def solution(mesh):
    dp, seq = mesh.shape["dp"], mesh.shape["seq"]
    fine = Mesh(mesh.devices.reshape(dp // 2, 2, seq // 2, 2), ("z", "x", "y", "c"))
    rows, seqs = ("z", "x"), ("y", "c")
    placed = (P(rows, seqs, None), P(rows, seqs), P(rows, None)) + (P(),) * 14 + (P(rows, seqs, None),)
    vec, mat = P(rows), P(rows, None)
    return jax.shard_map(
        functools.partial(local, dp=dp),
        mesh=fine,
        in_specs=placed,
        out_specs=(
            P(rows, seqs, None), P(rows, seqs, None), mat, vec, vec, vec, mat, vec, mat, vec, vec, vec, mat, vec, mat, vec,
        ),
        check_vma=False,
    )
```

time: 510 us -> 504 us (0.988)
  waiting for transfers between devices: 104 us -> 150 us
  Pallas kernels: 191 us -> 170 us
  matrix products: 60 us -> 42.7 us
    ppermute x61 -> x42, waiting for transfers between devices: 91.4 us -> 124 us  [swap(): return lax.ppermute(value, axis, [(0, 1), (1, 0)])]
    pallas_call x23 -> x14, Pallas kernels: 191 us -> 170 us  [call(): pl.pallas_call(kernel, grid_spec=pltpu.PrefetchScalarGridSpec(num_scalar_...]
    dot_general x11 -> x9, matrix products: 60 us -> 42.7 us  [dot(): lax.dot_general(left_op, right_op, (((left_dim,), (right_dim,)), ((), ())...]
    ppermute x61 -> x42, starting transfers between devices: 43.4 us -> 32 us  [swap(): return lax.ppermute(value, axis, [(0, 1), (1, 0)])]
    reduce_scatter x1, waiting for transfers between devices: 5.57 us -> 14.1 us  [local(): late_z = lax.psum_scatter(late_x, 'z', scatter_dimension=0, tiled=False)]
    ppermute x3, starting transfers between devices: 4.45 us -> 11 us  [local(): lax.ppermute(small, 'z', [(i, i ^ n) for i in range(depth)])]
    unnamed x151 -> x105, local copies, waits for them, and re-layouts: 12.4 us -> 10.2 us
    convert_element_type x12 -> x11, other arithmetic: 13 us -> 14 us  [add_low(): return (kept.astype(F32) + sent.astype(F32)).astype(BF16)]
  transfers between devices with their start and end apart: 67 -> 48, of which waited for: 23 -> 22; matrix products, arithmetic and copies ran while one was open for 19% -> 20% of each run, Pallas kernels for 30% -> 22%
where the time goes in v4:
time: 504 us; the launch traced here: 496 us
  Pallas kernels  170 us (34%)
  waiting for transfers between devices  150 us (30%)
  starting transfers between devices  43.4 us (9%)
  matrix products  42.7 us (8%)
  other arithmetic  37.1 us (7%)
  local copies, waits for them, and re-layouts  37 us (7%)
  between operations  15.2 us (3%)
    pallas_call x14, Pallas kernels, call(): pl.pallas_call(kernel, grid_spec=pltpu.PrefetchScalarGridSpec(num_scalar_...  170 us
    ppermute x42, waiting for transfers between devices, swap(): return lax.ppermute(value, axis, [(0, 1), (1, 0)])  124 us
    dot_general x9, matrix products, dot(): lax.dot_general(left_op, right_op, (((left_dim,), (right_dim,)), ((), ())...  42.7 us
    ppermute x42, starting transfers between devices, swap(): return lax.ppermute(value, axis, [(0, 1), (1, 0)])  32 us
    reduce_scatter x1, waiting for transfers between devices, local(): late_z = lax.psum_scatter(late_x, 'z', scatter_dimension=0, tiled=False)  14.1 us
    convert_element_type x11, other arithmetic, add_low(): return (kept.astype(F32) + sent.astype(F32)).astype(BF16)  14 us
    ppermute x3, waiting for transfers between devices, local(): lax.ppermute(small, 'z', [(i, i ^ n) for i in range(depth)])  11.9 us
    ppermute x3, starting transfers between devices, local(): lax.ppermute(small, 'z', [(i, i ^ n) for i in range(depth)])  11 us
  transfers between devices with their start and end apart: 48, of which 22 were waited for; matrix products, arithmetic and copies ran while one was open for 20% of the time, Pallas kernels for 22%

profile of v4, /device:TPU:0, one launch (start us, length us, event | category | flops | bytes accessed | tf_op | source)
XLA Modules:
  0.0 495.9 jit_solution(10754748138895558753)
XLA Ops:
  28.2 15.8 %cot_down.1 = (bf16[1536,2048]{1,0:T(8,128)(2,1)}, bf16[1024,2048]{1,0:T(8,128)(2,1)}, bf16[2048,1024]{1,0:T(8,128)(2,1)}, bf16[1536,1024]{1,0:T(8,128)(2,1)}) custom-call(s32[8]{0:T(128)} %add.314.refs_0_, bf16[768,1024]{1,0:T(8,128)(2,1)} %bitcast.126, bf16[768,1024]{1,0:T(8,128)(2,1)} %collective-permute-done.5.refs_2_, bf16[1024,4096]{1,0:T(8,128)(2,1)} %refs_3_.3, ...), custom_call_target="tpu_custom_call" | custom-call | flops 6442450944 | bytes 26214400 | tf_op jit(solution)/shard_map/cot_down/pallas_call | solution.py:94
  44.0 9.5 %qkv.2 = (bf16[3,4,3,256,256]{4,3,2,1,0:T(8,128)(2,1)}, bf16[4,3,256,1024]{3,2,1,0:T(8,128)(2,1)}, bf16[768,1024]{1,0:T(8,128)(2,1)}) custom-call(s32[1]{0:T(128)} %bitcast.refs_0_, bf16[3,256,1024]{2,1,0:T(8,128)(2,1)} %get-tuple-element.73.refs_1_, bf16[3,256,1024]{2,1,0:T(8,128)(2,1)} %collective-permute-done.4.refs_2_, bf16[1024,3072]{1,0:T(8,128)(2,1)} %refs_3_.5, ...), custom_call_target="tpu_custom_call" | custom-call | flops 2415919104 | bytes 7864320 | tf_op jit(solution)/shard_map/qkv/pallas_call | solution.py:94
  64.1 9.5 %qkv.3 = (bf16[3,4,3,256,256]{4,3,2,1,0:T(8,128)(2,1)}, bf16[4,3,256,1024]{3,2,1,0:T(8,128)(2,1)}, bf16[768,1024]{1,0:T(8,128)(2,1)}) custom-call(s32[1]{0:T(128)} %bitcast.refs_0_, bf16[3,256,1024]{2,1,0:T(8,128)(2,1)} %copy-done.9, bf16[3,256,1024]{2,1,0:T(8,128)(2,1)} %collective-permute-done.6.refs_2_, ...), custom_call_target="tpu_custom_call", output_to_operand_aliasing={{0}: (7, {}), {1}: (8, {})} | custom-call | flops 2415919104 | bytes 7864320 | tf_op jit(solution)/shard_map/qkv/pallas_call | solution.py:94
  73.6 14.1 %attend.2 = (bf16[4,3,256,256]{3,2,1,0:T(8,128)(2,1)}, bf16[2,256,256]{2,1,0:T(8,128)(2,1)}, bf16[2,2,256,256]{3,2,1,0:T(8,128)(2,1)}, f32[3,4,8,256]{3,2,1,0:T(8,128)}) custom-call(s32[12]{0:T(128)} %reshape.535.refs_0_, s32[48]{0:T(128)} %reshape.536.refs_1_, bf16[3,4,3,256,256]{4,3,2,1,0:T(8,128)(2,1)} %get-tuple-element.78.refs_2_, ...), custom_call_target="tpu_custom_call" | custom-call | flops 8589934592 | bytes 4194304 | tf_op jit(solution)/shard_map/attend/pallas_call | solution.py:94
  89.3 12.5 %collective-permute-done.11.refs_3_ = bf16[2,2,256,256]{3,2,1,0:T(8,128)(2,1)S(1)} collective-permute-done((bf16[2,2,256,256]{3,2,1,0:T(8,128)(2,1)}, bf16[2,2,256,256]{3,2,1,0:T(8,128)(2,1)S(1)}, u32[]{:S(2)}, u32[]{:S(2)}) %collective-permute-start.11) | collective-permute-done | bytes 524320 | tf_op jit(solution)/shard_map/ppermute | solution.py:27
  101.9 10.7 %attend.3 = (bf16[4,3,256,256]{3,2,1,0:T(8,128)(2,1)}, bf16[1,256,256]{2,1,0:T(8,128)(2,1)}, bf16[2,1,256,256]{3,2,1,0:T(8,128)(2,1)}, f32[3,4,8,256]{3,2,1,0:T(8,128)}) custom-call(s32[12]{0:T(128)} %reshape.535.refs_0_, s32[48]{0:T(128)} %reshape.536.refs_1_, ...), custom_call_target="tpu_custom_call", output_to_operand_aliasing={{0}: (4, {}), {3}: (5, {})} | custom-call | flops 4294967296 | bytes 2097152 | tf_op jit(solution)/shard_map/attend/pallas_call | solution.py:94
  117.5 6.1 %middle.2 = (f32[3,256,1024]{2,1,0:T(8,128)}, bf16[2,256,1024]{2,1,0:T(8,128)(2,1)}, bf16[3,256,1024]{2,1,0:T(8,128)(2,1)}) custom-call(s32[4]{0:T(128)} %pad_add_fusion.1.refs_0_, bf16[4,3,256,256]{3,2,1,0:T(8,128)(2,1)} %get-tuple-element.81.refs_1_.refs_3_, bf16[2,256,256]{2,1,0:T(8,128)(2,1)} %copy-done.19, bf16[2,2,256,256]{3,2,1,0:T(8,128)(2,1)} %copy-done.12, ...), custom_call_target="tpu_custom_call" | custom-call | flops 1073741824 | bytes 7340032 | tf_op jit(solution)/shard_map/middle/pallas_call | solution.py:94
  127.4 4.9 middle.3
  135.5 28.1 %hidden.1 = (bf16[1536,2048]{1,0:T(8,128)(2,1)}, bf16[1536,2048]{1,0:T(8,128)(2,1)}, f32[1,2048]{1,0:T(1,128)}, bf16[1536,1024]{1,0:T(8,128)(2,1)}, bf16[1536,1024]{1,0:T(8,128)(2,1)}) custom-call(bf16[2,256,1024]{2,1,0:T(8,128)(2,1)} %get-tuple-element.90.refs_0_, bf16[1,256,1024]{2,1,0:T(8,128)(2,1)} %get-tuple-element.91.refs_1_, ...), custom_call_target="tpu_custom_call" | custom-call | flops 12884901888 | bytes 36700160 | tf_op jit(solution)/shard_map/hidden/pallas_call | solution.py:94
  171.1 9.8 %middle_back.1 = (f32[3,256,1024]{2,1,0:T(8,128)}, bf16[3,256,1024]{2,1,0:T(8,128)(2,1)}, bf16[3,256,256]{2,1,0:T(8,128)(2,1)}, bf16[3,256,256]{2,1,0:T(8,128)(2...) custom-call(s32[4]{0:T(128)} %pad_add_fusion.1.refs_0_, bf16[1536,1024]{1,0:T(8,128)(2,1)} %get-tuple-element.95.refs_1_, ...), custom_call_target="tpu_custom_call" | custom-call | flops 1610612736 | bytes 14155776 | tf_op jit(solution)/shard_map/middle_back/pallas_call | solution.py:94
  181.3 11.2 %convolution_convert_fusion = bf16[1024,2048]{1,0:T(8,128)(2,1)} fusion(bf16[1536,1024]{1,0:T(8,128)(2,1)} %get-tuple-element.99, bf16[1536,2048]{1,0:T(8,128)(2,1)} %get-tuple-element.100), kind=kOutput, calls=%fused_computation.3 | convolution fusion | flops 6444548096 | bytes 13631488 | tf_op jit(solution)/shard_map/dot_general | solution.py:48
  192.8 7.8 %fusion.8 = bf16[1024,1024]{1,0:T(8,128)(2,1)} fusion(bf16[1536,1024]{1,0:T(8,128)(2,1)} %get-tuple-element.98, bf16[1536,2048]{1,0:T(8,128)(2,1)} %get-tuple-element.101), kind=kOutput, calls=%fused_computation.22 | convolution fusion | flops 3222274048 | bytes 8388608 | tf_op jit(solution)/shard_map/dot_general | solution.py:48
  221.0 27.1 %attend_back.2 = (bf16[4,3,256,768]{3,2,1,0:T(8,128)(2,1)}, bf16[2,256,1024]{2,1,0:T(8,128)(2,1)}, bf16[2,256,1024]{2,1,0:T(8,128)(2,1)}, bf16[2,256,1024]{2,1,0:T(8,128)(2,1)}, bf16[2,256,1024]{2,1,0:T(8,128)(2,1)}) custom-call(s32[12]{0:T(128)} %reshape.535.refs_0_, s32[48]{0:T(128)} %reshape.536.refs_1_, ...), custom_call_target="tpu_custom_call" | custom-call | flops 21474836480 | bytes 8388608 | tf_op jit(solution)/shard_map/attend_back/pallas_call | solution.py:94
  258.3 20.3 %attend_back.3 = (bf16[4,3,256,768]{3,2,1,0:T(8,128)(2,1)}, bf16[1,256,1024]{2,1,0:T(8,128)(2,1)}, bf16[1,256,1024]{2,1,0:T(8,128)(2,1)}, bf16[1,256,1024]{2,1,0:T(8,128)(2,1)}, bf16[1,256,1024]{2,1,0:T(8,128)(2,1)}) custom-call(s32[12]{0:T(128)} %reshape.535.refs_0_, s32[48]{0:T(128)} %reshape.536.refs_1_, ...), custom_call_target="tpu_custom_call", output_to_operand_aliasing={{0}: (13, {})} | custom-call | flops 10737418240 | bytes 4194304 | tf_op jit(solution)/shard_map/attend_back/pallas_call | solution.py:94
  279.3 18.8 %collective-permute-done.41 = bf16[1024,1024]{1,0:T(8,128)(2,1)} collective-permute-done((bf16[1024,1024]{1,0:T(8,128)(2,1)}, bf16[1024,1024]{1,0:T(8,128)(2,1)}, u32[]{:S(2)}, u32[]{:S(2)}) %collective-permute-start.41) | collective-permute-done | bytes 2097184 | tf_op jit(solution)/shard_map/ppermute | solution.py:27
  307.1 8.1 %bitcast_convert_fusion.1.refs_7_.refs_8_ = bf16[1024,768]{1,0:T(8,128)(2,1)} fusion(bf16[4,3,256,1024]{3,2,1,0:T(8,128)(2,1)} %get-tuple-element.119, bf16[4,3,256,768]{3,2,1,0:T(8,128)(2,1)S(1)} %bitcast.113), kind=kOutput, calls=%fused_computation.4 | convolution fusion | flops 4832624640 | bytes 12582912 | tf_op jit(solution)/shard_map/dot_general | solution.py:48
  316.0 12.8 %collective-permute-done.42 = bf16[1024,512]{1,0:T(8,128)(2,1)} collective-permute-done((bf16[1024,512]{1,0:T(8,128)(2,1)}, bf16[1024,512]{1,0:T(8,128)(2,1)}, u32[]{:S(2)}, u32[]{:S(2)}) %collective-permute-start.42) | collective-permute-done | bytes 1048608 | tf_op jit(solution)/shard_map/ppermute | solution.py:27
  331.4 19.8 %collective-permute-done.25.refs_2_ = bf16[2,256,1024]{2,1,0:T(8,128)(2,1)} collective-permute-done((bf16[2,256,1024]{2,1,0:T(8,128)(2,1)}, bf16[2,256,1024]{2,1,0:T(8,128)(2,1)}, u32[]{:S(2)}, u32[]{:S(2)}) %collective-permute-start.25) | collective-permute-done | bytes 1048608 | tf_op jit(solution)/shard_map/ppermute | solution.py:27
  351.2 5.8 %norm1_back.2 = (bf16[3,256,1024]{2,1,0:T(8,128)(2,1)}, f32[2,8,1024]{2,1,0:T(8,128)}, f32[8,1024]{1,0:T(8,128)}) custom-call(bf16[2,256,1024]{2,1,0:T(8,128)(2,1)} %get-tuple-element.117.refs_0_, bf16[2,256,1024]{2,1,0:T(8,128)(2,1)} %collective-permute-done.24.refs_1_, bf16[2,256,1024]{2,1,0:T(8,128)(2,1)} %collective-permute-done.25.refs_2_, ...), custom_call_target="tpu_custom_call" | custom-call | bytes 8388608 | tf_op jit(solution)/shard_map/norm1_back/pallas_call | solution.py:94
  374.6 23.4 %collective-permute-done.28 = bf16[38,1024]{1,0:T(8,128)(2,1)S(1)} collective-permute-done((bf16[38,1024]{1,0:T(8,128)(2,1)S(1)}, bf16[38,1024]{1,0:T(8,128)(2,1)S(1)}, u32[]{:S(2)}, u32[]{:S(2)}) %collective-permute-start.28) | collective-permute-done | bytes 77856 | tf_op jit(solution)/shard_map/ppermute | solution.py:27
  398.0 8.5 %collective-permute-start.29 = (bf16[2,38,1024]{2,1,0:T(8,128)(2,1)S(1)}, bf16[2,38,1024]{2,1,0:T(8,128)(2,1)S(1)}, u32[]{:S(2)}, u32[]{:S(2)}) collective-permute-start(bf16[2,38,1024]{2,1,0:T(8,128)(2,1)S(1)} %maximum_select_fusion.9), channel_id=1, source_target_pairs={{0,8},{8,0},{16,24},{24,16},{1,9},{9,1},{17,25},{25,17},{2,10},{10... | collective-permute-start | bytes 466952 | tf_op jit(solution)/shard_map/ppermute | solution.py:835
  411.9 9.0 %collective-permute-done.30 = bf16[2,38,1024]{2,1,0:T(8,128)(2,1)S(1)} collective-permute-done((bf16[2,38,1024]{2,1,0:T(8,128)(2,1)S(1)}, bf16[2,38,1024]{2,1,0:T(8,128)(2,1)S(1)}, u32[]{:S(2)}, u32[]{:S(2)}) %collective-permute-start.30) | collective-permute-done | bytes 155680 | tf_op jit(solution)/shard_map/ppermute | solution.py:835
  437.2 14.1 %reduce-scatter.4.cloned.1.call-done = bf16[1,128,1024]{2,1,0:T(8,128)(2,1)} async-done(((bf16[4,128,1024]{2,1,0:T(8,128)(2,1)}), bf16[1,128,1024]{2,1,0:T(8,128)(2,1)}) %reduce-scatter.4.cloned.1.call-update) | async-done | bytes 262160 | tf_op jit(solution)/shard_map/reduce_scatter | solution.py:808
  462.4 9.5 %collective-permute-done.36 = bf16[2,128,1024]{2,1,0:T(8,128)(2,1)S(1)} collective-permute-done((bf16[2,128,1024]{2,1,0:T(8,128)(2,1)S(1)}, bf16[2,128,1024]{2,1,0:T(8,128)(2,1)S(1)}, u32[]{:S(2)}, u32[]{:S(2)}) %collective-permute-start.36) | collective-permute-done | bytes 524320 | tf_op jit(solution)/shard_map/ppermute | solution.py:27
  (341 shorter events, 163.6 us)
Async XLA Ops:
  7.2 418.8 %reduce-scatter.6.cloned.1.call-start = ((), (), s32[]{:S(2)}) async-start(), calls=%async_computation.4 | async-start | bytes 5242880 | tf_op jit(solution)/shard_map/reduce_scatter | solution.py:761
  7.2 21.0 %collective-permute-start.5 = (bf16[768,1024]{1,0:T(8,128)(2,1)}, bf16[768,1024]{1,0:T(8,128)(2,1)}, u32[]{:S(2)}, u32[]{:S(2)}) collective-permute-start(bf16[768,1024]{1,0:T(8,128)(2,1)} %bitcast.125), channel_id=1, source_target_pairs={{0,1},{1,0},{2,3},{3,2},{4,5},{5,4},{6,7},{7,6},{8,9},{9,8},{10,11... | collective-permute-start | bytes 4718600 | tf_op jit(solution)/shard_map/ppermute | solution.py:27
  18.6 25.4 %collective-permute-start.4 = (bf16[3,256,1024]{2,1,0:T(8,128)(2,1)}, bf16[3,256,1024]{2,1,0:T(8,128)(2,1)}, u32[]{:S(2)}, u32[]{:S(2)}) collective-permute-start(bf16[3,256,1024]{2,1,0:T(8,128)(2,1)} %get-tuple-element.73.refs_1_), channel_id=1, source_target_pairs={{0,1},{1,0},{2,3},{3,2},{4,5},{5,4},{6,7},{7,6},{8,9},{9,8},{10,11... | collective-permute-start | bytes 4718600 | tf_op jit(solution)/shard_map/ppermute | solution.py:27
  18.7 37.8 %collective-permute-start.3 = (bf16[3,256,1024]{2,1,0:T(8,128)(2,1)}, bf16[3,256,1024]{2,1,0:T(8,128)(2,1)S(1)}, u32[]{:S(2)}, u32[]{:S(2)}) collective-permute-start(bf16[3,256,1024]{2,1,0:T(8,128)(2,1)} %get-tuple-element.73.refs_1_), channel_id=1, source_target_pairs={{0,2},{2,0},{1,3},{3,1},{4,6},{6,4},{5,7},{7,5},{8,10},{10,8},{9,1... | collective-permute-start | bytes 4718600 | tf_op jit(solution)/shard_map/ppermute | solution.py:27
  89.3 27.4 %collective-permute-start.10 = (bf16[2,256,256]{2,1,0:T(8,128)(2,1)}, bf16[2,256,256]{2,1,0:T(8,128)(2,1)S(1)}, u32[]{:S(2)}, u32[]{:S(2)}) collective-permute-start(bf16[2,256,256]{2,1,0:T(8,128)(2,1)} %get-tuple-element.85), channel_id=1, source_target_pairs={{0,1},{1,0},{2,3},{3,2},{4,5},{5,4},{6,7},{7,6},{8,9},{9,8},{10,11... | collective-permute-start | bytes 786440 | tf_op jit(solution)/shard_map/ppermute | solution.py:27
  101.8 14.9 %collective-permute-start.12 = (bf16[2,256,256]{2,1,0:T(8,128)(2,1)S(1)}, bf16[2,256,256]{2,1,0:T(8,128)(2,1)S(1)}, u32[]{:S(2)}, u32[]{:S(2)}) collective-permute-start(bf16[2,256,256]{2,1,0:T(8,128)(2,1)S(1)} %slice_bitcast_fusion.1), channel_id=1, source_target_pairs={{0,1},{1,0},{2,3},{3,2},{4,5},{5,4},{6,7},{7,6},{8,9},{9,8},{10,11... | collective-permute-start | bytes 786440 | tf_op jit(solution)/shard_map/ppermute | solution.py:27
  180.9 33.5 %collective-permute-start.18 = (bf16[2,3,256,256]{3,2,1,0:T(8,128)(2,1)}, bf16[2,3,256,256]{3,2,1,0:T(8,128)(2,1)S(1)}, u32[]{:S(2)}, u32[]{:S(2)}) collective-permute-start(bf16[2,3,256,256]{3,2,1,0:T(8,128)(2,1)} %get-tuple-element.96), channel_id=1, source_target_pairs={{0,2},{2,0},{1,3},{3,1},{4,6},{6,4},{5,7},{7,5},{8,10},{10,8},{9,1... | collective-permute-start | bytes 2359304 | tf_op jit(solution)/shard_map/ppermute | solution.py:27
  192.5 236.8 %reduce-scatter.8.cloned.1.call-start = ((), (), s32[]{:S(2)}) async-start(), calls=%async_computation.5 | async-start | bytes 1310720 | tf_op jit(solution)/shard_map/reduce_scatter | solution.py:797
  208.6 42.9 %collective-permute-start.32 = (bf16[1024,512]{1,0:T(8,128)(2,1)}, bf16[1024,512]{1,0:T(8,128)(2,1)}, u32[]{:S(2)}, u32[]{:S(2)}) collective-permute-start(bf16[1024,512]{1,0:T(8,128)(2,1)} %constant_dynamic-slice_fusion.9), channel_id=1, source_target_pairs={{0,1},{1,0},{2,3},{3,2},{4,5},{5,4},{6,7},{7,6},{8,9},{9,8},{10,11... | collective-permute-start | bytes 3145736 | tf_op jit(solution)/shard_map/ppermute | solution.py:27
  249.7 48.4 %collective-permute-start.41 = (bf16[1024,1024]{1,0:T(8,128)(2,1)}, bf16[1024,1024]{1,0:T(8,128)(2,1)}, u32[]{:S(2)}, u32[]{:S(2)}) collective-permute-start(bf16[1024,1024]{1,0:T(8,128)(2,1)} %fusion.8), channel_id=1, source_target_pairs={{0,4},{4,0},{1,5},{5,1},{2,6},{6,2},{3,7},{7,3},{8,12},{12,8},{9,1... | collective-permute-start | bytes 6291464 | tf_op jit(solution)/shard_map/ppermute | solution.py:27
  254.2 24.9 %collective-permute-start.33 = (bf16[1024,256]{1,0:T(8,128)(2,1)S(1)}, bf16[1024,256]{1,0:T(8,128)(2,1)S(1)}, u32[]{:S(2)}, u32[]{:S(2)}) collective-permute-start(bf16[1024,256]{1,0:T(8,128)(2,1)S(1)} %constant_dynamic-slice_fusion.8), channel_id=1, source_target_pairs={{0,2},{2,0},{1,3},{3,1},{4,6},{6,4},{5,7},{7,5},{8,10},{10,8},{9,1... | collective-permute-start | bytes 1572872 | tf_op jit(solution)/shard_map/ppermute | solution.py:27
  255.7 75.7 %collective-permute-start.24 = (bf16[2,256,1024]{2,1,0:T(8,128)(2,1)}, bf16[2,256,1024]{2,1,0:T(8,128)(2,1)}, u32[]{:S(2)}, u32[]{:S(2)}) collective-permute-start(bf16[2,256,1024]{2,1,0:T(8,128)(2,1)} %get-tuple-element.118), channel_id=1, source_target_pairs={{0,1},{1,0},{2,3},{3,2},{4,5},{5,4},{6,7},{7,6},{8,9},{9,8},{10,11... | collective-permute-start | bytes 3145736 | tf_op jit(solution)/shard_map/ppermute | solution.py:27
  278.6 25.8 %collective-permute-start.22 = (bf16[1,256,1024]{2,1,0:T(8,128)(2,1)}, bf16[1,256,1024]{2,1,0:T(8,128)(2,1)S(1)}, u32[]{:S(2)}, u32[]{:S(2)}) collective-permute-start(bf16[1,256,1024]{2,1,0:T(8,128)(2,1)} %get-tuple-element.115), channel_id=1, source_target_pairs={{0,1},{1,0},{2,3},{3,2},{4,5},{5,4},{6,7},{7,6},{8,9},{9,8},{10,11... | collective-permute-start | bytes 1572872 | tf_op jit(solution)/shard_map/ppermute | solution.py:27
  302.4 26.4 %collective-permute-start.42 = (bf16[1024,512]{1,0:T(8,128)(2,1)}, bf16[1024,512]{1,0:T(8,128)(2,1)}, u32[]{:S(2)}, u32[]{:S(2)}) collective-permute-start(bf16[1024,512]{1,0:T(8,128)(2,1)} %constant_dynamic-slice_fusion.1), channel_id=1, source_target_pairs={{0,2},{2,0},{1,3},{3,1},{4,6},{6,4},{5,7},{7,5},{8,10},{10,8},{9,1... | collective-permute-start | bytes 3145736 | tf_op jit(solution)/shard_map/ppermute | solution.py:27
  304.1 47.1 %collective-permute-start.25 = (bf16[2,256,1024]{2,1,0:T(8,128)(2,1)}, bf16[2,256,1024]{2,1,0:T(8,128)(2,1)}, u32[]{:S(2)}, u32[]{:S(2)}) collective-permute-start(bf16[2,256,1024]{2,1,0:T(8,128)(2,1)} %add_convert_fusion.5.refs_14_), channel_id=1, source_target_pairs={{0,2},{2,0},{1,3},{3,1},{4,6},{6,4},{5,7},{7,5},{8,10},{10,8},{9,1... | collective-permute-start | bytes 3145736 | tf_op jit(solution)/shard_map/ppermute | solution.py:27
  304.4 52.7 %collective-permute-start.21 = (bf16[1,256,1024]{2,1,0:T(8,128)(2,1)}, bf16[1,256,1024]{2,1,0:T(8,128)(2,1)S(1)}, u32[]{:S(2)}, u32[]{:S(2)}) collective-permute-start(bf16[1,256,1024]{2,1,0:T(8,128)(2,1)} %get-tuple-element.113), channel_id=1, source_target_pairs={{0,1},{1,0},{2,3},{3,2},{4,5},{5,4},{6,7},{7,6},{8,9},{9,8},{10,11... | collective-permute-start | bytes 1572872 | tf_op jit(solution)/shard_map/ppermute | solution.py:27
  305.4 55.8 %collective-permute-start.23 = (bf16[1,256,1024]{2,1,0:T(8,128)(2,1)}, bf16[1,256,1024]{2,1,0:T(8,128)(2,1)}, u32[]{:S(2)}, u32[]{:S(2)}) collective-permute-start(bf16[1,256,1024]{2,1,0:T(8,128)(2,1)} %add_convert_fusion.8), channel_id=1, source_target_pairs={{0,2},{2,0},{1,3},{3,1},{4,6},{6,4},{5,7},{7,5},{8,10},{10,8},{9,1... | collective-permute-start | bytes 1572872 | tf_op jit(solution)/shard_map/ppermute | solution.py:27
  331.4 119.9 %reduce-scatter.4.cloned.1.call-start = ((), (), s32[]{:S(2)}) async-start(), calls=%async_computation.3 | async-start | bytes 1310720 | tf_op jit(solution)/shard_map/reduce_scatter | solution.py:808
  371.0 50.2 %collective-permute-start.34 = (bf16[4,128,1024]{2,1,0:T(8,128)(2,1)}, bf16[4,128,1024]{2,1,0:T(8,128)(2,1)}, u32[]{:S(2)}, u32[]{:S(2)}) collective-permute-start(bf16[4,128,1024]{2,1,0:T(8,128)(2,1)} %constant_dynamic-slice_fusion.7), channel_id=1, source_target_pairs={{0,4},{4,0},{1,5},{5,1},{2,6},{6,2},{3,7},{7,3},{8,12},{12,8},{9,1... | collective-permute-start | bytes 3145736 | tf_op jit(solution)/shard_map/ppermute | solution.py:27
  372.8 25.2 %collective-permute-start.28 = (bf16[38,1024]{1,0:T(8,128)(2,1)S(1)}, bf16[38,1024]{1,0:T(8,128)(2,1)S(1)}, u32[]{:S(2)}, u32[]{:S(2)}) collective-permute-start(bf16[38,1024]{1,0:T(8,128)(2,1)S(1)} %add_convert_fusion.10), channel_id=1, source_target_pairs={{0,4},{4,0},{1,5},{5,1},{2,6},{6,2},{3,7},{7,3},{8,12},{12,8},{9,1... | collective-permute-start | bytes 233480 | tf_op jit(solution)/shard_map/ppermute | solution.py:27
  427.2 24.1 %collective-permute-start.37 = (bf16[128,2048]{1,0:T(8,128)(2,1)S(1)}, bf16[128,2048]{1,0:T(8,128)(2,1)S(1)}, u32[]{:S(2)}, u32[]{:S(2)}) collective-permute-start(bf16[128,2048]{1,0:T(8,128)(2,1)S(1)} %constant_dynamic-slice_fusion.3), channel_id=1, source_target_pairs={{0,4},{4,0},{1,5},{5,1},{2,6},{6,2},{3,7},{7,3},{8,12},{12,8},{9,1... | collective-permute-start | bytes 1572872 | tf_op jit(solution)/shard_map/ppermute | solution.py:27
  437.1 17.6 %collective-permute-start.44 = (bf16[256,1024]{1,0:T(8,128)(2,1)S(1)}, bf16[256,1024]{1,0:T(8,128)(2,1)S(1)}, u32[]{:S(2)}, u32[]{:S(2)}) collective-permute-start(bf16[256,1024]{1,0:T(8,128)(2,1)S(1)} %maximum_select_fusion.7), channel_id=1, source_target_pairs={{0,1},{1,0},{2,3},{3,2},{4,5},{5,4},{6,7},{7,6},{8,9},{9,8},{10,11... | collective-permute-start | bytes 1572872 | tf_op jit(solution)/shard_map/ppermute | solution.py:27
  453.2 18.7 %collective-permute-start.36 = (bf16[2,128,1024]{2,1,0:T(8,128)(2,1)S(1)}, bf16[2,128,1024]{2,1,0:T(8,128)(2,1)S(1)}, u32[]{:S(2)}, u32[]{:S(2)}) collective-permute-start(bf16[2,128,1024]{2,1,0:T(8,128)(2,1)S(1)} %maximum_select_fusion.4), channel_id=1, source_target_pairs={{0,2},{2,0},{1,3},{3,1},{4,6},{6,4},{5,7},{7,5},{8,10},{10,8},{9,1... | collective-permute-start | bytes 1572872 | tf_op jit(solution)/shard_map/ppermute | solution.py:27
  460.8 16.4 %collective-permute-start.39 = (bf16[128,1024]{1,0:T(8,128)(2,1)S(1)}, bf16[128,1024]{1,0:T(8,128)(2,1)S(1)}, u32[]{:S(2)}, u32[]{:S(2)}) collective-permute-start(bf16[128,1024]{1,0:T(8,128)(2,1)S(1)} %add_convert_fusion.9), channel_id=1, source_target_pairs={{0,2},{2,0},{1,3},{3,1},{4,6},{6,4},{5,7},{7,5},{8,10},{10,8},{9,1... | collective-permute-start | bytes 786440 | tf_op jit(solution)/shard_map/ppermute | solution.py:27
  (73 other events, 619.8 us)
Sparse Core Ops, SparseCore 0:
  192.6 78.9 reduce-scatter.5
  331.5 34.8 reduce-scatter.7
  424.0 27.2 reduce-scatter.3
